TPU v7x, 256 devices: a whole 4x4x8 slice. The times are simulated.
256 devices in a mesh: dp: 16 (over z_lo, y, core), tensor: 16 (over x, z_hi).
Axes of the slice: x: 4, y: 4, z: 8 (z_hi: 4, z_lo: 2; z = z_hi * 2 + z_lo), core: 2. Of those that a mesh axis runs over, the one named last changes fastest.
Arguments:
- layer_input: bfloat16 [8192, 6144], P(('dp', 'tensor')), may hold values from -24 to 24
- out_grad: bfloat16 [8192, 6144], P('dp', 'tensor'), may hold values from -6 to 6
- master: float32 [6144, 6144], P('dp', 'tensor'), may hold values from -300 to 300
- moment_code: bfloat16 [6144, 6144], P('dp', 'tensor'), may hold values from -1 to 1
- moment_scale: float32 [6144, 48], P('dp', 'tensor'), may hold values from 0.1 to 3
- second_code: bfloat16 [6144, 6144], P('dp', 'tensor'), may hold values from 0.049804688 to 1
- second_scale: float32 [6144, 48], P('dp', 'tensor'), may hold values from 0.001 to 0.01
Outputs:
- input_grad: bfloat16 [8192, 6144], P(('dp', 'tensor'))
- new_master: float32 [6144, 6144], P('dp', 'tensor')
- new_moment_code: bfloat16 [6144, 6144], P('dp', 'tensor')
- new_moment_scale: float32 [6144, 48], P('dp', 'tensor')
- new_second_code: bfloat16 [6144, 6144], P('dp', 'tensor')
- new_second_scale: float32 [6144, 48], P('dp', 'tensor')
- new_weight: bfloat16 [6144, 6144], P(None, 'tensor')
- trust_ratio: float32 [], replicated
All inputs are finite; a program needn't handle non-finite values. Where the computation divides by a largest or mean magnitude, that divisor is 1e-20 or more.
Results may differ from a plain program's by a relative error of at most 0.017.
Values may be sent and summed in bfloat16 or wider, within the bound.
No kernel may reach another device: no remote copies, remote signals or barrier semaphores. Data moves between devices by JAX's collectives and lax.ppermute only.
A program may use at most 128 MiB of HBM per device.

v0:
```python
import functools
import math

import jax
import jax.numpy as jnp
from jax import lax
from jax.experimental import pallas as pl
from jax.experimental.pallas import tpu as pltpu
from jax.sharding import PartitionSpec as P

FEAT_IN = 6144
SIZES = (2, 4, 2, 4, 4)
BOTH = ("dp", "tensor")
BF16, F32 = jnp.bfloat16, jnp.float32


def shift(array, z=0, y=0, core=0, x=0, high=0):
    moves = (z, y, core, x, high)
    pairs = []
    for source in range(math.prod(SIZES)):
        rest, place = source, []
        for size in reversed(SIZES):
            place.append(rest % size)
            rest //= size
        target = 0
        for size, at, move in zip(SIZES, reversed(place), moves):
            target = target * size + (at + move) % size
        pairs.append((source, target))
    return lax.ppermute(array, BOTH, pairs)


def roll(array, start):
    return lax.dynamic_slice_in_dim(
        jnp.concatenate([array, array], axis=0), start, array.shape[0], axis=0
    )


def take(array, index, axis):
    return lax.dynamic_index_in_dim(array, index, axis, keepdims=False)


def after(array, *others):
    return lax.optimization_barrier((array,) + others)[0]


def total_of(values):
    row = jnp.concatenate([jnp.full((1, 128), v, F32) for v in values] * (8 // len(values)))
    for axis in ("dp", "tensor"):
        spread = jnp.broadcast_to(row[None], (16, 8, 128))
        row = jnp.sum(lax.all_to_all(spread, axis, 0, 0, tiled=True), axis=0)
    return [row[i, 0] for i in range(len(values))]


def moments_kernel(
    own, one, two, three, master, mcode, mscale, scode, sscale,
    update, new_mcode, new_mscale, new_scode, new_sscale, sums,
):
    rows, cols = master.shape
    blocks = mscale.shape[1]
    wide = cols // blocks
    step = 64
    sums[...] = jnp.zeros_like(sums)

    def body(i, carry):
        at = pl.ds(pl.multiple_of(i * step, step), step)
        mscales, sscales = mscale[at, :], sscale[at, :]
        new_m, new_s = [], []
        for b in range(blocks):
            cut = slice(b * wide, (b + 1) * wide)
            grad = (
                own[at, cut]
                + one[at, cut].astype(F32)
                + two[at, cut].astype(F32)
                + three[at, cut].astype(F32)
            )
            weight = master[at, cut]
            moment = mcode[at, cut].astype(F32) * mscales[:, b : b + 1]
            second = scode[at, cut].astype(F32) * sscales[:, b : b + 1]
            moment = 0.9 * moment + 0.1 * grad
            second = 0.999 * second + 0.001 * grad * grad
            change = (
                moment / (1.0 - 0.9**10) / (jnp.sqrt(second / (1.0 - 0.999**10)) + 1e-06)
                + 0.1 * weight
            )
            update[at, cut] = change
            mtop = 2.0 * jnp.max(jnp.abs(moment), axis=1, keepdims=True) + 1e-06
            stop = 2.0 * jnp.max(jnp.abs(second), axis=1, keepdims=True) + 1e-06
            new_mcode[at, cut] = (moment / mtop).astype(BF16)
            new_scode[at, cut] = (second / stop).astype(BF16)
            new_m.append(mtop)
            new_s.append(stop)
            sums[0:1, :] += jnp.sum(weight * weight, axis=0, keepdims=True)
            sums[1:2, :] += jnp.sum(change * change, axis=0, keepdims=True)
        new_mscale[at, :] = jnp.concatenate(new_m, axis=1)
        new_sscale[at, :] = jnp.concatenate(new_s, axis=1)
        return carry

    lax.fori_loop(0, rows // step, body, 0)


def moments(own, others, master, mcode, mscale, scode, sscale):
    like = lambda a, dtype: jax.ShapeDtypeStruct(a.shape, dtype)
    block = master.shape[1] // mscale.shape[1]
    return pl.pallas_call(
        moments_kernel,
        out_shape=(
            like(master, F32),
            like(master, BF16),
            like(mscale, F32),
            like(master, BF16),
            like(sscale, F32),
            jax.ShapeDtypeStruct((8, block), F32),
        ),
        in_specs=[pl.BlockSpec(memory_space=pltpu.VMEM)] * 9,
        out_specs=[pl.BlockSpec(memory_space=pltpu.VMEM)] * 6,
        compiler_params=pltpu.CompilerParams(vmem_limit_bytes=32 * 1024 * 1024),
        cost_estimate=pl.CostEstimate(
            flops=40 * master.size, bytes_accessed=24 * master.size, transcendentals=master.size
        ),
    )(own, *others, master, mcode, mscale, scode, sscale)


def gather_rows(part):
    far = shift(part, z=1)
    near = [part] + [shift(part, y=s) for s in (1, 2, 3)]
    far = [far] + [shift(far, y=s) for s in (1, 2, 3)]
    pieces = []
    for r, row in enumerate((near, far)):
        for s, piece in enumerate(row):
            pieces.append(((r, s, 0), piece))
            pieces.append(((r, s, 1), shift(piece, core=1)))
    return pieces


def place_kernel(count, order, *refs):
    pieces, out = refs[:count], refs[count]
    step = pl.program_id(0)
    for i in range(count):

        @pl.when(step == i)
        def _(i=i):
            out[...] = pieces[i][...]


def place_rows(pieces, z, y, core):
    count = len(pieces)
    rows, cols = pieces[0][1].shape
    order = jnp.stack(
        [
            ((z + r) % 2 * 4 + (y + 4 - s) % 4) * 2 + (core + c) % 2
            for (r, s, c), _ in pieces
        ]
    ).astype(jnp.int32)
    return pl.pallas_call(
        functools.partial(place_kernel, count),
        out_shape=jax.ShapeDtypeStruct((count * rows, cols), BF16),
        grid_spec=pltpu.PrefetchScalarGridSpec(
            num_scalar_prefetch=1,
            grid=(count,),
            in_specs=[pl.BlockSpec((rows, cols), lambda i, order: (0, 0))] * count,
            out_specs=pl.BlockSpec((rows, cols), lambda i, order: (order[i], 0)),
        ),
        compiler_params=pltpu.CompilerParams(vmem_limit_bytes=32 * 1024 * 1024),
        cost_estimate=pl.CostEstimate(
            flops=0, bytes_accessed=4 * count * rows * cols, transcendentals=0
        ),
    )(order, *[piece for _, piece in pieces])


def local(layer_input, out_grad, master, moment_code, moment_scale, second_code, second_scale):
    inv_root = 1.0 / math.sqrt(FEAT_IN)
    d, t = lax.axis_index("dp"), lax.axis_index("tensor")
    z, y, core, x, high = d // 8, (d // 2) % 4, d % 2, t // 4, t % 4
    few, feat = layer_input.shape
    rows, cols = master.shape
    steps = (1, 2, 3)

    grads = out_grad.reshape(4, 4, few, cols)
    grads = roll(grads[::-1], 3 - x)
    parts = [take(grads, high, 1)] + [
        shift(take(grads, (high + s) % 4, 1), high=s) for s in steps
    ]
    near = jnp.concatenate(parts, axis=2).reshape(4 * few, 4 * cols)
    far = shift(near, z=1)
    crossed = far
    near = jnp.concatenate([near] + [shift(near, y=s) for s in steps])
    far = jnp.concatenate([far] + [shift(far, y=s) for s in steps])
    wide = [near, shift(near, core=1), far, shift(far, core=1)]

    mine = layer_input.reshape(few, 2, 4, 2, rows)
    mine = jnp.stack([take(mine, core, 3), shift(take(mine, 1 - core, 3), core=1)])
    mine = jnp.stack(
        [take(mine, y, 3)] + [shift(take(mine, (y + s) % 4, 3), y=s) for s in steps], axis=1
    )
    mine = jnp.stack([take(mine, z, 3), shift(take(mine, 1 - z, 3), z=1)])
    acts = jnp.stack([mine] + [shift(mine, x=s) for s in steps], axis=3)
    acts = acts.reshape(4, 16 * few, rows)

    part = sum(
        jnp.einsum("tk,tn->kn", acts[i], wide[i], preferred_element_type=F32) for i in range(4)
    )
    part = (part * inv_root).reshape(rows, 4, cols)
    sends = [part[:, s].astype(BF16) for s in steps]
    others = [shift(send, high=-s) for s, send in zip(steps, sends)]

    update, new_moment_code, new_moment_scale, new_second_code, new_second_scale, sums = moments(
        part[:, 0], others, master, moment_code, moment_scale, second_code, second_scale
    )

    weight16 = after(master.astype(BF16), crossed)
    weights = jnp.concatenate([weight16] + [shift(weight16, high=s) for s in steps], axis=1)
    weights = after(weights, *sends)
    outs = jnp.stack(
        [jnp.einsum("tn,kn->tk", w, weights, preferred_element_type=F32) for w in wide]
    )
    outs = (outs * inv_root).reshape(2, 2, 4, 4, few, rows)
    summed = outs[:, :, :, 0]
    for s in steps:
        summed = summed + shift(outs[:, :, :, s].astype(BF16), x=-s).astype(F32)
    back = summed.astype(BF16)
    near, far = back[0], shift(back[1], z=1)
    back = jnp.stack([jnp.where(z == 0, near, far), jnp.where(z == 0, far, near)], axis=2)
    back = jnp.stack([back[:, 0]] + [shift(back[:, s], y=-s) for s in steps], axis=2)
    near, far = back[0], shift(back[1], core=1)
    back = jnp.stack([jnp.where(core == 0, near, far), jnp.where(core == 0, far, near)])
    back = roll(back.transpose(2, 0, 1, 3, 4), (4 - y) % 4)
    input_grad = back.transpose(3, 2, 0, 1, 4).reshape(few, feat)

    weight_sq, update_sq = total_of((jnp.sum(sums[0]), jnp.sum(sums[1])))
    trust_ratio = jnp.sqrt(weight_sq) / (jnp.sqrt(update_sq) + 1e-06)
    new_master = master - 0.02 * trust_ratio * update
    new_weight = place_rows(gather_rows(new_master.astype(BF16)), z, y, core)
    return (
        input_grad,
        new_master,
        new_moment_code,
        new_moment_scale,
        new_second_code,
        new_second_scale,
        new_weight,
        trust_ratio,
    )


def solution(mesh):
    placed = (P(BOTH, None),) + (P("dp", "tensor"),) * 6
    return jax.shard_map(
        local,
        mesh=mesh,
        in_specs=placed,
        out_specs=(P(BOTH, None),) + (P("dp", "tensor"),) * 5 + (P(None, "tensor"), P()),
        check_vma=False,
    )
```

profile of v0, /device:TPU:1, one launch (start us, length us, event | category | flops | bytes accessed | tf_op | source)
XLA Modules:
  0.0 300.0 jit_solution(2623471096888096826)
XLA Ops:
  2.9 3.3 %collective-permute-start.10 = (bf16[32,2,4,384]{3,0,2,1:T(8,128)(2,1)S(1)}, bf16[32,2,4,384]{3,0,2,1:T(8,128)(2,1)S(1)}, u32[]{:S(2)}, u32[]{:S(2)}) collective-permute-start(bf16[32,2,4,384]{3,0,2,1:T(8,128)(2,1)S(1)} %bitcast.190), channel_id=1, source_target_pairs={{0,16},{1,17},{2,18},{3,19},{4,20},{5,21},{6,22},{7,23},{8,24},{9,... | collective-permute-start | bytes 589832 | tf_op jit(solution)/shard_map/ppermute | solution.py:29
  6.5 4.4 %collective-permute-start.2 = (bf16[4,32,384]{2,1,0:T(8,128)(2,1)S(1)}, bf16[4,32,384]{2,1,0:T(8,128)(2,1)S(1)}, u32[]{:S(2)}, u32[]{:S(2)}) collective-permute-start(bf16[4,32,384]{2,1,0:T(8,128)(2,1)S(1)} %get-tuple-element.86), channel_id=1, source_target_pairs={{0,3},{1,0},{2,1},{3,2},{4,7},{5,4},{6,5},{7,6},{8,11},{9,8},{10,9... | collective-permute-start | bytes 294920 | tf_op jit(solution)/shard_map/ppermute | solution.py:29
  11.9 2.3 collective-permute-start
  14.3 2.8 collective-permute-start.13
  17.5 3.5 %collective-permute-done.1 = bf16[4,32,384]{2,1,0:T(8,128)(2,1)S(1)} collective-permute-done((bf16[4,32,384]{2,1,0:T(8,128)(2,1)S(1)}, bf16[4,32,384]{2,1,0:T(8,128)(2,1)S(1)}, u32[]{:S(2)}, u32[]{:S(2)}) %collective-permute-start.1) | collective-permute-done | bytes 98336 | tf_op jit(solution)/shard_map/ppermute | solution.py:29
  21.1 2.4 collective-permute-start.6
  23.4 2.6 collective-permute-start.5
  27.1 1.6 collective-permute-start.11
  28.7 20.4 %collective-permute-done.11 = bf16[2,32,2,384]{3,1,2,0:T(8,128)(2,1)S(1)} collective-permute-done((bf16[2,32,2,384]{3,1,2,0:T(8,128)(2,1)S(1)}, bf16[2,32,2,384]{3,1,2,0:T(8,128)(2,1)S(1)}, u32[]{:S(2)}, u32[]{:S(2)}) %collective-permute-start.11) | collective-permute-done | bytes 98336 | tf_op jit(solution)/shard_map/ppermute | solution.py:29
  49.5 2.4 pad_maximum_fusion
  53.0 1.8 collective-permute-start.20
  56.1 12.9 %collective-permute-done.19 = bf16[128,1536]{1,0:T(8,128)(2,1)S(1)} collective-permute-done((bf16[128,1536]{1,0:T(8,128)(2,1)S(1)}, bf16[128,1536]{1,0:T(8,128)(2,1)S(1)}, u32[]{:S(2)}, u32[]{:S(2)}) %collective-permute-start.19) | collective-permute-done | bytes 393248 | tf_op jit(solution)/shard_map/ppermute | solution.py:29
  69.0 5.2 %collective-permute-done.21 = bf16[128,1536]{1,0:T(8,128)(2,1)S(1)} collective-permute-done((bf16[128,1536]{1,0:T(8,128)(2,1)S(1)}, bf16[128,1536]{1,0:T(8,128)(2,1)S(1)}, u32[]{:S(2)}, u32[]{:S(2)}) %collective-permute-start.21) | collective-permute-done | bytes 393248 | tf_op jit(solution)/shard_map/ppermute | solution.py:29
  75.3 2.6 collective-permute-start.17
  79.0 15.7 %collective-permute-done.17 = bf16[2,2,4,32,384]{4,3,2,1,0:T(8,128)(2,1)S(1)} collective-permute-done((bf16[2,2,4,32,384]{4,3,2,1,0:T(8,128)(2,1)S(1)}, bf16[2,2,4,32,384]{4,3,2,1,0:T(8,128)(2,1)S(1)}, u32[]{:S(2)}, u32[]{:S(2)}) %collective-permute-start.17) | collective-permute-done | bytes 393248 | tf_op jit(solution)/shard_map/ppermute | solution.py:29
  94.7 4.2 %collective-permute-done.15 = bf16[2,2,4,32,384]{4,3,2,1,0:T(8,128)(2,1)S(1)} collective-permute-done((bf16[2,2,4,32,384]{4,3,2,1,0:T(8,128)(2,1)S(1)}, bf16[2,2,4,32,384]{4,3,2,1,0:T(8,128)(2,1)S(1)}, u32[]{:S(2)}, u32[]{:S(2)}) %collective-permute-start.15) | collective-permute-done | bytes 393248 | tf_op jit(solution)/shard_map/ppermute | solution.py:29
  104.2 2.0 copy.64
  106.1 2.0 copy.65
  108.2 1.4 copy-done.5
  109.9 3.4 %collective-permute-start.31 = (bf16[384,384]{1,0:T(8,128)(2,1)S(1)}, bf16[384,384]{1,0:T(8,128)(2,1)S(1)}, u32[]{:S(2)}, u32[]{:S(2)}) collective-permute-start(bf16[384,384]{1,0:T(8,128)(2,1)S(1)} %get-tuple-element.65), channel_id=1, source_target_pairs={{0,3},{1,0},{2,1},{3,2},{4,7},{5,4},{6,5},{7,6},{8,11},{9,8},{10,9... | collective-permute-start | bytes 884744 | tf_op jit(solution)/shard_map/ppermute | solution.py:29
  113.2 2.0 collective-permute-start.32
  115.2 2.3 collective-permute-start.33
  118.9 5.1 %collective-permute-done.31.one = bf16[384,384]{1,0:T(8,128)(2,1)S(1)} collective-permute-done((bf16[384,384]{1,0:T(8,128)(2,1)S(1)}, bf16[384,384]{1,0:T(8,128)(2,1)S(1)}, u32[]{:S(2)}, u32[]{:S(2)}) %collective-permute-start.31) | collective-permute-done | bytes 294944 | tf_op jit(solution)/shard_map/ppermute | solution.py:29
  124.0 6.5 %collective-permute-done.32.two = bf16[384,384]{1,0:T(8,128)(2,1)S(1)} collective-permute-done((bf16[384,384]{1,0:T(8,128)(2,1)S(1)}, bf16[384,384]{1,0:T(8,128)(2,1)S(1)}, u32[]{:S(2)}, u32[]{:S(2)}) %collective-permute-start.32) | collective-permute-done | bytes 294944 | tf_op jit(solution)/shard_map/ppermute | solution.py:29
  130.5 4.2 %collective-permute-done.33.three = bf16[384,384]{1,0:T(8,128)(2,1)S(1)} collective-permute-done((bf16[384,384]{1,0:T(8,128)(2,1)S(1)}, bf16[384,384]{1,0:T(8,128)(2,1)S(1)}, u32[]{:S(2)}, u32[]{:S(2)}) %collective-permute-start.33) | collective-permute-done | bytes 294944 | tf_op jit(solution)/shard_map/ppermute | solution.py:29
  134.7 2.6 shard_map.134
  140.6 18.1 %all_to_all.10 = f32[16,8,128]{2,1,0:T(8,128)S(1)} all-to-all(f32[16,8,128]{2,1,0:T(8,128)S(1)} %broadcast_in_dim.20), channel_id=1, replica_groups=mesh['dp'=16,'tensor'=16] {'dp'}, dimensions={0} | all-to-all | bytes 131072 | tf_op jit(solution)/shard_map/all_to_all | solution.py:50
  158.8 15.6 %all_to_all.11 = f32[16,8,128]{2,1,0:T(8,128)S(1)} all-to-all(f32[16,8,128]{2,1,0:T(8,128)S(1)} %broadcast_in_dim.21), channel_id=1, replica_groups=mesh['dp'=16,'tensor'=16] {'tensor'}, dimensions={0} | all-to-all | bytes 131072 | tf_op jit(solution)/shard_map/all_to_all | solution.py:50
  178.0 11.3 %collective-permute-start.8 = (bf16[384,384]{1,0:T(8,128)(2,1)S(1)}, bf16[384,384]{1,0:T(8,128)(2,1)S(1)}, u32[]{:S(2)}, u32[]{:S(2)}) collective-permute-start(bf16[384,384]{1,0:T(8,128)(2,1)S(1)} %get-tuple-element.16), channel_id=1, source_target_pairs={{0,2},{1,3},{2,0},{3,1},{4,6},{5,7},{6,4},{7,5},{8,10},{9,11},{10,... | collective-permute-start | bytes 884744 | tf_op jit(solution)/shard_map/ppermute | solution.py:29
  189.3 3.8 %collective-permute-done.9 = bf16[384,384]{1,0:T(8,128)(2,1)S(1)} collective-permute-done((bf16[384,384]{1,0:T(8,128)(2,1)S(1)}, bf16[384,384]{1,0:T(8,128)(2,1)S(1)}, u32[]{:S(2)}, u32[]{:S(2)}) %collective-permute-start.9) | collective-permute-done | bytes 294944 | tf_op jit(solution)/shard_map/ppermute | solution.py:29
  193.0 13.3 %collective-permute-done.8 = bf16[384,384]{1,0:T(8,128)(2,1)S(1)} collective-permute-done((bf16[384,384]{1,0:T(8,128)(2,1)S(1)}, bf16[384,384]{1,0:T(8,128)(2,1)S(1)}, u32[]{:S(2)}, u32[]{:S(2)}) %collective-permute-start.8) | collective-permute-done | bytes 294944 | tf_op jit(solution)/shard_map/ppermute | solution.py:29
  206.3 4.7 %collective-permute-done.7 = bf16[384,384]{1,0:T(8,128)(2,1)S(1)} collective-permute-done((bf16[384,384]{1,0:T(8,128)(2,1)S(1)}, bf16[384,384]{1,0:T(8,128)(2,1)S(1)}, u32[]{:S(2)}, u32[]{:S(2)}) %collective-permute-start.7) | collective-permute-done | bytes 294944 | tf_op jit(solution)/shard_map/ppermute | solution.py:29
  217.2 3.5 %collective-permute-start.24 = (bf16[2,2,4,32,384]{4,3,2,1,0:T(8,128)(2,1)S(1)}, bf16[2,2,4,32,384]{4,3,2,1,0:T(8,128)(2,1)S(1)}, u32[]{:S(2)}, u32[]{:S(2)}) collective-permute-start(bf16[2,2,4,32,384]{4,3,2,1,0:T(8,128)(2,1)S(1)} %get-tuple-element.62), channel_id=1, source_target_pairs={{0,8},{1,9},{2,10},{3,11},{4,12},{5,13},{6,14},{7,15},{8,0},{9,1},... | collective-permute-start | bytes 1179656 | tf_op jit(solution)/shard_map/ppermute | solution.py:29
  220.8 5.6 %collective-permute-done.25 = bf16[2,2,4,32,384]{4,3,2,1,0:T(8,128)(2,1)S(1)} collective-permute-done((bf16[2,2,4,32,384]{4,3,2,1,0:T(8,128)(2,1)S(1)}, bf16[2,2,4,32,384]{4,3,2,1,0:T(8,128)(2,1)S(1)}, u32[]{:S(2)}, u32[]{:S(2)}) %collective-permute-start.25) | collective-permute-done | bytes 393248 | tf_op jit(solution)/shard_map/ppermute | solution.py:29
  226.3 9.4 %collective-permute-done.24 = bf16[2,2,4,32,384]{4,3,2,1,0:T(8,128)(2,1)S(1)} collective-permute-done((bf16[2,2,4,32,384]{4,3,2,1,0:T(8,128)(2,1)S(1)}, bf16[2,2,4,32,384]{4,3,2,1,0:T(8,128)(2,1)S(1)}, u32[]{:S(2)}, u32[]{:S(2)}) %collective-permute-start.24) | collective-permute-done | bytes 393248 | tf_op jit(solution)/shard_map/ppermute | solution.py:29
  235.7 1.7 collective-permute-done.23
  237.6 7.2 %collective-permute-start.26 = (bf16[2,4,32,384]{3,2,1,0:T(8,128)(2,1)S(1)}, bf16[2,4,32,384]{3,2,1,0:T(8,128)(2,1)S(1)}, u32[]{:S(2)}, u32[]{:S(2)}) collective-permute-start(bf16[2,4,32,384]{3,2,1,0:T(8,128)(2,1)S(1)} %slice_bitcast_fusion.18), channel_id=1, source_target_pairs={{0,128},{1,129},{2,130},{3,131},{4,132},{5,133},{6,134},{7,135},{8... | collective-permute-start | bytes 589832 | tf_op jit(solution)/shard_map/ppermute | solution.py:29
  244.8 2.4 collective-permute-start.34
  248.4 1.7 collective-permute-start.39
  251.6 5.7 %collective-permute-done.37.refs_4_ = bf16[384,384]{1,0:T(8,128)(2,1)S(1)} collective-permute-done((bf16[384,384]{1,0:T(8,128)(2,1)S(1)}, bf16[384,384]{1,0:T(8,128)(2,1)S(1)}, u32[]{:S(2)}, u32[]{:S(2)}) %collective-permute-start.37) | collective-permute-done | bytes 294944 | tf_op jit(solution)/shard_map/ppermute | solution.py:29
  258.6 2.8 collective-permute-done.39.refs_6_
  262.7 1.7 collective-permute-start.43
  264.3 2.0 collective-permute-start.45
  266.3 2.0 collective-permute-start.47
  268.4 12.8 %collective-permute-done.27 = bf16[2,2,32,384]{3,2,0,1:T(8,128)(2,1)S(1)} collective-permute-done((bf16[2,2,32,384]{3,2,0,1:T(8,128)(2,1)S(1)}, bf16[2,2,32,384]{3,2,0,1:T(8,128)(2,1)S(1)}, u32[]{:S(2)}, u32[]{:S(2)}) %collective-permute-start.27) | collective-permute-done | bytes 98336 | tf_op jit(solution)/shard_map/ppermute | solution.py:29
  284.5 1.6 copy.77
  286.2 1.6 copy.78
  287.8 8.2 %shard_map.135 = bf16[6144,384]{1,0:T(8,128)(2,1)} custom-call(s32[16]{0:T(128)S(1)} %stack.191.order, bf16[384,384]{1,0:T(8,128)(2,1)S(1)} %get-tuple-element.58.refs_0_, bf16[384,384]{1,0:T(8,128)(2,1)S(1)} %collective-permute-done.34.refs_1_, bf16[384,384]{1,0:T(8,128)(2,1)S(1)} %collective-permute-done.35.refs_2_, ...), custom_call_target="tpu_custom_call" | custom-call | bytes 9437184 | tf_op jit(solution)/shard_map/pallas_call | solution.py:154
  (153 shorter events, 40.0 us)
Async XLA Ops:
  2.9 11.3 %collective-permute-start.10 = (bf16[32,2,4,384]{3,0,2,1:T(8,128)(2,1)S(1)}, bf16[32,2,4,384]{3,0,2,1:T(8,128)(2,1)S(1)}, u32[]{:S(2)}, u32[]{:S(2)}) collective-permute-start(bf16[32,2,4,384]{3,0,2,1:T(8,128)(2,1)S(1)} %bitcast.190), channel_id=1, source_target_pairs={{0,16},{1,17},{2,18},{3,19},{4,20},{5,21},{6,22},{7,23},{8,24},{9,... | collective-permute-start | bytes 589832 | tf_op jit(solution)/shard_map/ppermute | solution.py:29
  6.5 11.0 %collective-permute-start.2 = (bf16[4,32,384]{2,1,0:T(8,128)(2,1)S(1)}, bf16[4,32,384]{2,1,0:T(8,128)(2,1)S(1)}, u32[]{:S(2)}, u32[]{:S(2)}) collective-permute-start(bf16[4,32,384]{2,1,0:T(8,128)(2,1)S(1)} %get-tuple-element.86), channel_id=1, source_target_pairs={{0,3},{1,0},{2,1},{3,2},{4,7},{5,4},{6,5},{7,6},{8,11},{9,8},{10,9... | collective-permute-start | bytes 294920 | tf_op jit(solution)/shard_map/ppermute | solution.py:29
  10.9 10.1 %collective-permute-start.1 = (bf16[4,32,384]{2,1,0:T(8,128)(2,1)S(1)}, bf16[4,32,384]{2,1,0:T(8,128)(2,1)S(1)}, u32[]{:S(2)}, u32[]{:S(2)}) collective-permute-start(bf16[4,32,384]{2,1,0:T(8,128)(2,1)S(1)} %get-tuple-element.88), channel_id=1, source_target_pairs={{0,2},{1,3},{2,0},{3,1},{4,6},{5,7},{6,4},{7,5},{8,10},{9,11},{10,... | collective-permute-start | bytes 294920 | tf_op jit(solution)/shard_map/ppermute | solution.py:29
  11.9 9.2 %collective-permute-start = (bf16[4,32,384]{2,1,0:T(8,128)(2,1)S(1)}, bf16[4,32,384]{2,1,0:T(8,128)(2,1)S(1)}, u32[]{:S(2)}, u32[]{:S(2)}) collective-permute-start(bf16[4,32,384]{2,1,0:T(8,128)(2,1)S(1)} %get-tuple-element.87), channel_id=1, source_target_pairs={{0,1},{1,2},{2,3},{3,0},{4,5},{5,6},{6,7},{7,4},{8,9},{9,10},{10,1... | collective-permute-start | bytes 294920 | tf_op jit(solution)/shard_map/ppermute | solution.py:29
  14.3 12.1 %collective-permute-start.13 = (bf16[2,32,2,384]{3,1,2,0:T(8,128)(2,1)S(1)}, bf16[2,32,2,384]{3,1,2,0:T(8,128)(2,1)S(1)}, u32[]{:S(2)}, u32[]{:S(2)}) collective-permute-start(bf16[2,32,2,384]{3,1,2,0:T(8,128)(2,1)S(1)} %get-tuple-element.82), channel_id=1, source_target_pairs={{0,96},{1,97},{2,98},{3,99},{4,100},{5,101},{6,102},{7,103},{8,104... | collective-permute-start | bytes 294920 | tf_op jit(solution)/shard_map/ppermute | solution.py:29
  17.1 10.0 %collective-permute-start.12 = (bf16[2,32,2,384]{3,1,2,0:T(8,128)(2,1)S(1)}, bf16[2,32,2,384]{3,1,2,0:T(8,128)(2,1)S(1)}, u32[]{:S(2)}, u32[]{:S(2)}) collective-permute-start(bf16[2,32,2,384]{3,1,2,0:T(8,128)(2,1)S(1)} %get-tuple-element.81), channel_id=1, source_target_pairs={{0,64},{1,65},{2,66},{3,67},{4,68},{5,69},{6,70},{7,71},{8,72},{9,... | collective-permute-start | bytes 294920 | tf_op jit(solution)/shard_map/ppermute | solution.py:29
  21.1 28.4 %collective-permute-start.6 = (bf16[128,1536]{1,0:T(8,128)(2,1)S(1)}, bf16[128,1536]{1,0:T(8,128)(2,1)S(1)}, u32[]{:S(2)}, u32[]{:S(2)}) collective-permute-start(bf16[128,1536]{1,0:T(8,128)(2,1)S(1)} %pad_maximum_fusion.3), channel_id=1, source_target_pairs={{0,128},{1,129},{2,130},{3,131},{4,132},{5,133},{6,134},{7,135},{8... | collective-permute-start | bytes 1179656 | tf_op jit(solution)/shard_map/ppermute | solution.py:29
  23.4 26.0 %collective-permute-start.5 = (bf16[128,1536]{1,0:T(8,128)(2,1)S(1)}, bf16[128,1536]{1,0:T(8,128)(2,1)S(1)}, u32[]{:S(2)}, u32[]{:S(2)}) collective-permute-start(bf16[128,1536]{1,0:T(8,128)(2,1)S(1)} %pad_maximum_fusion.3), channel_id=1, source_target_pairs={{0,96},{1,97},{2,98},{3,99},{4,100},{5,101},{6,102},{7,103},{8,104... | collective-permute-start | bytes 1179656 | tf_op jit(solution)/shard_map/ppermute | solution.py:29
  26.1 23.4 %collective-permute-start.4 = (bf16[128,1536]{1,0:T(8,128)(2,1)S(1)}, bf16[128,1536]{1,0:T(8,128)(2,1)S(1)}, u32[]{:S(2)}, u32[]{:S(2)}) collective-permute-start(bf16[128,1536]{1,0:T(8,128)(2,1)S(1)} %pad_maximum_fusion.3), channel_id=1, source_target_pairs={{0,64},{1,65},{2,66},{3,67},{4,68},{5,69},{6,70},{7,71},{8,72},{9,... | collective-permute-start | bytes 1179656 | tf_op jit(solution)/shard_map/ppermute | solution.py:29
  26.4 23.1 %collective-permute-start.3 = (bf16[128,1536]{1,0:T(8,128)(2,1)S(1)}, bf16[128,1536]{1,0:T(8,128)(2,1)S(1)}, u32[]{:S(2)}, u32[]{:S(2)}) collective-permute-start(bf16[128,1536]{1,0:T(8,128)(2,1)S(1)} %pad_maximum_fusion.3), channel_id=1, source_target_pairs={{0,32},{1,33},{2,34},{3,35},{4,36},{5,37},{6,38},{7,39},{8,40},{9,... | collective-permute-start | bytes 1179656 | tf_op jit(solution)/shard_map/ppermute | solution.py:29
  27.1 22.0 %collective-permute-start.11 = (bf16[2,32,2,384]{3,1,2,0:T(8,128)(2,1)S(1)}, bf16[2,32,2,384]{3,1,2,0:T(8,128)(2,1)S(1)}, u32[]{:S(2)}, u32[]{:S(2)}) collective-permute-start(bf16[2,32,2,384]{3,1,2,0:T(8,128)(2,1)S(1)} %get-tuple-element.80), channel_id=1, source_target_pairs={{0,32},{1,33},{2,34},{3,35},{4,36},{5,37},{6,38},{7,39},{8,40},{9,... | collective-permute-start | bytes 294920 | tf_op jit(solution)/shard_map/ppermute | solution.py:29
  49.3 26.0 %collective-permute-start.14 = (bf16[2,4,32,384]{3,2,1,0:T(8,128)(2,1)S(1)}, bf16[2,4,32,384]{3,2,1,0:T(8,128)(2,1)S(1)}, u32[]{:S(2)}, u32[]{:S(2)}) collective-permute-start(bf16[2,4,32,384]{3,2,1,0:T(8,128)(2,1)S(1)} %get-tuple-element.78), channel_id=1, source_target_pairs={{0,128},{1,129},{2,130},{3,131},{4,132},{5,133},{6,134},{7,135},{8... | collective-permute-start | bytes 589832 | tf_op jit(solution)/shard_map/ppermute | solution.py:29
  49.4 19.5 %collective-permute-start.19 = (bf16[128,1536]{1,0:T(8,128)(2,1)S(1)}, bf16[128,1536]{1,0:T(8,128)(2,1)S(1)}, u32[]{:S(2)}, u32[]{:S(2)}) collective-permute-start(bf16[128,1536]{1,0:T(8,128)(2,1)S(1)} %collective-permute-done.6), channel_id=1, source_target_pairs={{0,32},{1,33},{2,34},{3,35},{4,36},{5,37},{6,38},{7,39},{8,40},{9,... | collective-permute-start | bytes 1179656 | tf_op jit(solution)/shard_map/ppermute | solution.py:29
  51.9 47.4 %collective-permute-start.18 = (bf16[512,1536]{1,0:T(8,128)(2,1)S(1)}, bf16[512,1536]{1,0:T(8,128)(2,1)S(1)}, u32[]{:S(2)}, u32[]{:S(2)}) collective-permute-start(bf16[512,1536]{1,0:T(8,128)(2,1)S(1)} %pad_maximum_fusion), channel_id=1, source_target_pairs={{0,16},{1,17},{2,18},{3,19},{4,20},{5,21},{6,22},{7,23},{8,24},{9,... | collective-permute-start | bytes 4718600 | tf_op jit(solution)/shard_map/ppermute | solution.py:29
  53.0 16.0 %collective-permute-start.20 = (bf16[128,1536]{1,0:T(8,128)(2,1)S(1)}, bf16[128,1536]{1,0:T(8,128)(2,1)S(1)}, u32[]{:S(2)}, u32[]{:S(2)}) collective-permute-start(bf16[128,1536]{1,0:T(8,128)(2,1)S(1)} %collective-permute-done.6), channel_id=1, source_target_pairs={{0,64},{1,65},{2,66},{3,67},{4,68},{5,69},{6,70},{7,71},{8,72},{9,... | collective-permute-start | bytes 1179656 | tf_op jit(solution)/shard_map/ppermute | solution.py:29
  54.8 19.4 %collective-permute-start.21 = (bf16[128,1536]{1,0:T(8,128)(2,1)S(1)}, bf16[128,1536]{1,0:T(8,128)(2,1)S(1)}, u32[]{:S(2)}, u32[]{:S(2)}) collective-permute-start(bf16[128,1536]{1,0:T(8,128)(2,1)S(1)} %collective-permute-done.6), channel_id=1, source_target_pairs={{0,96},{1,97},{2,98},{3,99},{4,100},{5,101},{6,102},{7,103},{8,104... | collective-permute-start | bytes 1179656 | tf_op jit(solution)/shard_map/ppermute | solution.py:29
  74.3 27.9 %collective-permute-start.22 = (bf16[512,1536]{1,0:T(8,128)(2,1)S(1)}, bf16[512,1536]{1,0:T(8,128)(2,1)S(1)}, u32[]{:S(2)}, u32[]{:S(2)}) collective-permute-start(bf16[512,1536]{1,0:T(8,128)(2,1)S(1)} %constant_dynamic-update-slice_fusion), channel_id=1, source_target_pairs={{0,16},{1,17},{2,18},{3,19},{4,20},{5,21},{6,22},{7,23},{8,24},{9,... | collective-permute-start | bytes 4718600 | tf_op jit(solution)/shard_map/ppermute | solution.py:29
  75.3 19.4 %collective-permute-start.17 = (bf16[2,2,4,32,384]{4,3,2,1,0:T(8,128)(2,1)S(1)}, bf16[2,2,4,32,384]{4,3,2,1,0:T(8,128)(2,1)S(1)}, u32[]{:S(2)}, u32[]{:S(2)}) collective-permute-start(bf16[2,2,4,32,384]{4,3,2,1,0:T(8,128)(2,1)S(1)} %get-tuple-element.76), channel_id=1, source_target_pairs={{0,12},{1,13},{2,14},{3,15},{4,0},{5,1},{6,2},{7,3},{8,4},{9,5},{1... | collective-permute-start | bytes 1179656 | tf_op jit(solution)/shard_map/ppermute | solution.py:29
  77.9 16.8 %collective-permute-start.16 = (bf16[2,2,4,32,384]{4,3,2,1,0:T(8,128)(2,1)S(1)}, bf16[2,2,4,32,384]{4,3,2,1,0:T(8,128)(2,1)S(1)}, u32[]{:S(2)}, u32[]{:S(2)}) collective-permute-start(bf16[2,2,4,32,384]{4,3,2,1,0:T(8,128)(2,1)S(1)} %get-tuple-element.76), channel_id=1, source_target_pairs={{0,8},{1,9},{2,10},{3,11},{4,12},{5,13},{6,14},{7,15},{8,0},{9,1},... | collective-permute-start | bytes 1179656 | tf_op jit(solution)/shard_map/ppermute | solution.py:29
  78.4 20.4 %collective-permute-start.15 = (bf16[2,2,4,32,384]{4,3,2,1,0:T(8,128)(2,1)S(1)}, bf16[2,2,4,32,384]{4,3,2,1,0:T(8,128)(2,1)S(1)}, u32[]{:S(2)}, u32[]{:S(2)}) collective-permute-start(bf16[2,2,4,32,384]{4,3,2,1,0:T(8,128)(2,1)S(1)} %get-tuple-element.76), channel_id=1, source_target_pairs={{0,4},{1,5},{2,6},{3,7},{4,8},{5,9},{6,10},{7,11},{8,12},{9,13},{1... | collective-permute-start | bytes 1179656 | tf_op jit(solution)/shard_map/ppermute | solution.py:29
  109.9 14.1 %collective-permute-start.31 = (bf16[384,384]{1,0:T(8,128)(2,1)S(1)}, bf16[384,384]{1,0:T(8,128)(2,1)S(1)}, u32[]{:S(2)}, u32[]{:S(2)}) collective-permute-start(bf16[384,384]{1,0:T(8,128)(2,1)S(1)} %get-tuple-element.65), channel_id=1, source_target_pairs={{0,3},{1,0},{2,1},{3,2},{4,7},{5,4},{6,5},{7,6},{8,11},{9,8},{10,9... | collective-permute-start | bytes 884744 | tf_op jit(solution)/shard_map/ppermute | solution.py:29
  113.2 17.3 %collective-permute-start.32 = (bf16[384,384]{1,0:T(8,128)(2,1)S(1)}, bf16[384,384]{1,0:T(8,128)(2,1)S(1)}, u32[]{:S(2)}, u32[]{:S(2)}) collective-permute-start(bf16[384,384]{1,0:T(8,128)(2,1)S(1)} %get-tuple-element.64), channel_id=1, source_target_pairs={{0,2},{1,3},{2,0},{3,1},{4,6},{5,7},{6,4},{7,5},{8,10},{9,11},{10,... | collective-permute-start | bytes 884744 | tf_op jit(solution)/shard_map/ppermute | solution.py:29
  115.2 19.5 %collective-permute-start.33 = (bf16[384,384]{1,0:T(8,128)(2,1)S(1)}, bf16[384,384]{1,0:T(8,128)(2,1)S(1)}, u32[]{:S(2)}, u32[]{:S(2)}) collective-permute-start(bf16[384,384]{1,0:T(8,128)(2,1)S(1)} %get-tuple-element.63), channel_id=1, source_target_pairs={{0,1},{1,2},{2,3},{3,0},{4,5},{5,6},{6,7},{7,4},{8,9},{9,10},{10,1... | collective-permute-start | bytes 884744 | tf_op jit(solution)/shard_map/ppermute | solution.py:29
  177.2 15.8 %collective-permute-start.9 = (bf16[384,384]{1,0:T(8,128)(2,1)S(1)}, bf16[384,384]{1,0:T(8,128)(2,1)S(1)}, u32[]{:S(2)}, u32[]{:S(2)}) collective-permute-start(bf16[384,384]{1,0:T(8,128)(2,1)S(1)} %get-tuple-element.16), channel_id=1, source_target_pairs={{0,3},{1,0},{2,1},{3,2},{4,7},{5,4},{6,5},{7,6},{8,11},{9,8},{10,9... | collective-permute-start | bytes 884744 | tf_op jit(solution)/shard_map/ppermute | solution.py:29
  178.0 28.4 %collective-permute-start.8 = (bf16[384,384]{1,0:T(8,128)(2,1)S(1)}, bf16[384,384]{1,0:T(8,128)(2,1)S(1)}, u32[]{:S(2)}, u32[]{:S(2)}) collective-permute-start(bf16[384,384]{1,0:T(8,128)(2,1)S(1)} %get-tuple-element.16), channel_id=1, source_target_pairs={{0,2},{1,3},{2,0},{3,1},{4,6},{5,7},{6,4},{7,5},{8,10},{9,11},{10,... | collective-permute-start | bytes 884744 | tf_op jit(solution)/shard_map/ppermute | solution.py:29
  189.2 21.8 %collective-permute-start.7 = (bf16[384,384]{1,0:T(8,128)(2,1)S(1)}, bf16[384,384]{1,0:T(8,128)(2,1)S(1)}, u32[]{:S(2)}, u32[]{:S(2)}) collective-permute-start(bf16[384,384]{1,0:T(8,128)(2,1)S(1)} %get-tuple-element.16), channel_id=1, source_target_pairs={{0,1},{1,2},{2,3},{3,0},{4,5},{5,6},{6,7},{7,4},{8,9},{9,10},{10,1... | collective-permute-start | bytes 884744 | tf_op jit(solution)/shard_map/ppermute | solution.py:29
  217.1 9.2 %collective-permute-start.25 = (bf16[2,2,4,32,384]{4,3,2,1,0:T(8,128)(2,1)S(1)}, bf16[2,2,4,32,384]{4,3,2,1,0:T(8,128)(2,1)S(1)}, u32[]{:S(2)}, u32[]{:S(2)}) collective-permute-start(bf16[2,2,4,32,384]{4,3,2,1,0:T(8,128)(2,1)S(1)} %get-tuple-element.61), channel_id=1, source_target_pairs={{0,4},{1,5},{2,6},{3,7},{4,8},{5,9},{6,10},{7,11},{8,12},{9,13},{1... | collective-permute-start | bytes 1179656 | tf_op jit(solution)/shard_map/ppermute | solution.py:29
  217.2 18.5 %collective-permute-start.24 = (bf16[2,2,4,32,384]{4,3,2,1,0:T(8,128)(2,1)S(1)}, bf16[2,2,4,32,384]{4,3,2,1,0:T(8,128)(2,1)S(1)}, u32[]{:S(2)}, u32[]{:S(2)}) collective-permute-start(bf16[2,2,4,32,384]{4,3,2,1,0:T(8,128)(2,1)S(1)} %get-tuple-element.62), channel_id=1, source_target_pairs={{0,8},{1,9},{2,10},{3,11},{4,12},{5,13},{6,14},{7,15},{8,0},{9,1},... | collective-permute-start | bytes 1179656 | tf_op jit(solution)/shard_map/ppermute | solution.py:29
  220.7 16.7 %collective-permute-start.23 = (bf16[2,2,4,32,384]{4,3,2,1,0:T(8,128)(2,1)S(1)}, bf16[2,2,4,32,384]{4,3,2,1,0:T(8,128)(2,1)S(1)}, u32[]{:S(2)}, u32[]{:S(2)}) collective-permute-start(bf16[2,2,4,32,384]{4,3,2,1,0:T(8,128)(2,1)S(1)} %get-tuple-element.60), channel_id=1, source_target_pairs={{0,12},{1,13},{2,14},{3,15},{4,0},{5,1},{6,2},{7,3},{8,4},{9,5},{1... | collective-permute-start | bytes 1179656 | tf_op jit(solution)/shard_map/ppermute | solution.py:29
  220.7 29.4 %collective-permute-start.35 = (bf16[384,384]{1,0:T(8,128)(2,1)S(1)}, bf16[384,384]{1,0:T(8,128)(2,1)S(1)}, u32[]{:S(2)}, u32[]{:S(2)}) collective-permute-start(bf16[384,384]{1,0:T(8,128)(2,1)S(1)} %get-tuple-element.58.refs_0_), channel_id=1, source_target_pairs={{0,32},{1,33},{2,34},{3,35},{4,36},{5,37},{6,38},{7,39},{8,40},{9,... | collective-permute-start | bytes 884744 | tf_op jit(solution)/shard_map/ppermute | solution.py:29
  237.6 12.5 %collective-permute-start.26 = (bf16[2,4,32,384]{3,2,1,0:T(8,128)(2,1)S(1)}, bf16[2,4,32,384]{3,2,1,0:T(8,128)(2,1)S(1)}, u32[]{:S(2)}, u32[]{:S(2)}) collective-permute-start(bf16[2,4,32,384]{3,2,1,0:T(8,128)(2,1)S(1)} %slice_bitcast_fusion.18), channel_id=1, source_target_pairs={{0,128},{1,129},{2,130},{3,131},{4,132},{5,133},{6,134},{7,135},{8... | collective-permute-start | bytes 589832 | tf_op jit(solution)/shard_map/ppermute | solution.py:29
  244.8 6.2 %collective-permute-start.34 = (bf16[384,384]{1,0:T(8,128)(2,1)S(1)}, bf16[384,384]{1,0:T(8,128)(2,1)S(1)}, u32[]{:S(2)}, u32[]{:S(2)}) collective-permute-start(bf16[384,384]{1,0:T(8,128)(2,1)S(1)} %get-tuple-element.58.refs_0_), channel_id=1, source_target_pairs={{0,16},{1,17},{2,18},{3,19},{4,20},{5,21},{6,22},{7,23},{8,24},{9,... | collective-permute-start | bytes 884744 | tf_op jit(solution)/shard_map/ppermute | solution.py:29
  247.2 10.2 %collective-permute-start.37 = (bf16[384,384]{1,0:T(8,128)(2,1)S(1)}, bf16[384,384]{1,0:T(8,128)(2,1)S(1)}, u32[]{:S(2)}, u32[]{:S(2)}) collective-permute-start(bf16[384,384]{1,0:T(8,128)(2,1)S(1)} %get-tuple-element.58.refs_0_), channel_id=1, source_target_pairs={{0,64},{1,65},{2,66},{3,67},{4,68},{5,69},{6,70},{7,71},{8,72},{9,... | collective-permute-start | bytes 884744 | tf_op jit(solution)/shard_map/ppermute | solution.py:29
  248.4 12.9 %collective-permute-start.39 = (bf16[384,384]{1,0:T(8,128)(2,1)S(1)}, bf16[384,384]{1,0:T(8,128)(2,1)S(1)}, u32[]{:S(2)}, u32[]{:S(2)}) collective-permute-start(bf16[384,384]{1,0:T(8,128)(2,1)S(1)} %get-tuple-element.58.refs_0_), channel_id=1, source_target_pairs={{0,96},{1,97},{2,98},{3,99},{4,100},{5,101},{6,102},{7,103},{8,104... | collective-permute-start | bytes 884744 | tf_op jit(solution)/shard_map/ppermute | solution.py:29
  250.1 12.6 %collective-permute-start.41 = (bf16[384,384]{1,0:T(8,128)(2,1)S(1)}, bf16[384,384]{1,0:T(8,128)(2,1)S(1)}, u32[]{:S(2)}, u32[]{:S(2)}) collective-permute-start(bf16[384,384]{1,0:T(8,128)(2,1)S(1)} %get-tuple-element.58.refs_0_), channel_id=1, source_target_pairs={{0,128},{1,129},{2,130},{3,131},{4,132},{5,133},{6,134},{7,135},{8... | collective-permute-start | bytes 884744 | tf_op jit(solution)/shard_map/ppermute | solution.py:29
  250.1 14.2 %collective-permute-start.36 = (bf16[384,384]{1,0:T(8,128)(2,1)S(1)}, bf16[384,384]{1,0:T(8,128)(2,1)S(1)}, u32[]{:S(2)}, u32[]{:S(2)}) collective-permute-start(bf16[384,384]{1,0:T(8,128)(2,1)S(1)} %collective-permute-done.35.refs_2_), channel_id=1, source_target_pairs={{0,16},{1,17},{2,18},{3,19},{4,20},{5,21},{6,22},{7,23},{8,24},{9,... | collective-permute-start | bytes 884744 | tf_op jit(solution)/shard_map/ppermute | solution.py:29
  251.0 15.3 %collective-permute-start.29 = (bf16[2,2,32,384]{3,2,0,1:T(8,128)(2,1)S(1)}, bf16[2,2,32,384]{3,2,0,1:T(8,128)(2,1)S(1)}, u32[]{:S(2)}, u32[]{:S(2)}) collective-permute-start(bf16[2,2,32,384]{3,2,0,1:T(8,128)(2,1)S(1)} %get-tuple-element.73), channel_id=1, source_target_pairs={{0,32},{1,33},{2,34},{3,35},{4,36},{5,37},{6,38},{7,39},{8,40},{9,... | collective-permute-start | bytes 294920 | tf_op jit(solution)/shard_map/ppermute | solution.py:29
  257.4 10.9 %collective-permute-start.28 = (bf16[2,2,32,384]{3,2,0,1:T(8,128)(2,1)S(1)}, bf16[2,2,32,384]{3,2,0,1:T(8,128)(2,1)S(1)}, u32[]{:S(2)}, u32[]{:S(2)}) collective-permute-start(bf16[2,2,32,384]{3,2,0,1:T(8,128)(2,1)S(1)} %get-tuple-element.74), channel_id=1, source_target_pairs={{0,64},{1,65},{2,66},{3,67},{4,68},{5,69},{6,70},{7,71},{8,72},{9,... | collective-permute-start | bytes 294920 | tf_op jit(solution)/shard_map/ppermute | solution.py:29
  261.3 21.2 %collective-permute-start.38 = (bf16[384,384]{1,0:T(8,128)(2,1)S(1)}, bf16[384,384]{1,0:T(8,128)(2,1)S(1)}, u32[]{:S(2)}, u32[]{:S(2)}) collective-permute-start(bf16[384,384]{1,0:T(8,128)(2,1)S(1)} %collective-permute-done.37.refs_4_), channel_id=1, source_target_pairs={{0,16},{1,17},{2,18},{3,19},{4,20},{5,21},{6,22},{7,23},{8,24},{9,... | collective-permute-start | bytes 884744 | tf_op jit(solution)/shard_map/ppermute | solution.py:29
  262.7 19.9 %collective-permute-start.43 = (bf16[384,384]{1,0:T(8,128)(2,1)S(1)}, bf16[384,384]{1,0:T(8,128)(2,1)S(1)}, u32[]{:S(2)}, u32[]{:S(2)}) collective-permute-start(bf16[384,384]{1,0:T(8,128)(2,1)S(1)} %collective-permute-done.41.refs_8_), channel_id=1, source_target_pairs={{0,32},{1,33},{2,34},{3,35},{4,36},{5,37},{6,38},{7,39},{8,40},{9,... | collective-permute-start | bytes 884744 | tf_op jit(solution)/shard_map/ppermute | solution.py:29
  264.3 18.7 %collective-permute-start.45 = (bf16[384,384]{1,0:T(8,128)(2,1)S(1)}, bf16[384,384]{1,0:T(8,128)(2,1)S(1)}, u32[]{:S(2)}, u32[]{:S(2)}) collective-permute-start(bf16[384,384]{1,0:T(8,128)(2,1)S(1)} %collective-permute-done.41.refs_8_), channel_id=1, source_target_pairs={{0,64},{1,65},{2,66},{3,67},{4,68},{5,69},{6,70},{7,71},{8,72},{9,... | collective-permute-start | bytes 884744 | tf_op jit(solution)/shard_map/ppermute | solution.py:29
  266.3 16.9 %collective-permute-start.47 = (bf16[384,384]{1,0:T(8,128)(2,1)S(1)}, bf16[384,384]{1,0:T(8,128)(2,1)S(1)}, u32[]{:S(2)}, u32[]{:S(2)}) collective-permute-start(bf16[384,384]{1,0:T(8,128)(2,1)S(1)} %collective-permute-done.41.refs_8_), channel_id=1, source_target_pairs={{0,96},{1,97},{2,98},{3,99},{4,100},{5,101},{6,102},{7,103},{8,104... | collective-permute-start | bytes 884744 | tf_op jit(solution)/shard_map/ppermute | solution.py:29
  268.3 12.9 %collective-permute-start.27 = (bf16[2,2,32,384]{3,2,0,1:T(8,128)(2,1)S(1)}, bf16[2,2,32,384]{3,2,0,1:T(8,128)(2,1)S(1)}, u32[]{:S(2)}, u32[]{:S(2)}) collective-permute-start(bf16[2,2,32,384]{3,2,0,1:T(8,128)(2,1)S(1)} %get-tuple-element.72), channel_id=1, source_target_pairs={{0,96},{1,97},{2,98},{3,99},{4,100},{5,101},{6,102},{7,103},{8,104... | collective-permute-start | bytes 294920 | tf_op jit(solution)/shard_map/ppermute | solution.py:29
  282.5 5.3 %collective-permute-start.42 = (bf16[384,384]{1,0:T(8,128)(2,1)S(1)}, bf16[384,384]{1,0:T(8,128)(2,1)}, u32[]{:S(2)}, u32[]{:S(2)}) collective-permute-start(bf16[384,384]{1,0:T(8,128)(2,1)S(1)} %collective-permute-done.41.refs_8_), channel_id=1, source_target_pairs={{0,16},{1,17},{2,18},{3,19},{4,20},{5,21},{6,22},{7,23},{8,24},{9,... | collective-permute-start | bytes 884744 | tf_op jit(solution)/shard_map/ppermute | solution.py:29
  282.6 5.2 %collective-permute-start.44 = (bf16[384,384]{1,0:T(8,128)(2,1)S(1)}, bf16[384,384]{1,0:T(8,128)(2,1)}, u32[]{:S(2)}, u32[]{:S(2)}) collective-permute-start(bf16[384,384]{1,0:T(8,128)(2,1)S(1)} %collective-permute-done.43.refs_10_), channel_id=1, source_target_pairs={{0,16},{1,17},{2,18},{3,19},{4,20},{5,21},{6,22},{7,23},{8,24},{9,... | collective-permute-start | bytes 884744 | tf_op jit(solution)/shard_map/ppermute | solution.py:29
  283.1 4.7 %collective-permute-start.46 = (bf16[384,384]{1,0:T(8,128)(2,1)S(1)}, bf16[384,384]{1,0:T(8,128)(2,1)}, u32[]{:S(2)}, u32[]{:S(2)}) collective-permute-start(bf16[384,384]{1,0:T(8,128)(2,1)S(1)} %collective-permute-done.45.refs_12_), channel_id=1, source_target_pairs={{0,16},{1,17},{2,18},{3,19},{4,20},{5,21},{6,22},{7,23},{8,24},{9,... | collective-permute-start | bytes 884744 | tf_op jit(solution)/shard_map/ppermute | solution.py:29
  283.2 4.6 %collective-permute-start.48 = (bf16[384,384]{1,0:T(8,128)(2,1)S(1)}, bf16[384,384]{1,0:T(8,128)(2,1)}, u32[]{:S(2)}, u32[]{:S(2)}) collective-permute-start(bf16[384,384]{1,0:T(8,128)(2,1)S(1)} %collective-permute-done.47.refs_14_), channel_id=1, source_target_pairs={{0,16},{1,17},{2,18},{3,19},{4,20},{5,21},{6,22},{7,23},{8,24},{9,... | collective-permute-start | bytes 884744 | tf_op jit(solution)/shard_map/ppermute | solution.py:29
  284.3 11.7 %collective-permute-start.30 = (bf16[2,4,32,384]{3,2,0,1:T(8,128)(2,1)}, bf16[2,4,32,384]{3,2,0,1:T(8,128)(2,1)}, u32[]{:S(2)}, u32[]{:S(2)}) collective-permute-start(bf16[2,4,32,384]{3,2,0,1:T(8,128)(2,1)} %slice_bitcast_fusion.16), channel_id=1, source_target_pairs={{0,16},{1,17},{2,18},{3,19},{4,20},{5,21},{6,22},{7,23},{8,24},{9,... | collective-permute-start | bytes 589832 | tf_op jit(solution)/shard_map/ppermute | solution.py:29
  (20 other events, 230.6 us)
where the time goes:
time: 305 us; the launch traced here: 300 us
  waiting for transfers between devices  137 us (45%)
  starting transfers between devices  78.5 us (26%)
  blocking collectives  33.7 us (11%)
  local copies, waits for them, and re-layouts  21.3 us (7%)
  Pallas kernels  10.8 us (4%)
  matrix products  7.2 us (2%)
  other arithmetic  6.93 us (2%)
  between operations  4.09 us (1%)
    ppermute x49, waiting for transfers between devices, shift(): return lax.ppermute(array, BOTH, pairs)  137 us
    ppermute x49, starting transfers between devices, shift(): return lax.ppermute(array, BOTH, pairs)  78.5 us
    all_to_all x2, blocking collectives, total_of(): row = jnp.sum(lax.all_to_all(spread, axis, 0, 0, tiled=True), axis=0)  33.7 us
    unnamed x45, local copies, waits for them, and re-layouts  9.2 us
    pallas_call x1, Pallas kernels, place_rows(): pl.pallas_call(functools.partial(place_kernel, count), out_shape=jax.Shap...  8.18 us
  transfers between devices with their start and end apart: 49, of which 18 were waited for; matrix products, arithmetic and copies ran while one was open for 4% of the time, Pallas kernels for 3%

commit v1 on v0

v1 whole, which is shorter than its diff:
```python
import math

import jax
import jax.numpy as jnp
from jax import lax
from jax.experimental import pallas as pl
from jax.experimental.pallas import tpu as pltpu
from jax.sharding import PartitionSpec as P

FEAT_IN = 6144
SIZES = (2, 4, 2, 4, 4)
BOTH = ("dp", "tensor")
NEAR = [list(range(8)), list(range(8, 16))]
BF16, F32 = jnp.bfloat16, jnp.float32


def shift(array, z=0, y=0, core=0, x=0, high=0):
    moves = (z, y, core, x, high)
    pairs = []
    for source in range(math.prod(SIZES)):
        rest, place = source, []
        for size in reversed(SIZES):
            place.append(rest % size)
            rest //= size
        target = 0
        for size, at, move in zip(SIZES, reversed(place), moves):
            target = target * size + (at + move) % size
        pairs.append((source, target))
    return lax.ppermute(array, BOTH, pairs)


def roll(array, start):
    return lax.dynamic_slice_in_dim(
        jnp.concatenate([array, array], axis=0), start, array.shape[0], axis=0
    )


def take(array, index, axis):
    return lax.dynamic_index_in_dim(array, index, axis, keepdims=False)


def after(array, *others):
    return lax.optimization_barrier((array,) + others)[0]


def total_of(row, axis):
    spread = jnp.broadcast_to(row[None], (16, 8, 128))
    return jnp.sum(lax.all_to_all(spread, axis, 0, 0, tiled=True), axis=0)


def moments_kernel(
    own, other, master, mcode, mscale, scode, sscale,
    update, new_mcode, new_mscale, new_scode, new_sscale, sums,
):
    rows, cols = master.shape
    blocks = mscale.shape[1]
    wide = cols // blocks
    step = 64
    sums[...] = jnp.zeros_like(sums)

    def body(i, carry):
        at = pl.ds(pl.multiple_of(i * step, step), step)
        mscales, sscales = mscale[at, :], sscale[at, :]
        new_m, new_s = [], []
        for b in range(blocks):
            cut = slice(b * wide, (b + 1) * wide)
            grad = own[at, cut] + other[at, cut].astype(F32)
            weight = master[at, cut]
            moment = mcode[at, cut].astype(F32) * mscales[:, b : b + 1]
            second = scode[at, cut].astype(F32) * sscales[:, b : b + 1]
            moment = 0.9 * moment + 0.1 * grad
            second = 0.999 * second + 0.001 * grad * grad
            change = (
                moment / (1.0 - 0.9**10) / (jnp.sqrt(second / (1.0 - 0.999**10)) + 1e-06)
                + 0.1 * weight
            )
            update[at, cut] = change
            mtop = 2.0 * jnp.max(jnp.abs(moment), axis=1, keepdims=True) + 1e-06
            stop = 2.0 * jnp.max(jnp.abs(second), axis=1, keepdims=True) + 1e-06
            new_mcode[at, cut] = (moment / mtop).astype(BF16)
            new_scode[at, cut] = (second / stop).astype(BF16)
            new_m.append(mtop)
            new_s.append(stop)
            sums[0:1, :] += jnp.sum(weight * weight, axis=0, keepdims=True)
            sums[1:2, :] += jnp.sum(change * change, axis=0, keepdims=True)
        new_mscale[at, :] = jnp.concatenate(new_m, axis=1)
        new_sscale[at, :] = jnp.concatenate(new_s, axis=1)
        return carry

    lax.fori_loop(0, rows // step, body, 0)
    sums[...] = jnp.broadcast_to(jnp.sum(sums[...], axis=1, keepdims=True), sums.shape)


def moments(own, other, master, mcode, mscale, scode, sscale):
    like = lambda a, dtype: jax.ShapeDtypeStruct(a.shape, dtype)
    block = master.shape[1] // mscale.shape[1]
    return pl.pallas_call(
        moments_kernel,
        out_shape=(
            like(master, F32),
            like(master, BF16),
            like(mscale, F32),
            like(master, BF16),
            like(sscale, F32),
            jax.ShapeDtypeStruct((8, block), F32),
        ),
        in_specs=[pl.BlockSpec(memory_space=pltpu.VMEM)] * 7,
        out_specs=[pl.BlockSpec(memory_space=pltpu.VMEM)] * 6,
        compiler_params=pltpu.CompilerParams(vmem_limit_bytes=32 * 1024 * 1024),
        cost_estimate=pl.CostEstimate(
            flops=master.size, bytes_accessed=master.size, transcendentals=0
        ),
    )(own, other, master, mcode, mscale, scode, sscale)


def local(layer_input, out_grad, master, moment_code, moment_scale, second_code, second_scale):
    inv_root = 1.0 / math.sqrt(FEAT_IN)
    d, t = lax.axis_index("dp"), lax.axis_index("tensor")
    z, x, high = d // 8, t // 4, t % 4
    few, feat = layer_input.shape
    rows, cols = master.shape
    steps = (1, 2, 3)

    grads = out_grad.reshape(4, 4, few, cols).transpose(1, 0, 2, 3)
    grads = roll(grads[::-1], 3 - high)
    parts = [take(grads, x, 1)] + [shift(take(grads, (x + s) % 4, 1), x=s) for s in steps]
    mine = layer_input.reshape(few, 2, 8, rows).transpose(2, 0, 1, 3).reshape(8, few, 2 * rows)
    mine = lax.all_to_all(mine, "dp", 0, 0, tiled=True, axis_index_groups=NEAR)
    moved = [shift(mine, high=s) for s in steps]
    weights = master.astype(BF16)
    far = shift(weights, z=1)
    parts, far = lax.optimization_barrier((parts, mine, far))[::2]
    weights = jnp.concatenate([jnp.where(z == 0, weights, far), jnp.where(z == 0, far, weights)])
    weights = jnp.concatenate([weights] + [shift(weights, x=s) for s in steps], axis=1)
    near = jnp.concatenate(parts, axis=2).reshape(4 * few, 4 * cols)
    wide = lax.all_gather(near, "dp", axis=0, tiled=True, axis_index_groups=NEAR)

    acts = jnp.stack([mine] + moved, axis=1).reshape(32 * few, 2 * rows)

    acts = after(acts, weights)
    part = jnp.einsum("tk,tn->kn", acts, wide, preferred_element_type=F32) * inv_root
    part = [part[:, s * cols : (s + 1) * cols] for s in range(4)]
    sends = [part[s].astype(BF16) for s in steps]
    others = [shift(send, x=-s) for s, send in zip(steps, sends)]

    weights = after(weights, *sends)
    outs = jnp.einsum("tn,kn->tk", wide, weights, preferred_element_type=F32) * inv_root
    outs = outs.reshape(8, 4, few, 2 * rows)
    pieces = [outs[:, s].astype(BF16) for s in steps]
    others = lax.optimization_barrier((tuple(others), tuple(pieces)))[0]
    grad = part[0] + sum(other.astype(F32) for other in others)
    grad = grad.reshape(2, rows, cols)
    far = shift(take(grad, 1 - z, 0).astype(BF16), z=1)
    update, new_moment_code, new_moment_scale, new_second_code, new_second_scale, sums = moments(
        take(grad, z, 0), far, master, moment_code, moment_scale, second_code, second_scale
    )
    summed = outs[:, 0]
    for s, piece in zip(steps, pieces):
        summed = summed + shift(piece, high=-s).astype(F32)
    sums = total_of(sums, "dp")
    summed, sums = lax.optimization_barrier((summed, sums))
    sums = total_of(sums, "tensor")
    weight_sq, update_sq = sums[0, 0], sums[1, 0]
    trust_ratio = jnp.sqrt(weight_sq) / (jnp.sqrt(update_sq) + 1e-06)
    rate = 0.02 * trust_ratio
    new_master = master - rate * update
    new_weight = lax.all_gather(new_master.astype(BF16), "dp", axis=0, tiled=True)

    back = lax.all_to_all(
        after(summed.astype(BF16), sums), "dp", 0, 0, tiled=True, axis_index_groups=NEAR
    )
    input_grad = back.reshape(8, few, 2, rows).transpose(1, 2, 0, 3).reshape(few, feat)

    return (
        input_grad,
        new_master,
        new_moment_code,
        new_moment_scale,
        new_second_code,
        new_second_scale,
        new_weight,
        trust_ratio,
    )


def solution(mesh):
    placed = (P(BOTH, None),) + (P("dp", "tensor"),) * 6
    return jax.shard_map(
        local,
        mesh=mesh,
        in_specs=placed,
        out_specs=(P(BOTH, None),) + (P("dp", "tensor"),) * 5 + (P(None, "tensor"), P()),
        check_vma=False,
    )
```

time: 305 us -> 218 us (0.71); the launches traced: 300 us -> 217 us
  waiting for transfers between devices: 137 us -> 96.1 us
  starting transfers between devices: 78.5 us -> 53.7 us
  blocking collectives: 33.7 us -> 14.2 us
  between operations: 4.09 us -> 16.9 us
  Pallas kernels: 10.8 us -> 2.62 us
  local copies, waits for them, and re-layouts: 21.3 us -> 16.5 us
    ppermute x49 -> x17, waiting for transfers between devices: 137 us -> 61.9 us  [shift(): return lax.ppermute(array, BOTH, pairs)]
    ppermute x49 -> x17, starting transfers between devices: 78.5 us -> 35.1 us  [shift(): return lax.ppermute(array, BOTH, pairs)]
    all_gather x0 -> x2, waiting for transfers between devices: none -> 19.7 us  [the longest x1 19.7 us: local(): lax.all_gather(new_master.astype(BF16), 'dp', axis=0, tiled=True)]
    all_to_all x2 -> x1, blocking collectives: 33.7 us -> 14.2 us  [total_of(): return jnp.sum(lax.all_to_all(spread, axis, 0, 0, tiled=True), axis=0)]
    all_to_all x0 -> x3, starting transfers between devices: none -> 18.5 us  [the longest x1 6.89 us: total_of(): return jnp.sum(lax.all_to_all(spread, axis, 0, 0, tiled=True), axis=0)]
    all_to_all x0 -> x3, waiting for transfers between devices: none -> 14.4 us  [the longest x1 11 us: local(): lax.all_to_all(after(summed.astype(BF16), sums), 'dp', 0, 0, tiled=True,...]
    pallas_call x1 -> x0, Pallas kernels: 8.18 us -> none  [place_rows(): pl.pallas_call(functools.partial(place_kernel, count), out_shape=jax.Shap...]
    unnamed x45 -> x27, local copies, waits for them, and re-layouts: 9.2 us -> 11.1 us
  transfers between devices with their start and end apart: 49 -> 22, of which waited for: 18 -> 12; matrix products, arithmetic and copies ran while one was open for 4% -> 8% of each run, Pallas kernels for 3% -> 1%
where the time goes in v1:
time: 218 us; the launch traced here: 217 us
  waiting for transfers between devices  96.1 us (44%)
  starting transfers between devices  53.7 us (25%)
  between operations  16.9 us (8%)
  local copies, waits for them, and re-layouts  16.5 us (8%)
  blocking collectives  14.2 us (7%)
  other arithmetic  9.84 us (5%)
  matrix products  7.36 us (3%)
  Pallas kernels  2.62 us (1%)
    ppermute x17, waiting for transfers between devices, shift(): return lax.ppermute(array, BOTH, pairs)  61.9 us
    ppermute x17, starting transfers between devices, shift(): return lax.ppermute(array, BOTH, pairs)  35.1 us
    all_gather x1, waiting for transfers between devices, local(): lax.all_gather(new_master.astype(BF16), 'dp', axis=0, tiled=True)  19.7 us
    all_to_all x1, blocking collectives, total_of(): return jnp.sum(lax.all_to_all(spread, axis, 0, 0, tiled=True), axis=0)  14.2 us
    unnamed x27, local copies, waits for them, and re-layouts  11.1 us
    all_to_all x1, waiting for transfers between devices, local(): lax.all_to_all(after(summed.astype(BF16), sums), 'dp', 0, 0, tiled=True,...  11 us
    all_to_all x1, starting transfers between devices, total_of(): return jnp.sum(lax.all_to_all(spread, axis, 0, 0, tiled=True), axis=0)  6.89 us
    all_to_all x1, starting transfers between devices, local(): mine = lax.all_to_all(mine, 'dp', 0, 0, tiled=True, axis_index_groups=NEAR)  6.6 us
  transfers between devices with their start and end apart: 22, of which 12 were waited for; matrix products, arithmetic and copies ran while one was open for 8% of the time, Pallas kernels for 1%

profile of v1, /device:TPU:1, one launch (start us, length us, event | category | flops | bytes accessed | tf_op | source)
XLA Modules:
  0.0 217.1 jit_solution(14131490688717074096)
XLA Ops:
  7.2 1.1 copy.46
  8.6 1.0 reshape.56
  9.6 6.6 %all-to-all-start = ((bf16[8,32,768]{2,1,0:T(8,128)(2,1)}), bf16[8,32,768]{2,1,0:T(8,128)(2,1)S(1)}, u32[]{:S(2)}, u32[]{:S(2)}) async-start(bf16[8,32,768]{2,1,0:T(8,128)(2,1)} %reshape.56), calls=%async_computation | async-start | bytes 786432 | tf_op jit(solution)/shard_map/all_to_all | solution.py:128
  16.3 1.1 collective-permute-start.3
  17.6 1.3 collective-permute-start
  18.9 2.5 %collective-permute-start.1 = (bf16[4,32,384]{2,1,0:T(8,128)(2,1)S(1)}, bf16[4,32,384]{2,1,0:T(8,128)(2,1)S(1)}, u32[]{:S(2)}, u32[]{:S(2)}) collective-permute-start(bf16[4,32,384]{2,1,0:T(8,128)(2,1)S(1)} %get-tuple-element.83), channel_id=1, source_target_pairs={{0,8},{1,9},{2,10},{3,11},{4,12},{5,13},{6,14},{7,15},{8,0},{9,1},... | collective-permute-start | bytes 294920 | tf_op jit(solution)/shard_map/ppermute | solution.py:29
  21.4 1.2 collective-permute-start.2
  23.0 3.1 %collective-permute-done.1 = bf16[4,32,384]{2,1,0:T(8,128)(2,1)S(1)} collective-permute-done((bf16[4,32,384]{2,1,0:T(8,128)(2,1)S(1)}, bf16[4,32,384]{2,1,0:T(8,128)(2,1)S(1)}, u32[]{:S(2)}, u32[]{:S(2)}) %collective-permute-start.1) | collective-permute-done | bytes 98336 | tf_op jit(solution)/shard_map/ppermute | solution.py:29
  26.1 0.8 pad_maximum_fusion.3
  26.9 6.1 %collective-permute-start.8 = (bf16[8,32,768]{2,1,0:T(8,128)(2,1)S(1)}, bf16[8,32,768]{2,1,0:T(8,128)(2,1)S(1)}, u32[]{:S(2)}, u32[]{:S(2)}) collective-permute-start(bf16[8,32,768]{2,1,0:T(8,128)(2,1)S(1)} %all-to-all-done), channel_id=1, source_target_pairs={{0,2},{1,3},{2,0},{3,1},{4,6},{5,7},{6,4},{7,5},{8,10},{9,11},{10,... | collective-permute-start | bytes 1179656 | tf_op jit(solution)/shard_map/ppermute | solution.py:29
  33.1 0.9 pad_maximum_fusion.2
  34.5 2.3 %collective-permute-start.5 = (bf16[768,384]{1,0:T(8,128)(2,1)}, bf16[768,384]{1,0:T(8,128)(2,1)}, u32[]{:S(2)}, u32[]{:S(2)}) collective-permute-start(bf16[768,384]{1,0:T(8,128)(2,1)} %pad_maximum_fusion.2), channel_id=1, source_target_pairs={{0,8},{1,9},{2,10},{3,11},{4,12},{5,13},{6,14},{7,15},{8,0},{9,1},... | collective-permute-start | bytes 1769480 | tf_op jit(solution)/shard_map/ppermute | solution.py:29
  36.8 1.4 collective-permute-start.6
  38.4 3.9 %collective-permute-done.8 = bf16[8,32,768]{2,1,0:T(8,128)(2,1)S(1)} collective-permute-done((bf16[8,32,768]{2,1,0:T(8,128)(2,1)S(1)}, bf16[8,32,768]{2,1,0:T(8,128)(2,1)S(1)}, u32[]{:S(2)}, u32[]{:S(2)}) %collective-permute-start.8) | collective-permute-done | bytes 393248 | tf_op jit(solution)/shard_map/ppermute | solution.py:29
  42.3 10.8 %collective-permute-start.7 = (bf16[8,32,768]{2,1,0:T(8,128)(2,1)S(1)}, bf16[8,32,768]{2,1,0:T(8,128)(2,1)S(1)}, u32[]{:S(2)}, u32[]{:S(2)}) collective-permute-start(bf16[8,32,768]{2,1,0:T(8,128)(2,1)S(1)} %all-to-all-done), channel_id=1, source_target_pairs={{0,1},{1,2},{2,3},{3,0},{4,5},{5,6},{6,7},{7,4},{8,9},{9,10},{10,1... | collective-permute-start | bytes 1179656 | tf_op jit(solution)/shard_map/ppermute | solution.py:29
  53.1 15.3 %collective-permute-done.9 = bf16[8,32,768]{2,1,0:T(8,128)(2,1)S(1)} collective-permute-done((bf16[8,32,768]{2,1,0:T(8,128)(2,1)S(1)}, bf16[8,32,768]{2,1,0:T(8,128)(2,1)S(1)}, u32[]{:S(2)}, u32[]{:S(2)}) %collective-permute-start.9) | collective-permute-done | bytes 393248 | tf_op jit(solution)/shard_map/ppermute | solution.py:29
  68.4 3.8 %collective-permute-done.7 = bf16[8,32,768]{2,1,0:T(8,128)(2,1)S(1)} collective-permute-done((bf16[8,32,768]{2,1,0:T(8,128)(2,1)S(1)}, bf16[8,32,768]{2,1,0:T(8,128)(2,1)S(1)}, u32[]{:S(2)}, u32[]{:S(2)}) %collective-permute-start.7) | collective-permute-done | bytes 393248 | tf_op jit(solution)/shard_map/ppermute | solution.py:29
  72.5 3.9 %pad_maximum_fusion = bf16[768,1536]{1,0:T(8,128)(2,1)} fusion(bf16[768,384]{1,0:T(8,128)(2,1)} %collective-permute-done.6, bf16[768,384]{1,0:T(8,128)(2,1)} %collective-permute-done.5, bf16[768,384]{1,0:T(8,128)(2,1)S(1)} %collective-permute-done.4, bf16[384,384]{1,0:T(8,128)(2,1)S(1)} %get-tuple-element.79, bf16[384,384]{1,0:T(8,128)(2,1)S(1)} %get-tuple-element.78), kind=kLoop, calls=%fused_computation.1 | loop fusion | flops 11796480 | bytes 4718592 | tf_op jit(solution)/shard_map/concatenate | solution.py:134
  76.4 4.7 %fusion.15 = (bf16[768,1536]{1,0:T(8,128)(2,1)S(1)}, f32[768,1536]{1,0:T(8,128)S(1)}) fusion(bf16[1024,768]{1,0:T(8,128)(2,1)S(1)} %bitcast.58, bf16[1024,1536]{1,0:T(8,128)(2,1)} %all-gather.3.cloned.1.call-done), kind=kOutput, calls=%fused_computation.40 | convolution fusion | flops 2418278400 | bytes 11796480 | tf_op jit(solution)/shard_map/tk,tn->kn/dot_general | solution.py:141
  81.4 1.4 collective-permute-start.13
  82.8 0.6 collective-permute-start.14
  83.4 0.7 collective-permute-start.15
  84.1 2.6 %convolution_multiply_fusion.1 = f32[1024,768]{1,0:T(8,128)S(1)} fusion(bf16[1024,1536]{1,0:T(8,128)(2,1)S(1)} %copy-done.5, bf16[768,1536]{1,0:T(8,128)(2,1)S(1)} %copy-done.6), kind=kOutput, calls=%fused_computation.2 | convolution fusion | flops 2416705536 | bytes 8650752 | tf_op jit(solution)/shard_map/tn,kn->tk/dot_general | solution.py:147
  87.0 1.4 copy-done.3
  88.4 1.0 slice_bitcast_fusion.3
  89.4 0.7 collective-permute-start.10
  90.2 3.2 %collective-permute-start.11 = (bf16[8,32,768]{2,1,0:T(8,128)(2,1)}, bf16[8,32,768]{2,1,0:T(8,128)(2,1)}, u32[]{:S(2)}, u32[]{:S(2)}) collective-permute-start(bf16[8,32,768]{2,1,0:T(8,128)(2,1)} %get-tuple-element.77), channel_id=1, source_target_pairs={{0,2},{1,3},{2,0},{3,1},{4,6},{5,7},{6,4},{7,5},{8,10},{9,11},{10,... | collective-permute-start | bytes 1179656 | tf_op jit(solution)/shard_map/ppermute | solution.py:29
  93.4 2.4 %collective-permute-done.13 = bf16[768,384]{1,0:T(8,128)(2,1)S(1)} collective-permute-done((bf16[768,384]{1,0:T(8,128)(2,1)S(1)}, bf16[768,384]{1,0:T(8,128)(2,1)S(1)}, u32[]{:S(2)}, u32[]{:S(2)}) %collective-permute-start.13) | collective-permute-done | bytes 589856 | tf_op jit(solution)/shard_map/ppermute | solution.py:29
  95.9 1.0 collective-permute-start.12
  96.8 1.6 collective-permute-done.14
  98.4 13.9 %collective-permute-done.15 = bf16[768,384]{1,0:T(8,128)(2,1)S(1)} collective-permute-done((bf16[768,384]{1,0:T(8,128)(2,1)S(1)}, bf16[768,384]{1,0:T(8,128)(2,1)S(1)}, u32[]{:S(2)}, u32[]{:S(2)}) %collective-permute-start.15) | collective-permute-done | bytes 589856 | tf_op jit(solution)/shard_map/ppermute | solution.py:29
  112.6 1.0 copy-done.4
  114.0 1.1 dynamic-slice_bitcast_fusion.own
  115.2 17.5 %collective-permute-done.16.other = bf16[384,384]{1,0:T(8,128)(2,1)S(1)} collective-permute-done((bf16[384,384]{1,0:T(8,128)(2,1)S(1)}, bf16[384,384]{1,0:T(8,128)(2,1)S(1)}, u32[]{:S(2)}, u32[]{:S(2)}) %collective-permute-start.16) | collective-permute-done | bytes 294944 | tf_op jit(solution)/shard_map/ppermute | solution.py:29
  132.6 2.6 %shard_map.134 = (f32[384,384]{1,0:T(8,128)S(1)}, bf16[384,384]{1,0:T(8,128)(2,1)}, f32[384,3]{1,0:T(8,128)S(1)}, bf16[384,384]{1,0:T(8,128)(2,1)}, f32[384,3]{1,0:T(8,128)S(1)}, /*index=5*/f32[8,128]{1,0:T(8,128)S(1)}) custom-call(f32[384,384]{1,0:T(8,128)S(1)} %dynamic-slice_bitcast_fusion.own, bf16[384,384]{1,0:T(8,128)(2,1)S(1)} %collective-permute-done.16.other, ...), custom_call_target="tpu_custom_call" | custom-call | flops 147456 | bytes 147456 | tf_op jit(solution)/shard_map/pallas_call | solution.py:97
  135.2 0.6 broadcast_in_dim.4
  135.9 6.9 %all-to-all-start.1 = ((f32[16,8,128]{2,1,0:T(8,128)}), f32[16,8,128]{2,1,0:T(8,128)S(1)}, u32[]{:S(2)}, u32[]{:S(2)}) async-start(f32[16,8,128]{2,1,0:T(8,128)} %broadcast_in_dim.4), calls=%async_computation.1 | async-start | bytes 131072 | tf_op jit(solution)/shard_map/all_to_all | solution.py:48
  142.8 2.3 %fusion.2 = bf16[8,32,768]{2,1,0:T(8,128)(2,1)} fusion(f32[8,4,32,768]{3,2,1,0:T(8,128)} %bitcast.60, bf16[8,32,768]{2,1,0:T(8,128)(2,1)} %collective-permute-done.12, bf16[8,32,768]{2,1,0:T(8,128)(2,1)} %collective-permute-done.11, bf16[8,32,768]{2,1,0:T(8,128)(2,1)S(1)} %collective-permute-done.10), kind=kLoop, calls=%fused_computation.16 | loop fusion | flops 1376256 | bytes 2359296 | tf_op jit(solution)/shard_map/add | solution.py:159
  145.1 3.5 %all-to-all-done.1 = f32[16,8,128]{2,1,0:T(8,128)S(1)} async-done(((f32[16,8,128]{2,1,0:T(8,128)}), f32[16,8,128]{2,1,0:T(8,128)S(1)}, u32[]{:S(2)}, u32[]{:S(2)}) %all-to-all-start.1) | async-done | bytes 65568 | tf_op jit(solution)/shard_map/all_to_all | solution.py:48
  148.6 14.2 %all_to_all.20 = f32[16,8,128]{2,1,0:T(8,128)S(1)} all-to-all(f32[16,8,128]{2,1,0:T(8,128)S(1)} %broadcast_in_dim.5), channel_id=1, replica_groups=mesh['dp'=16,'tensor'=16] {'tensor'}, dimensions={0} | all-to-all | bytes 131072 | tf_op jit(solution)/shard_map/all_to_all | solution.py:48
  164.7 1.0 fusion.12
  165.7 5.1 %all-to-all-start.3 = ((bf16[8,32,768]{2,1,0:T(8,128)(2,1)}), bf16[8,32,768]{2,1,0:T(8,128)(2,1)S(1)}, u32[]{:S(2)}, u32[]{:S(2)}) async-start(bf16[8,32,768]{2,1,0:T(8,128)(2,1)} %fusion.2), calls=%async_computation.3 | async-start | bytes 786432 | tf_op jit(solution)/shard_map/all_to_all | solution.py:169
  170.8 0.7 copy.41
  171.5 0.7 copy.42
  172.2 11.0 %all-to-all-done.3 = bf16[8,32,768]{2,1,0:T(8,128)(2,1)S(1)} async-done(((bf16[8,32,768]{2,1,0:T(8,128)(2,1)}), bf16[8,32,768]{2,1,0:T(8,128)(2,1)S(1)}, u32[]{:S(2)}, u32[]{:S(2)}) %all-to-all-start.3) | async-done | bytes 393248 | tf_op jit(solution)/shard_map/all_to_all | solution.py:169
  183.7 0.8 copy.47
  184.5 19.7 %all-gather.5.cloned.1.call-done = bf16[6144,384]{1,0:T(8,128)(2,1)} async-done(((bf16[384,384]{1,0:T(8,128)(2,1)}), bf16[6144,384]{1,0:T(8,128)(2,1)}) %all-gather.5.cloned.1.call-update) | async-done | bytes 4718608 | tf_op jit(solution)/shard_map/all_gather | solution.py:167
  204.2 5.0 %copy.51 = bf16[6144,384]{1,0:T(8,128)(2,1)} copy(bf16[6144,384]{1,0:T(8,128)(2,1)} %all-gather.5.cloned.1.call-done) | data formatting | bytes 9437184
  (55 shorter events, 4.4 us)
Async XLA Ops:
  7.2 9.1 %copy-start = (f32[384,384]{1,0:T(8,128)S(1)}, f32[384,384]{1,0:T(8,128)}, u32[]{:S(2)}) copy-start(f32[384,384]{1,0:T(8,128)} %master.1) | copy-start | bytes 1769476
  7.2 10.2 %copy-start.7 = (bf16[512,384]{1,0:T(8,128)(2,1)S(1)}, bf16[512,384]{1,0:T(8,128)(2,1)}, u32[]{:S(2)}) copy-start(bf16[512,384]{1,0:T(8,128)(2,1)} %param.8) | copy-start | bytes 1179652
  9.6 16.4 %all-to-all-start = ((bf16[8,32,768]{2,1,0:T(8,128)(2,1)}), bf16[8,32,768]{2,1,0:T(8,128)(2,1)S(1)}, u32[]{:S(2)}, u32[]{:S(2)}) async-start(bf16[8,32,768]{2,1,0:T(8,128)(2,1)} %reshape.56), calls=%async_computation | async-start | bytes 786432 | tf_op jit(solution)/shard_map/all_to_all | solution.py:128
  16.2 60.2 %all-gather.3.cloned.1.call-start = ((), (), s32[]{:S(2)}) async-start(), calls=%async_computation.4 | async-start | bytes 3538944 | tf_op jit(solution)/shard_map/all_gather | solution.py:136
  16.3 9.8 %collective-permute-start.3 = (bf16[384,384]{1,0:T(8,128)(2,1)S(1)}, bf16[384,384]{1,0:T(8,128)(2,1)S(1)}, u32[]{:S(2)}, u32[]{:S(2)}) collective-permute-start(bf16[384,384]{1,0:T(8,128)(2,1)S(1)} %convert_element_type.48), channel_id=1, source_target_pairs={{0,128},{1,129},{2,130},{3,131},{4,132},{5,133},{6,134},{7,135},{8... | collective-permute-start | bytes 884744 | tf_op jit(solution)/shard_map/ppermute | solution.py:29
  17.6 5.3 %collective-permute-start = (bf16[4,32,384]{2,1,0:T(8,128)(2,1)S(1)}, bf16[4,32,384]{2,1,0:T(8,128)(2,1)S(1)}, u32[]{:S(2)}, u32[]{:S(2)}) collective-permute-start(bf16[4,32,384]{2,1,0:T(8,128)(2,1)S(1)} %get-tuple-element.82), channel_id=1, source_target_pairs={{0,4},{1,5},{2,6},{3,7},{4,8},{5,9},{6,10},{7,11},{8,12},{9,13},{1... | collective-permute-start | bytes 294920 | tf_op jit(solution)/shard_map/ppermute | solution.py:29
  18.9 7.1 %collective-permute-start.1 = (bf16[4,32,384]{2,1,0:T(8,128)(2,1)S(1)}, bf16[4,32,384]{2,1,0:T(8,128)(2,1)S(1)}, u32[]{:S(2)}, u32[]{:S(2)}) collective-permute-start(bf16[4,32,384]{2,1,0:T(8,128)(2,1)S(1)} %get-tuple-element.83), channel_id=1, source_target_pairs={{0,8},{1,9},{2,10},{3,11},{4,12},{5,13},{6,14},{7,15},{8,0},{9,1},... | collective-permute-start | bytes 294920 | tf_op jit(solution)/shard_map/ppermute | solution.py:29
  21.4 4.7 %collective-permute-start.2 = (bf16[4,32,384]{2,1,0:T(8,128)(2,1)S(1)}, bf16[4,32,384]{2,1,0:T(8,128)(2,1)S(1)}, u32[]{:S(2)}, u32[]{:S(2)}) collective-permute-start(bf16[4,32,384]{2,1,0:T(8,128)(2,1)S(1)} %get-tuple-element.80), channel_id=1, source_target_pairs={{0,12},{1,13},{2,14},{3,15},{4,0},{5,1},{6,2},{7,3},{8,4},{9,5},{1... | collective-permute-start | bytes 294920 | tf_op jit(solution)/shard_map/ppermute | solution.py:29
  26.9 15.4 %collective-permute-start.8 = (bf16[8,32,768]{2,1,0:T(8,128)(2,1)S(1)}, bf16[8,32,768]{2,1,0:T(8,128)(2,1)S(1)}, u32[]{:S(2)}, u32[]{:S(2)}) collective-permute-start(bf16[8,32,768]{2,1,0:T(8,128)(2,1)S(1)} %all-to-all-done), channel_id=1, source_target_pairs={{0,2},{1,3},{2,0},{3,1},{4,6},{5,7},{6,4},{7,5},{8,10},{9,11},{10,... | collective-permute-start | bytes 1179656 | tf_op jit(solution)/shard_map/ppermute | solution.py:29
  33.9 38.5 %collective-permute-start.4 = (bf16[768,384]{1,0:T(8,128)(2,1)}, bf16[768,384]{1,0:T(8,128)(2,1)S(1)}, u32[]{:S(2)}, u32[]{:S(2)}) collective-permute-start(bf16[768,384]{1,0:T(8,128)(2,1)} %pad_maximum_fusion.2), channel_id=1, source_target_pairs={{0,4},{1,5},{2,6},{3,7},{4,8},{5,9},{6,10},{7,11},{8,12},{9,13},{1... | collective-permute-start | bytes 1769480 | tf_op jit(solution)/shard_map/ppermute | solution.py:29
  34.5 38.0 %collective-permute-start.5 = (bf16[768,384]{1,0:T(8,128)(2,1)}, bf16[768,384]{1,0:T(8,128)(2,1)}, u32[]{:S(2)}, u32[]{:S(2)}) collective-permute-start(bf16[768,384]{1,0:T(8,128)(2,1)} %pad_maximum_fusion.2), channel_id=1, source_target_pairs={{0,8},{1,9},{2,10},{3,11},{4,12},{5,13},{6,14},{7,15},{8,0},{9,1},... | collective-permute-start | bytes 1769480 | tf_op jit(solution)/shard_map/ppermute | solution.py:29
  36.8 35.7 %collective-permute-start.6 = (bf16[768,384]{1,0:T(8,128)(2,1)}, bf16[768,384]{1,0:T(8,128)(2,1)}, u32[]{:S(2)}, u32[]{:S(2)}) collective-permute-start(bf16[768,384]{1,0:T(8,128)(2,1)} %pad_maximum_fusion.2), channel_id=1, source_target_pairs={{0,12},{1,13},{2,14},{3,15},{4,0},{5,1},{6,2},{7,3},{8,4},{9,5},{1... | collective-permute-start | bytes 1769480 | tf_op jit(solution)/shard_map/ppermute | solution.py:29
  38.1 30.2 %collective-permute-start.9 = (bf16[8,32,768]{2,1,0:T(8,128)(2,1)S(1)}, bf16[8,32,768]{2,1,0:T(8,128)(2,1)S(1)}, u32[]{:S(2)}, u32[]{:S(2)}) collective-permute-start(bf16[8,32,768]{2,1,0:T(8,128)(2,1)S(1)} %all-to-all-done), channel_id=1, source_target_pairs={{0,3},{1,0},{2,1},{3,2},{4,7},{5,4},{6,5},{7,6},{8,11},{9,8},{10,9... | collective-permute-start | bytes 1179656 | tf_op jit(solution)/shard_map/ppermute | solution.py:29
  42.3 29.8 %collective-permute-start.7 = (bf16[8,32,768]{2,1,0:T(8,128)(2,1)S(1)}, bf16[8,32,768]{2,1,0:T(8,128)(2,1)S(1)}, u32[]{:S(2)}, u32[]{:S(2)}) collective-permute-start(bf16[8,32,768]{2,1,0:T(8,128)(2,1)S(1)} %all-to-all-done), channel_id=1, source_target_pairs={{0,1},{1,2},{2,3},{3,0},{4,5},{5,6},{6,7},{7,4},{8,9},{9,10},{10,1... | collective-permute-start | bytes 1179656 | tf_op jit(solution)/shard_map/ppermute | solution.py:29
  76.4 7.7 %copy-start.6 = (bf16[768,1536]{1,0:T(8,128)(2,1)S(1)}, bf16[768,1536]{1,0:T(8,128)(2,1)}, u32[]{:S(2)}) copy-start(bf16[768,1536]{1,0:T(8,128)(2,1)} %pad_maximum_fusion) | copy-start | bytes 7077892
  81.2 2.9 %copy-start.5 = (bf16[1024,1536]{1,0:T(8,128)(2,1)S(1)}, bf16[1024,1536]{1,0:T(8,128)(2,1)}, u32[]{:S(2)}) copy-start(bf16[1024,1536]{1,0:T(8,128)(2,1)} %all-gather.3.cloned.1.call-done) | copy-start | bytes 9437188
  81.4 14.5 %collective-permute-start.13 = (bf16[768,384]{1,0:T(8,128)(2,1)S(1)}, bf16[768,384]{1,0:T(8,128)(2,1)S(1)}, u32[]{:S(2)}, u32[]{:S(2)}) collective-permute-start(bf16[768,384]{1,0:T(8,128)(2,1)S(1)} %get-tuple-element.74), channel_id=1, source_target_pairs={{0,12},{1,13},{2,14},{3,15},{4,0},{5,1},{6,2},{7,3},{8,4},{9,5},{1... | collective-permute-start | bytes 1769480 | tf_op jit(solution)/shard_map/ppermute | solution.py:29
  82.8 15.6 %collective-permute-start.14 = (bf16[768,384]{1,0:T(8,128)(2,1)S(1)}, bf16[768,384]{1,0:T(8,128)(2,1)S(1)}, u32[]{:S(2)}, u32[]{:S(2)}) collective-permute-start(bf16[768,384]{1,0:T(8,128)(2,1)S(1)} %get-tuple-element.73), channel_id=1, source_target_pairs={{0,8},{1,9},{2,10},{3,11},{4,12},{5,13},{6,14},{7,15},{8,0},{9,1},... | collective-permute-start | bytes 1769480 | tf_op jit(solution)/shard_map/ppermute | solution.py:29
  83.4 28.9 %collective-permute-start.15 = (bf16[768,384]{1,0:T(8,128)(2,1)S(1)}, bf16[768,384]{1,0:T(8,128)(2,1)S(1)}, u32[]{:S(2)}, u32[]{:S(2)}) collective-permute-start(bf16[768,384]{1,0:T(8,128)(2,1)S(1)} %get-tuple-element.72), channel_id=1, source_target_pairs={{0,4},{1,5},{2,6},{3,7},{4,8},{5,9},{6,10},{7,11},{8,12},{9,13},{1... | collective-permute-start | bytes 1769480 | tf_op jit(solution)/shard_map/ppermute | solution.py:29
  86.7 1.7 copy-start.3
  89.4 53.4 %collective-permute-start.10 = (bf16[8,32,768]{2,1,0:T(8,128)(2,1)}, bf16[8,32,768]{2,1,0:T(8,128)(2,1)S(1)}, u32[]{:S(2)}, u32[]{:S(2)}) collective-permute-start(bf16[8,32,768]{2,1,0:T(8,128)(2,1)} %get-tuple-element.75), channel_id=1, source_target_pairs={{0,3},{1,0},{2,1},{3,2},{4,7},{5,4},{6,5},{7,6},{8,11},{9,8},{10,9... | collective-permute-start | bytes 1179656 | tf_op jit(solution)/shard_map/ppermute | solution.py:29
  90.2 52.6 %collective-permute-start.11 = (bf16[8,32,768]{2,1,0:T(8,128)(2,1)}, bf16[8,32,768]{2,1,0:T(8,128)(2,1)}, u32[]{:S(2)}, u32[]{:S(2)}) collective-permute-start(bf16[8,32,768]{2,1,0:T(8,128)(2,1)} %get-tuple-element.77), channel_id=1, source_target_pairs={{0,2},{1,3},{2,0},{3,1},{4,6},{5,7},{6,4},{7,5},{8,10},{9,11},{10,... | collective-permute-start | bytes 1179656 | tf_op jit(solution)/shard_map/ppermute | solution.py:29
  95.9 47.0 %collective-permute-start.12 = (bf16[8,32,768]{2,1,0:T(8,128)(2,1)}, bf16[8,32,768]{2,1,0:T(8,128)(2,1)}, u32[]{:S(2)}, u32[]{:S(2)}) collective-permute-start(bf16[8,32,768]{2,1,0:T(8,128)(2,1)} %get-tuple-element.76), channel_id=1, source_target_pairs={{0,1},{1,2},{2,3},{3,0},{4,5},{5,6},{6,7},{7,4},{8,9},{9,10},{10,1... | collective-permute-start | bytes 1179656 | tf_op jit(solution)/shard_map/ppermute | solution.py:29
  112.3 1.4 copy-start.8
  112.3 1.6 copy-start.9
  112.3 20.3 %copy-start.1 = (bf16[384,384]{1,0:T(8,128)(2,1)S(1)}, bf16[384,384]{1,0:T(8,128)(2,1)}, u32[]{:S(2)}) copy-start(bf16[384,384]{1,0:T(8,128)(2,1)} %mcode.1) | copy-start | bytes 884740
  112.3 20.3 %copy-start.2 = (bf16[384,384]{1,0:T(8,128)(2,1)S(1)}, bf16[384,384]{1,0:T(8,128)(2,1)}, u32[]{:S(2)}) copy-start(bf16[384,384]{1,0:T(8,128)(2,1)} %scode.1) | copy-start | bytes 884740
  112.5 1.0 copy-start.4
  113.6 19.0 %collective-permute-start.16 = (bf16[384,384]{1,0:T(8,128)(2,1)S(1)}, bf16[384,384]{1,0:T(8,128)(2,1)S(1)}, u32[]{:S(2)}, u32[]{:S(2)}) collective-permute-start(bf16[384,384]{1,0:T(8,128)(2,1)S(1)} %fusion.3), channel_id=1, source_target_pairs={{0,128},{1,129},{2,130},{3,131},{4,132},{5,133},{6,134},{7,135},{8... | collective-permute-start | bytes 884744 | tf_op jit(solution)/shard_map/ppermute | solution.py:29
  135.9 12.7 %all-to-all-start.1 = ((f32[16,8,128]{2,1,0:T(8,128)}), f32[16,8,128]{2,1,0:T(8,128)S(1)}, u32[]{:S(2)}, u32[]{:S(2)}) async-start(f32[16,8,128]{2,1,0:T(8,128)} %broadcast_in_dim.4), calls=%async_computation.1 | async-start | bytes 131072 | tf_op jit(solution)/shard_map/all_to_all | solution.py:48
  142.8 61.4 %all-gather.5.cloned.1.call-start = ((), (), s32[]{:S(2)}) async-start(), calls=%async_computation.5 | async-start | bytes 5013504 | tf_op jit(solution)/shard_map/all_gather | solution.py:167
  165.7 17.4 %all-to-all-start.3 = ((bf16[8,32,768]{2,1,0:T(8,128)(2,1)}), bf16[8,32,768]{2,1,0:T(8,128)(2,1)S(1)}, u32[]{:S(2)}, u32[]{:S(2)}) async-start(bf16[8,32,768]{2,1,0:T(8,128)(2,1)} %fusion.2), calls=%async_computation.3 | async-start | bytes 786432 | tf_op jit(solution)/shard_map/all_to_all | solution.py:169
Sparse Core Ops, SparseCore 0:
  27.0 32.9 all-gather.2
  165.9 38.2 all-gather.4

commit v2 on v1

--- a/solution.py
+++ b/solution.py
@@ -11,6 +11,7 @@
 SIZES = (2, 4, 2, 4, 4)
 BOTH = ("dp", "tensor")
 NEAR = [list(range(8)), list(range(8, 16))]
+LINE = [[4 * x + high for high in range(4)] for x in range(4)]
 BF16, F32 = jnp.bfloat16, jnp.float32
 
 
@@ -29,12 +30,6 @@
     return lax.ppermute(array, BOTH, pairs)
 
 
-def roll(array, start):
-    return lax.dynamic_slice_in_dim(
-        jnp.concatenate([array, array], axis=0), start, array.shape[0], axis=0
-    )
-
-
 def take(array, index, axis):
     return lax.dynamic_index_in_dim(array, index, axis, keepdims=False)
 
@@ -49,22 +44,23 @@
 
 
 def moments_kernel(
-    own, other, master, mcode, mscale, scode, sscale,
+    upper, far, lower, one, two, three, master, mcode, mscale, scode, sscale,
     update, new_mcode, new_mscale, new_scode, new_sscale, sums,
 ):
     rows, cols = master.shape
     blocks = mscale.shape[1]
     wide = cols // blocks
     step = 64
+    steps = rows // 2 // step
     sums[...] = jnp.zeros_like(sums)
 
-    def body(i, carry):
+    def some(i, gradient):
         at = pl.ds(pl.multiple_of(i * step, step), step)
         mscales, sscales = mscale[at, :], sscale[at, :]
         new_m, new_s = [], []
         for b in range(blocks):
             cut = slice(b * wide, (b + 1) * wide)
-            grad = own[at, cut] + other[at, cut].astype(F32)
+            grad = gradient(cut)
             weight = master[at, cut]
             moment = mcode[at, cut].astype(F32) * mscales[:, b : b + 1]
             second = scode[at, cut].astype(F32) * sscales[:, b : b + 1]
@@ -85,13 +81,24 @@
             sums[1:2, :] += jnp.sum(change * change, axis=0, keepdims=True)
         new_mscale[at, :] = jnp.concatenate(new_m, axis=1)
         new_sscale[at, :] = jnp.concatenate(new_s, axis=1)
+
+    def body(i, carry):
+        at = pl.ds(pl.multiple_of(i * step, step), step)
+        some(i, lambda cut: upper[at, cut] + far[at, cut].astype(F32))
+        some(
+            i + steps,
+            lambda cut: lower[at, cut]
+            + one[at, cut].astype(F32)
+            + two[at, cut].astype(F32)
+            + three[at, cut].astype(F32),
+        )
         return carry
 
-    lax.fori_loop(0, rows // step, body, 0)
+    lax.fori_loop(0, steps, body, 0)
     sums[...] = jnp.broadcast_to(jnp.sum(sums[...], axis=1, keepdims=True), sums.shape)
 
 
-def moments(own, other, master, mcode, mscale, scode, sscale):
+def moments(upper, far, lower, others, master, mcode, mscale, scode, sscale):
     like = lambda a, dtype: jax.ShapeDtypeStruct(a.shape, dtype)
     block = master.shape[1] // mscale.shape[1]
     return pl.pallas_call(
@@ -104,13 +111,13 @@
             like(sscale, F32),
             jax.ShapeDtypeStruct((8, block), F32),
         ),
-        in_specs=[pl.BlockSpec(memory_space=pltpu.VMEM)] * 7,
+        in_specs=[pl.BlockSpec(memory_space=pltpu.VMEM)] * 11,
         out_specs=[pl.BlockSpec(memory_space=pltpu.VMEM)] * 6,
         compiler_params=pltpu.CompilerParams(vmem_limit_bytes=32 * 1024 * 1024),
         cost_estimate=pl.CostEstimate(
             flops=master.size, bytes_accessed=master.size, transcendentals=0
         ),
-    )(own, other, master, mcode, mscale, scode, sscale)
+    )(upper, far, lower, *others, master, mcode, mscale, scode, sscale)
 
 
 def local(layer_input, out_grad, master, moment_code, moment_scale, second_code, second_scale):
@@ -121,42 +128,58 @@
     rows, cols = master.shape
     steps = (1, 2, 3)
 
-    grads = out_grad.reshape(4, 4, few, cols).transpose(1, 0, 2, 3)
-    grads = roll(grads[::-1], 3 - high)
-    parts = [take(grads, x, 1)] + [shift(take(grads, (x + s) % 4, 1), x=s) for s in steps]
+    grads = out_grad.reshape(4, 4, few, cols)
+    parts = [take(grads, x, 0)] + [shift(take(grads, (x + s) % 4, 0), x=s) for s in steps]
     mine = layer_input.reshape(few, 2, 8, rows).transpose(2, 0, 1, 3).reshape(8, few, 2 * rows)
     mine = lax.all_to_all(mine, "dp", 0, 0, tiled=True, axis_index_groups=NEAR)
-    moved = [shift(mine, high=s) for s in steps]
     weights = master.astype(BF16)
     far = shift(weights, z=1)
     parts, far = lax.optimization_barrier((parts, mine, far))[::2]
     weights = jnp.concatenate([jnp.where(z == 0, weights, far), jnp.where(z == 0, far, weights)])
-    weights = jnp.concatenate([weights] + [shift(weights, x=s) for s in steps], axis=1)
+    moved = [shift(mine, high=1), shift(mine, high=-1)]
+    wings = [shift(weights, x=1), shift(weights, x=-1)]
+    moved, wings = lax.optimization_barrier((moved, wings))
+    across = [shift(moved[0][:4], high=1), shift(moved[1][4:], high=-1)]
+    moved = [moved[0], jnp.concatenate(across), moved[1]]
+    across = [shift(wings[0][:rows], x=1), shift(wings[1][rows:], x=-1)]
     near = jnp.concatenate(parts, axis=2).reshape(4 * few, 4 * cols)
     wide = lax.all_gather(near, "dp", axis=0, tiled=True, axis_index_groups=NEAR)
 
-    acts = jnp.stack([mine] + moved, axis=1).reshape(32 * few, 2 * rows)
-
-    acts = after(acts, weights)
-    part = jnp.einsum("tk,tn->kn", acts, wide, preferred_element_type=F32) * inv_root
-    part = [part[:, s * cols : (s + 1) * cols] for s in range(4)]
-    sends = [part[s].astype(BF16) for s in steps]
+    groups = wide.reshape(8, 4, few, 4 * cols)
+    part = sum(
+        jnp.einsum(
+            "tk,tn->kn",
+            piece.reshape(8 * few, 2 * rows),
+            take(groups, (high + 4 - q) % 4, 1).reshape(8 * few, 4 * cols),
+            preferred_element_type=F32,
+        )
+        for q, piece in enumerate([mine] + moved)
+    )
+    part = (part * inv_root).reshape(2, rows, 4 * cols)
+    half = rows // 2
+    block = lambda a, s: a[..., s * cols : (s + 1) * cols]
+    upper, lower = part[:, :half], part[:, half:]
+    sends = [block(upper, s).astype(BF16) for s in steps]
+    sends.append(take(lower, 1 - z, 0).astype(BF16))
     others = [shift(send, x=-s) for s, send in zip(steps, sends)]
-
-    weights = after(weights, *sends)
+    others, crossed = lax.optimization_barrier((others, shift(sends[3], z=1)))
+    lower = take(lower, z, 0) + crossed.astype(F32)
+    upper = block(upper, 0) + sum(other.astype(F32) for other in others)
+    far = shift(take(upper, 1 - z, 0).astype(BF16), z=1)
+    others = [shift(block(lower, s).astype(BF16), x=-s) for s in steps]
+
+    across = lax.optimization_barrier((across, sends))[0]
+    weights = jnp.concatenate([weights, wings[0], jnp.concatenate(across), wings[1]], axis=1)
     outs = jnp.einsum("tn,kn->tk", wide, weights, preferred_element_type=F32) * inv_root
-    outs = outs.reshape(8, 4, few, 2 * rows)
-    pieces = [outs[:, s].astype(BF16) for s in steps]
-    others = lax.optimization_barrier((tuple(others), tuple(pieces)))[0]
-    grad = part[0] + sum(other.astype(F32) for other in others)
-    grad = grad.reshape(2, rows, cols)
-    far = shift(take(grad, 1 - z, 0).astype(BF16), z=1)
+    outs = after(outs.astype(BF16), lower).reshape(8, 4, few, 2 * rows).transpose(1, 0, 2, 3)
+    summed = lax.psum_scatter(
+        outs.reshape(32 * few, 2 * rows), "tensor", scatter_dimension=0, tiled=True, axis_index_groups=LINE
+    ).reshape(8, few, 2 * rows)
+
     update, new_moment_code, new_moment_scale, new_second_code, new_second_scale, sums = moments(
-        take(grad, z, 0), far, master, moment_code, moment_scale, second_code, second_scale
-    )
-    summed = outs[:, 0]
-    for s, piece in zip(steps, pieces):
-        summed = summed + shift(piece, high=-s).astype(F32)
+        take(upper, z, 0), far, block(lower, 0), others,
+        master, moment_code, moment_scale, second_code, second_scale,
+    )
     sums = total_of(sums, "dp")
     summed, sums = lax.optimization_barrier((summed, sums))
     sums = total_of(sums, "tensor")
@@ -167,7 +190,7 @@
     new_weight = lax.all_gather(new_master.astype(BF16), "dp", axis=0, tiled=True)
 
     back = lax.all_to_all(
-        after(summed.astype(BF16), sums), "dp", 0, 0, tiled=True, axis_index_groups=NEAR
+        after(summed, sums), "dp", 0, 0, tiled=True, axis_index_groups=NEAR
     )
     input_grad = back.reshape(8, few, 2, rows).transpose(1, 2, 0, 3).reshape(few, feat)
 

time: 218 us -> 208 us (0.954)
  blocking collectives: 14.2 us -> 32.4 us
  waiting for transfers between devices: 96.1 us -> 80.9 us
  starting transfers between devices: 53.7 us -> 41.6 us
  other arithmetic: 9.84 us -> 5.68 us
  local copies, waits for them, and re-layouts: 16.5 us -> 20.3 us
    ppermute x17 -> x20, waiting for transfers between devices: 61.9 us -> 40.4 us  [shift(): return lax.ppermute(array, BOTH, pairs)]
    all_to_all x1 -> x2, blocking collectives: 14.2 us -> 32.4 us  [total_of(): return jnp.sum(lax.all_to_all(spread, axis, 0, 0, tiled=True), axis=0)]
    reduce_scatter x0 -> x1, waiting for transfers between devices: none -> 8.22 us  [local(): lax.psum_scatter(outs.reshape(32 * few, 2 * rows), 'tensor', scatter_dime...]
    all_to_all x2 -> x1, waiting for transfers between devices: 14.4 us -> 7.52 us  [local(): lax.all_to_all(after(summed, sums), 'dp', 0, 0, tiled=True, axis_index_gr...]
    ppermute x17 -> x20, starting transfers between devices: 35.1 us -> 28.6 us  [shift(): return lax.ppermute(array, BOTH, pairs)]
    all_to_all x2 -> x1, starting transfers between devices: 12 us -> 6.32 us  [local(): lax.all_to_all(after(summed, sums), 'dp', 0, 0, tiled=True, axis_index_gr...]
    all_gather x1, waiting for transfers between devices: 19.7 us -> 24.7 us  [local(): lax.all_gather(new_master.astype(BF16), 'dp', axis=0, tiled=True)]
    slice x1 -> x8, local copies, waits for them, and re-layouts: 0.18 us -> 3.32 us  [the longest x2 2.02 us: local(): across = [shift(wings[0][:rows], x=1), shift(wings[1][rows:], x=-1)]]
  transfers between devices with their start and end apart: 22 -> 25, of which waited for: 12 -> 13; matrix products, arithmetic and copies ran while one was open for 8% -> 9% of each run, Pallas kernels for 1% -> 1%
where the time goes in v2:
time: 208 us
  waiting for transfers between devices  80.9 us (39%)
  starting transfers between devices  41.6 us (20%)
  blocking collectives  32.4 us (16%)
  local copies, waits for them, and re-layouts  20.3 us (10%)
  between operations  16.6 us (8%)
  matrix products  7.4 us (4%)
  other arithmetic  5.68 us (3%)
  Pallas kernels  2.78 us (1%)
    ppermute x20, waiting for transfers between devices, shift(): return lax.ppermute(array, BOTH, pairs)  40.4 us
    all_to_all x2, blocking collectives, total_of(): return jnp.sum(lax.all_to_all(spread, axis, 0, 0, tiled=True), axis=0)  32.4 us
    ppermute x20, starting transfers between devices, shift(): return lax.ppermute(array, BOTH, pairs)  28.6 us
    all_gather x1, waiting for transfers between devices, local(): lax.all_gather(new_master.astype(BF16), 'dp', axis=0, tiled=True)  24.7 us
    unnamed x31, local copies, waits for them, and re-layouts  11.2 us
    reduce_scatter x1, waiting for transfers between devices, local(): lax.psum_scatter(outs.reshape(32 * few, 2 * rows), 'tensor', scatter_dime...  8.22 us
    all_to_all x1, waiting for transfers between devices, local(): lax.all_to_all(after(summed, sums), 'dp', 0, 0, tiled=True, axis_index_gr...  7.52 us
    all_to_all x1, starting transfers between devices, local(): mine = lax.all_to_all(mine, 'dp', 0, 0, tiled=True, axis_index_groups=NEAR)  6.6 us
  transfers between devices with their start and end apart: 25, of which 13 were waited for; matrix products, arithmetic and copies ran while one was open for 9% of the time, Pallas kernels for 1%

profile of v2, /device:TPU:1, one launch (start us, length us, event | category | flops | bytes accessed | tf_op | source)
XLA Modules:
  0.0 207.7 jit_solution(8096689478269646633)
XLA Ops:
  7.2 1.1 copy.39
  8.6 1.0 reshape.88
  9.6 6.6 %all-to-all-start = ((bf16[8,32,768]{2,1,0:T(8,128)(2,1)}), bf16[8,32,768]{2,1,0:T(8,128)(2,1)S(1)}, u32[]{:S(2)}, u32[]{:S(2)}) async-start(bf16[8,32,768]{2,1,0:T(8,128)(2,1)} %reshape.88), calls=%async_computation | async-start | bytes 786432 | tf_op jit(solution)/shard_map/all_to_all | solution.py:134
  16.3 1.1 collective-permute-start.3
  17.4 1.3 collective-permute-start
  18.7 2.5 %collective-permute-start.1 = (bf16[4,32,384]{2,1,0:T(8,128)(2,1)S(1)}, bf16[4,32,384]{2,1,0:T(8,128)(2,1)S(1)}, u32[]{:S(2)}, u32[]{:S(2)}) collective-permute-start(bf16[4,32,384]{2,1,0:T(8,128)(2,1)S(1)} %get-tuple-element.107), channel_id=1, source_target_pairs={{0,8},{1,9},{2,10},{3,11},{4,12},{5,13},{6,14},{7,15},{8,0},{9,1},... | collective-permute-start | bytes 294920 | tf_op jit(solution)/shard_map/ppermute | solution.py:30
  21.2 1.2 collective-permute-start.2
  22.8 3.1 %collective-permute-done.1 = bf16[4,32,384]{2,1,0:T(8,128)(2,1)S(1)} collective-permute-done((bf16[4,32,384]{2,1,0:T(8,128)(2,1)S(1)}, bf16[4,32,384]{2,1,0:T(8,128)(2,1)S(1)}, u32[]{:S(2)}, u32[]{:S(2)}) %collective-permute-start.1) | collective-permute-done | bytes 98336 | tf_op jit(solution)/shard_map/ppermute | solution.py:30
  27.5 2.1 %collective-permute-start.7 = (bf16[768,384]{1,0:T(8,128)(2,1)S(1)}, bf16[768,384]{1,0:T(8,128)(2,1)}, u32[]{:S(2)}, u32[]{:S(2)}) collective-permute-start(bf16[768,384]{1,0:T(8,128)(2,1)S(1)} %pad_maximum_fusion), channel_id=1, source_target_pairs={{0,12},{1,13},{2,14},{3,15},{4,0},{5,1},{6,2},{7,3},{8,4},{9,5},{1... | collective-permute-start | bytes 1769480 | tf_op jit(solution)/shard_map/ppermute | solution.py:30
  29.6 3.0 %collective-permute-start.4 = (bf16[8,32,768]{2,1,0:T(8,128)(2,1)S(1)}, bf16[8,32,768]{2,1,0:T(8,128)(2,1)S(1)}, u32[]{:S(2)}, u32[]{:S(2)}) collective-permute-start(bf16[8,32,768]{2,1,0:T(8,128)(2,1)S(1)} %all-to-all-done), channel_id=1, source_target_pairs={{0,1},{1,2},{2,3},{3,0},{4,5},{5,6},{6,7},{7,4},{8,9},{9,10},{10,1... | collective-permute-start | bytes 1179656 | tf_op jit(solution)/shard_map/ppermute | solution.py:30
  32.6 2.1 %collective-permute-start.5 = (bf16[8,32,768]{2,1,0:T(8,128)(2,1)S(1)}, bf16[8,32,768]{2,1,0:T(8,128)(2,1)S(1)}, u32[]{:S(2)}, u32[]{:S(2)}) collective-permute-start(bf16[8,32,768]{2,1,0:T(8,128)(2,1)S(1)} %all-to-all-done), channel_id=1, source_target_pairs={{0,3},{1,0},{2,1},{3,2},{4,7},{5,4},{6,5},{7,6},{8,11},{9,8},{10,9... | collective-permute-start | bytes 1179656 | tf_op jit(solution)/shard_map/ppermute | solution.py:30
  34.8 10.2 %collective-permute-done.4 = bf16[8,32,768]{2,1,0:T(8,128)(2,1)S(1)} collective-permute-done((bf16[8,32,768]{2,1,0:T(8,128)(2,1)S(1)}, bf16[8,32,768]{2,1,0:T(8,128)(2,1)S(1)}, u32[]{:S(2)}, u32[]{:S(2)}) %collective-permute-start.4) | collective-permute-done | bytes 393248 | tf_op jit(solution)/shard_map/ppermute | solution.py:30
  45.0 8.6 %collective-permute-done.5 = bf16[8,32,768]{2,1,0:T(8,128)(2,1)S(1)} collective-permute-done((bf16[8,32,768]{2,1,0:T(8,128)(2,1)S(1)}, bf16[8,32,768]{2,1,0:T(8,128)(2,1)S(1)}, u32[]{:S(2)}, u32[]{:S(2)}) %collective-permute-start.5) | collective-permute-done | bytes 393248 | tf_op jit(solution)/shard_map/ppermute | solution.py:30
  53.5 0.8 copy-done.8
  54.4 2.6 %collective-permute-start.10 = (bf16[4,32,768]{2,1,0:T(8,128)(2,1)S(1)}, bf16[4,32,768]{2,1,0:T(8,128)(2,1)S(1)}, u32[]{:S(2)}, u32[]{:S(2)}) collective-permute-start(bf16[4,32,768]{2,1,0:T(8,128)(2,1)S(1)} %slice.58), channel_id=1, source_target_pairs={{0,1},{1,2},{2,3},{3,0},{4,5},{5,6},{6,7},{7,4},{8,9},{9,10},{10,1... | collective-permute-start | bytes 589832 | tf_op jit(solution)/shard_map/ppermute | solution.py:30
  56.9 1.2 collective-permute-start.11
  58.1 1.0 slice.56
  59.2 1.0 slice.57
  60.2 2.9 %collective-permute-start.9 = (bf16[384,384]{1,0:T(8,128)(2,1)S(1)}, bf16[384,384]{1,0:T(8,128)(2,1)}, u32[]{:S(2)}, u32[]{:S(2)}) collective-permute-start(bf16[384,384]{1,0:T(8,128)(2,1)S(1)} %slice.57), channel_id=1, source_target_pairs={{0,12},{1,13},{2,14},{3,15},{4,0},{5,1},{6,2},{7,3},{8,4},{9,5},{1... | collective-permute-start | bytes 884744 | tf_op jit(solution)/shard_map/ppermute | solution.py:30
  63.2 1.6 collective-permute-done.10
  64.8 1.0 pad_maximum_fusion.2
  65.7 2.1 constant_dynamic-slice_fusion.3
  68.6 0.8 fusion.25
  70.3 1.1 fusion.2
  71.9 1.7 copy-done.3
  73.8 2.5 %collective-permute-start.12 = (bf16[2,192,384]{2,1,0:T(8,128)(2,1)S(1)}, bf16[2,192,384]{2,1,0:T(8,128)(2,1)S(1)}, u32[]{:S(2)}, u32[]{:S(2)}) collective-permute-start(bf16[2,192,384]{2,1,0:T(8,128)(2,1)S(1)} %get-tuple-element.100), channel_id=1, source_target_pairs={{0,12},{1,13},{2,14},{3,15},{4,0},{5,1},{6,2},{7,3},{8,4},{9,5},{1... | collective-permute-start | bytes 884744 | tf_op jit(solution)/shard_map/ppermute | solution.py:30
  77.0 3.9 %multiply_convert_fusion = bf16[1024,768]{1,0:T(8,128)(2,1)S(1)} fusion(bf16[1024,1536]{1,0:T(8,128)(2,1)S(1)} %copy-done.4, bf16[768,384]{1,0:T(8,128)(2,1)} %collective-permute-done.7, bf16[384,384]{1,0:T(8,128)(2,1)} %collective-permute-done.9, bf16[384,384]{1,0:T(8,128)(2,1)} %collective-permute-done.8, bf16[768,384]{1,0:T(8,128)(2,1)S(1)} %copy-done.9, ...), kind=kOutput, calls=%fused_computation.4 | convolution fusion | flops 2431647744 | bytes 7077888 | tf_op jit(solution)/shard_map/tn,kn->tk/dot_general | solution.py:173
  80.8 3.3 %collective-permute-done.12 = bf16[2,192,384]{2,1,0:T(8,128)(2,1)S(1)} collective-permute-done((bf16[2,192,384]{2,1,0:T(8,128)(2,1)S(1)}, bf16[2,192,384]{2,1,0:T(8,128)(2,1)S(1)}, u32[]{:S(2)}, u32[]{:S(2)}) %collective-permute-start.12) | collective-permute-done | bytes 294944 | tf_op jit(solution)/shard_map/ppermute | solution.py:30
  84.2 6.4 %collective-permute-done.14 = bf16[2,192,384]{2,1,0:T(8,128)(2,1)S(1)} collective-permute-done((bf16[2,192,384]{2,1,0:T(8,128)(2,1)S(1)}, bf16[2,192,384]{2,1,0:T(8,128)(2,1)S(1)}, u32[]{:S(2)}, u32[]{:S(2)}) %collective-permute-start.14) | collective-permute-done | bytes 294944 | tf_op jit(solution)/shard_map/ppermute | solution.py:30
  90.6 1.2 fusion.21
  91.8 1.3 copy.33
  93.2 1.3 slice_add_fusion
  94.5 3.3 %collective-permute-start.16 = (bf16[192,384]{1,0:T(8,128)(2,1)S(1)}, bf16[192,384]{1,0:T(8,128)(2,1)S(1)}, u32[]{:S(2)}, u32[]{:S(2)}) collective-permute-start(bf16[192,384]{1,0:T(8,128)(2,1)S(1)} %fusion.18), channel_id=1, source_target_pairs={{0,128},{1,129},{2,130},{3,131},{4,132},{5,133},{6,134},{7,135},{8... | collective-permute-start | bytes 442376 | tf_op jit(solution)/shard_map/ppermute | solution.py:30
  98.0 1.4 collective-permute-start.19
  99.7 1.0 slice.76.lower
  100.7 1.4 collective-permute-done.17.one
  102.2 1.4 collective-permute-done.18.two
  103.6 3.8 %collective-permute-done.19.three = bf16[192,384]{1,0:T(8,128)(2,1)S(1)} collective-permute-done((bf16[192,384]{1,0:T(8,128)(2,1)S(1)}, bf16[192,384]{1,0:T(8,128)(2,1)S(1)}, u32[]{:S(2)}, u32[]{:S(2)}) %collective-permute-start.19) | collective-permute-done | bytes 147488 | tf_op jit(solution)/shard_map/ppermute | solution.py:30
  107.4 2.8 %shard_map.134 = (f32[384,384]{1,0:T(8,128)S(1)}, bf16[384,384]{1,0:T(8,128)(2,1)}, f32[384,3]{1,0:T(8,128)S(1)}, bf16[384,384]{1,0:T(8,128)(2,1)}, f32[384,3]{1,0:T(8,128)S(1)}, /*index=5*/f32[8,128]{1,0:T(8,128)S(1)}) custom-call(f32[192,384]{1,0:T(8,128)S(1)} %dynamic-slice_bitcast_fusion.upper, bf16[192,384]{1,0:T(8,128)(2,1)S(1)} %collective-permute-done.16.far, ...), custom_call_target="tpu_custom_call" | custom-call | flops 147456 | bytes 147456 | tf_op jit(solution)/shard_map/pallas_call | solution.py:104
  110.2 16.3 %all_to_all.20 = f32[16,8,128]{2,1,0:T(8,128)S(1)} all-to-all(f32[16,8,128]{2,1,0:T(8,128)S(1)} %broadcast_in_dim.4), channel_id=1, replica_groups=mesh['dp'=16,'tensor'=16] {'dp'}, dimensions={0} | all-to-all | bytes 131072 | tf_op jit(solution)/shard_map/all_to_all | solution.py:43
  126.5 8.2 %reduce-scatter.2.cloned.1.call-done = bf16[256,768]{1,0:T(8,128)(2,1)} async-done(((bf16[1024,768]{1,0:T(8,128)(2,1)}), bf16[256,768]{1,0:T(8,128)(2,1)}) %reduce-scatter.2.cloned.1.call-update) | async-done | bytes 393232 | tf_op jit(solution)/shard_map/reduce_scatter | solution.py:175
  134.8 16.1 %all_to_all.21 = f32[16,8,128]{2,1,0:T(8,128)S(1)} all-to-all(f32[16,8,128]{2,1,0:T(8,128)S(1)} %broadcast_in_dim.5), channel_id=1, replica_groups=mesh['dp'=16,'tensor'=16] {'tensor'}, dimensions={0} | all-to-all | bytes 131072 | tf_op jit(solution)/shard_map/all_to_all | solution.py:43
  152.8 1.0 fusion.20
  153.8 6.3 %all-to-all-start.3 = ((bf16[8,32,768]{2,1,0:T(8,128)(2,1)}), bf16[8,32,768]{2,1,0:T(8,128)(2,1)S(1)}, u32[]{:S(2)}, u32[]{:S(2)}) async-start(bf16[8,32,768]{2,1,0:T(8,128)(2,1)} %bitcast.83), calls=%async_computation.4 | async-start | bytes 786432 | tf_op jit(solution)/shard_map/all_to_all | solution.py:192
  161.5 7.5 %all-to-all-done.3 = bf16[8,32,768]{2,1,0:T(8,128)(2,1)S(1)} async-done(((bf16[8,32,768]{2,1,0:T(8,128)(2,1)}), bf16[8,32,768]{2,1,0:T(8,128)(2,1)S(1)}, u32[]{:S(2)}, u32[]{:S(2)}) %all-to-all-start.3) | async-done | bytes 393248 | tf_op jit(solution)/shard_map/all_to_all | solution.py:192
  169.5 0.8 copy.40
  170.3 24.7 %all-gather.5.cloned.1.call-done = bf16[6144,384]{1,0:T(8,128)(2,1)} async-done(((bf16[384,384]{1,0:T(8,128)(2,1)}), bf16[6144,384]{1,0:T(8,128)(2,1)}) %all-gather.5.cloned.1.call-update) | async-done | bytes 4718608 | tf_op jit(solution)/shard_map/all_gather | solution.py:190
  195.1 5.0 %copy.44 = bf16[6144,384]{1,0:T(8,128)(2,1)} copy(bf16[6144,384]{1,0:T(8,128)(2,1)} %all-gather.5.cloned.1.call-done) | data formatting | bytes 9437184
  (76 shorter events, 8.6 us)
Async XLA Ops:
  7.2 9.1 %copy-start = (f32[384,384]{1,0:T(8,128)S(1)}, f32[384,384]{1,0:T(8,128)}, u32[]{:S(2)}) copy-start(f32[384,384]{1,0:T(8,128)} %master.1) | copy-start | bytes 1769476
  7.2 10.2 %copy-start.5 = (bf16[512,384]{1,0:T(8,128)(2,1)S(1)}, bf16[512,384]{1,0:T(8,128)(2,1)}, u32[]{:S(2)}) copy-start(bf16[512,384]{1,0:T(8,128)(2,1)} %param.8) | copy-start | bytes 1179652
  9.6 16.2 %all-to-all-start = ((bf16[8,32,768]{2,1,0:T(8,128)(2,1)}), bf16[8,32,768]{2,1,0:T(8,128)(2,1)S(1)}, u32[]{:S(2)}, u32[]{:S(2)}) async-start(bf16[8,32,768]{2,1,0:T(8,128)(2,1)} %reshape.88), calls=%async_computation | async-start | bytes 786432 | tf_op jit(solution)/shard_map/all_to_all | solution.py:134
  16.2 49.5 %all-gather.3.cloned.1.call-start = ((), (), s32[]{:S(2)}) async-start(), calls=%async_computation.5 | async-start | bytes 3538944 | tf_op jit(solution)/shard_map/all_gather | solution.py:146
  16.3 9.6 %collective-permute-start.3 = (bf16[384,384]{1,0:T(8,128)(2,1)S(1)}, bf16[384,384]{1,0:T(8,128)(2,1)S(1)}, u32[]{:S(2)}, u32[]{:S(2)}) collective-permute-start(bf16[384,384]{1,0:T(8,128)(2,1)S(1)} %convert_element_type.39), channel_id=1, source_target_pairs={{0,128},{1,129},{2,130},{3,131},{4,132},{5,133},{6,134},{7,135},{8... | collective-permute-start | bytes 884744 | tf_op jit(solution)/shard_map/ppermute | solution.py:30
  17.4 5.3 %collective-permute-start = (bf16[4,32,384]{2,1,0:T(8,128)(2,1)S(1)}, bf16[4,32,384]{2,1,0:T(8,128)(2,1)S(1)}, u32[]{:S(2)}, u32[]{:S(2)}) collective-permute-start(bf16[4,32,384]{2,1,0:T(8,128)(2,1)S(1)} %get-tuple-element.108), channel_id=1, source_target_pairs={{0,4},{1,5},{2,6},{3,7},{4,8},{5,9},{6,10},{7,11},{8,12},{9,13},{1... | collective-permute-start | bytes 294920 | tf_op jit(solution)/shard_map/ppermute | solution.py:30
  18.7 7.1 %collective-permute-start.1 = (bf16[4,32,384]{2,1,0:T(8,128)(2,1)S(1)}, bf16[4,32,384]{2,1,0:T(8,128)(2,1)S(1)}, u32[]{:S(2)}, u32[]{:S(2)}) collective-permute-start(bf16[4,32,384]{2,1,0:T(8,128)(2,1)S(1)} %get-tuple-element.107), channel_id=1, source_target_pairs={{0,8},{1,9},{2,10},{3,11},{4,12},{5,13},{6,14},{7,15},{8,0},{9,1},... | collective-permute-start | bytes 294920 | tf_op jit(solution)/shard_map/ppermute | solution.py:30
  21.2 4.7 %collective-permute-start.2 = (bf16[4,32,384]{2,1,0:T(8,128)(2,1)S(1)}, bf16[4,32,384]{2,1,0:T(8,128)(2,1)S(1)}, u32[]{:S(2)}, u32[]{:S(2)}) collective-permute-start(bf16[4,32,384]{2,1,0:T(8,128)(2,1)S(1)} %get-tuple-element.106), channel_id=1, source_target_pairs={{0,12},{1,13},{2,14},{3,15},{4,0},{5,1},{6,2},{7,3},{8,4},{9,5},{1... | collective-permute-start | bytes 294920 | tf_op jit(solution)/shard_map/ppermute | solution.py:30
  26.7 108.1 %reduce-scatter.2.cloned.1.call-start = ((), (), s32[]{:S(2)}) async-start(), calls=%async_computation.6 | async-start | bytes 1966080 | tf_op jit(solution)/shard_map/reduce_scatter | solution.py:175
  26.9 26.6 %collective-permute-start.6 = (bf16[768,384]{1,0:T(8,128)(2,1)S(1)}, bf16[768,384]{1,0:T(8,128)(2,1)S(1)}, u32[]{:S(2)}, u32[]{:S(2)}) collective-permute-start(bf16[768,384]{1,0:T(8,128)(2,1)S(1)} %pad_maximum_fusion), channel_id=1, source_target_pairs={{0,4},{1,5},{2,6},{3,7},{4,8},{5,9},{6,10},{7,11},{8,12},{9,13},{1... | collective-permute-start | bytes 1769480 | tf_op jit(solution)/shard_map/ppermute | solution.py:30
  27.5 26.9 %collective-permute-start.7 = (bf16[768,384]{1,0:T(8,128)(2,1)S(1)}, bf16[768,384]{1,0:T(8,128)(2,1)}, u32[]{:S(2)}, u32[]{:S(2)}) collective-permute-start(bf16[768,384]{1,0:T(8,128)(2,1)S(1)} %pad_maximum_fusion), channel_id=1, source_target_pairs={{0,12},{1,13},{2,14},{3,15},{4,0},{5,1},{6,2},{7,3},{8,4},{9,5},{1... | collective-permute-start | bytes 1769480 | tf_op jit(solution)/shard_map/ppermute | solution.py:30
  29.6 15.3 %collective-permute-start.4 = (bf16[8,32,768]{2,1,0:T(8,128)(2,1)S(1)}, bf16[8,32,768]{2,1,0:T(8,128)(2,1)S(1)}, u32[]{:S(2)}, u32[]{:S(2)}) collective-permute-start(bf16[8,32,768]{2,1,0:T(8,128)(2,1)S(1)} %all-to-all-done), channel_id=1, source_target_pairs={{0,1},{1,2},{2,3},{3,0},{4,5},{5,6},{6,7},{7,4},{8,9},{9,10},{10,1... | collective-permute-start | bytes 1179656 | tf_op jit(solution)/shard_map/ppermute | solution.py:30
  32.6 20.9 %collective-permute-start.5 = (bf16[8,32,768]{2,1,0:T(8,128)(2,1)S(1)}, bf16[8,32,768]{2,1,0:T(8,128)(2,1)S(1)}, u32[]{:S(2)}, u32[]{:S(2)}) collective-permute-start(bf16[8,32,768]{2,1,0:T(8,128)(2,1)S(1)} %all-to-all-done), channel_id=1, source_target_pairs={{0,3},{1,0},{2,1},{3,2},{4,7},{5,4},{6,5},{7,6},{8,11},{9,8},{10,9... | collective-permute-start | bytes 1179656 | tf_op jit(solution)/shard_map/ppermute | solution.py:30
  53.5 0.8 copy-start.8
  54.4 10.4 %collective-permute-start.10 = (bf16[4,32,768]{2,1,0:T(8,128)(2,1)S(1)}, bf16[4,32,768]{2,1,0:T(8,128)(2,1)S(1)}, u32[]{:S(2)}, u32[]{:S(2)}) collective-permute-start(bf16[4,32,768]{2,1,0:T(8,128)(2,1)S(1)} %slice.58), channel_id=1, source_target_pairs={{0,1},{1,2},{2,3},{3,0},{4,5},{5,6},{6,7},{7,4},{8,9},{9,10},{10,1... | collective-permute-start | bytes 589832 | tf_op jit(solution)/shard_map/ppermute | solution.py:30
  56.9 7.8 %collective-permute-start.11 = (bf16[4,32,768]{2,1,0:T(8,128)(2,1)S(1)}, bf16[4,32,768]{2,1,0:T(8,128)(2,1)}, u32[]{:S(2)}, u32[]{:S(2)}) collective-permute-start(bf16[4,32,768]{2,1,0:T(8,128)(2,1)S(1)} %slice.59), channel_id=1, source_target_pairs={{0,3},{1,0},{2,1},{3,2},{4,7},{5,4},{6,5},{7,6},{8,11},{9,8},{10,9... | collective-permute-start | bytes 589832 | tf_op jit(solution)/shard_map/ppermute | solution.py:30
  59.1 17.1 %collective-permute-start.8 = (bf16[384,384]{1,0:T(8,128)(2,1)S(1)}, bf16[384,384]{1,0:T(8,128)(2,1)}, u32[]{:S(2)}, u32[]{:S(2)}) collective-permute-start(bf16[384,384]{1,0:T(8,128)(2,1)S(1)} %slice.56), channel_id=1, source_target_pairs={{0,4},{1,5},{2,6},{3,7},{4,8},{5,9},{6,10},{7,11},{8,12},{9,13},{1... | collective-permute-start | bytes 884744 | tf_op jit(solution)/shard_map/ppermute | solution.py:30
  60.2 16.7 %collective-permute-start.9 = (bf16[384,384]{1,0:T(8,128)(2,1)S(1)}, bf16[384,384]{1,0:T(8,128)(2,1)}, u32[]{:S(2)}, u32[]{:S(2)}) collective-permute-start(bf16[384,384]{1,0:T(8,128)(2,1)S(1)} %slice.57), channel_id=1, source_target_pairs={{0,12},{1,13},{2,14},{3,15},{4,0},{5,1},{6,2},{7,3},{8,4},{9,5},{1... | collective-permute-start | bytes 884744 | tf_op jit(solution)/shard_map/ppermute | solution.py:30
  71.4 2.3 %copy-start.3 = (f32[768,1536]{1,0:T(8,128)}, f32[768,1536]{1,0:T(8,128)S(1)}, u32[]{:S(2)}) copy-start(f32[768,1536]{1,0:T(8,128)S(1)} %fusion.2) | copy-start | bytes 14155780
  71.6 5.3 %copy-start.4 = (bf16[1024,1536]{1,0:T(8,128)(2,1)S(1)}, bf16[1024,1536]{1,0:T(8,128)(2,1)}, u32[]{:S(2)}) copy-start(bf16[1024,1536]{1,0:T(8,128)(2,1)} %all-gather.3.cloned.1.call-done) | copy-start | bytes 9437188
  71.6 5.3 %copy-start.9 = (bf16[768,384]{1,0:T(8,128)(2,1)S(1)}, bf16[768,384]{1,0:T(8,128)(2,1)}, u32[]{:S(2)}) copy-start(bf16[768,384]{1,0:T(8,128)(2,1)} %copy-done.8) | copy-start | bytes 1769476
  73.7 16.9 %collective-permute-start.15 = (bf16[192,1536]{1,0:T(8,128)(2,1)S(1)}, bf16[192,1536]{1,0:T(8,128)(2,1)S(1)}, u32[]{:S(2)}, u32[]{:S(2)}) collective-permute-start(bf16[192,1536]{1,0:T(8,128)(2,1)S(1)} %fusion.17), channel_id=1, source_target_pairs={{0,128},{1,129},{2,130},{3,131},{4,132},{5,133},{6,134},{7,135},{8... | collective-permute-start | bytes 1769480 | tf_op jit(solution)/shard_map/ppermute | solution.py:30
  73.8 10.4 %collective-permute-start.12 = (bf16[2,192,384]{2,1,0:T(8,128)(2,1)S(1)}, bf16[2,192,384]{2,1,0:T(8,128)(2,1)S(1)}, u32[]{:S(2)}, u32[]{:S(2)}) collective-permute-start(bf16[2,192,384]{2,1,0:T(8,128)(2,1)S(1)} %get-tuple-element.100), channel_id=1, source_target_pairs={{0,12},{1,13},{2,14},{3,15},{4,0},{5,1},{6,2},{7,3},{8,4},{9,5},{1... | collective-permute-start | bytes 884744 | tf_op jit(solution)/shard_map/ppermute | solution.py:30
  76.3 7.9 %collective-permute-start.13 = (bf16[2,192,384]{2,1,0:T(8,128)(2,1)S(1)}, bf16[2,192,384]{2,1,0:T(8,128)(2,1)S(1)}, u32[]{:S(2)}, u32[]{:S(2)}) collective-permute-start(bf16[2,192,384]{2,1,0:T(8,128)(2,1)S(1)} %get-tuple-element.99), channel_id=1, source_target_pairs={{0,8},{1,9},{2,10},{3,11},{4,12},{5,13},{6,14},{7,15},{8,0},{9,1},... | collective-permute-start | bytes 884744 | tf_op jit(solution)/shard_map/ppermute | solution.py:30
  76.3 14.3 %collective-permute-start.14 = (bf16[2,192,384]{2,1,0:T(8,128)(2,1)S(1)}, bf16[2,192,384]{2,1,0:T(8,128)(2,1)S(1)}, u32[]{:S(2)}, u32[]{:S(2)}) collective-permute-start(bf16[2,192,384]{2,1,0:T(8,128)(2,1)S(1)} %get-tuple-element.98), channel_id=1, source_target_pairs={{0,4},{1,5},{2,6},{3,7},{4,8},{5,9},{6,10},{7,11},{8,12},{9,13},{1... | collective-permute-start | bytes 884744 | tf_op jit(solution)/shard_map/ppermute | solution.py:30
  84.2 6.4 %copy-start.6 = (bf16[2,192,384]{2,1,0:T(8,128)(2,1)}, bf16[2,192,384]{2,1,0:T(8,128)(2,1)S(1)}, u32[]{:S(2)}) copy-start(bf16[2,192,384]{2,1,0:T(8,128)(2,1)S(1)} %collective-permute-done.13) | copy-start | bytes 884740
  91.8 1.4 copy-start.7
  93.1 6.3 %copy-start.10 = (f32[384,3]{0,1:T(4,128)S(1)}, f32[384,3]{0,1:T(4,128)}, u32[]{:S(2)}) copy-start(f32[384,3]{0,1:T(4,128)} %param.11) | copy-start | bytes 13828
  93.1 6.4 %copy-start.11 = (f32[384,3]{0,1:T(4,128)S(1)}, f32[384,3]{0,1:T(4,128)}, u32[]{:S(2)}) copy-start(f32[384,3]{0,1:T(4,128)} %param.13) | copy-start | bytes 13828
  93.1 14.3 %copy-start.1 = (bf16[384,384]{1,0:T(8,128)(2,1)S(1)}, bf16[384,384]{1,0:T(8,128)(2,1)}, u32[]{:S(2)}) copy-start(bf16[384,384]{1,0:T(8,128)(2,1)} %mcode.1) | copy-start | bytes 884740
  93.1 14.3 %copy-start.2 = (bf16[384,384]{1,0:T(8,128)(2,1)S(1)}, bf16[384,384]{1,0:T(8,128)(2,1)}, u32[]{:S(2)}) copy-start(bf16[384,384]{1,0:T(8,128)(2,1)} %scode.1) | copy-start | bytes 884740
  93.1 102.0 %all-gather.5.cloned.1.call-start = ((), (), s32[]{:S(2)}) async-start(), calls=%async_computation.7 | async-start | bytes 5013504 | tf_op jit(solution)/shard_map/all_gather | solution.py:190
  94.5 6.3 %collective-permute-start.16 = (bf16[192,384]{1,0:T(8,128)(2,1)S(1)}, bf16[192,384]{1,0:T(8,128)(2,1)S(1)}, u32[]{:S(2)}, u32[]{:S(2)}) collective-permute-start(bf16[192,384]{1,0:T(8,128)(2,1)S(1)} %fusion.18), channel_id=1, source_target_pairs={{0,128},{1,129},{2,130},{3,131},{4,132},{5,133},{6,134},{7,135},{8... | collective-permute-start | bytes 442376 | tf_op jit(solution)/shard_map/ppermute | solution.py:30
  97.8 4.4 %collective-permute-start.17 = (bf16[192,384]{1,0:T(8,128)(2,1)S(1)}, bf16[192,384]{1,0:T(8,128)(2,1)S(1)}, u32[]{:S(2)}, u32[]{:S(2)}) collective-permute-start(bf16[192,384]{1,0:T(8,128)(2,1)S(1)} %get-tuple-element.103), channel_id=1, source_target_pairs={{0,12},{1,13},{2,14},{3,15},{4,0},{5,1},{6,2},{7,3},{8,4},{9,5},{1... | collective-permute-start | bytes 442376 | tf_op jit(solution)/shard_map/ppermute | solution.py:30
  97.9 5.7 %collective-permute-start.18 = (bf16[192,384]{1,0:T(8,128)(2,1)S(1)}, bf16[192,384]{1,0:T(8,128)(2,1)S(1)}, u32[]{:S(2)}, u32[]{:S(2)}) collective-permute-start(bf16[192,384]{1,0:T(8,128)(2,1)S(1)} %get-tuple-element.102), channel_id=1, source_target_pairs={{0,8},{1,9},{2,10},{3,11},{4,12},{5,13},{6,14},{7,15},{8,0},{9,1},... | collective-permute-start | bytes 442376 | tf_op jit(solution)/shard_map/ppermute | solution.py:30
  98.0 9.4 %collective-permute-start.19 = (bf16[192,384]{1,0:T(8,128)(2,1)S(1)}, bf16[192,384]{1,0:T(8,128)(2,1)S(1)}, u32[]{:S(2)}, u32[]{:S(2)}) collective-permute-start(bf16[192,384]{1,0:T(8,128)(2,1)S(1)} %get-tuple-element.101), channel_id=1, source_target_pairs={{0,4},{1,5},{2,6},{3,7},{4,8},{5,9},{6,10},{7,11},{8,12},{9,13},{1... | collective-permute-start | bytes 442376 | tf_op jit(solution)/shard_map/ppermute | solution.py:30
  153.8 15.2 %all-to-all-start.3 = ((bf16[8,32,768]{2,1,0:T(8,128)(2,1)}), bf16[8,32,768]{2,1,0:T(8,128)(2,1)S(1)}, u32[]{:S(2)}, u32[]{:S(2)}) async-start(bf16[8,32,768]{2,1,0:T(8,128)(2,1)} %bitcast.83), calls=%async_computation.4 | async-start | bytes 786432 | tf_op jit(solution)/shard_map/all_to_all | solution.py:192
Sparse Core Ops, SparseCore 0:
  26.8 32.9 all-gather.2
  93.2 41.4 reduce-scatter.1
  153.9 41.0 all-gather.4

commit v3 on v2

--- a/solution.py
+++ b/solution.py
@@ -38,14 +38,9 @@
     return lax.optimization_barrier((array,) + others)[0]
 
 
-def total_of(row, axis):
-    spread = jnp.broadcast_to(row[None], (16, 8, 128))
-    return jnp.sum(lax.all_to_all(spread, axis, 0, 0, tiled=True), axis=0)
-
-
 def moments_kernel(
     upper, far, lower, one, two, three, master, mcode, mscale, scode, sscale,
-    update, new_mcode, new_mscale, new_scode, new_sscale, sums,
+    update, new_mcode, new_mscale, new_scode, new_sscale, spread, sums,
 ):
     rows, cols = master.shape
     blocks = mscale.shape[1]
@@ -95,12 +90,13 @@
         return carry
 
     lax.fori_loop(0, steps, body, 0)
-    sums[...] = jnp.broadcast_to(jnp.sum(sums[...], axis=1, keepdims=True), sums.shape)
+    totals = jnp.broadcast_to(jnp.sum(sums[...], axis=1, keepdims=True), sums.shape)
+    for i in range(spread.shape[0]):
+        spread[i] = totals
 
 
 def moments(upper, far, lower, others, master, mcode, mscale, scode, sscale):
     like = lambda a, dtype: jax.ShapeDtypeStruct(a.shape, dtype)
-    block = master.shape[1] // mscale.shape[1]
     return pl.pallas_call(
         moments_kernel,
         out_shape=(
@@ -109,15 +105,47 @@
             like(mscale, F32),
             like(master, BF16),
             like(sscale, F32),
-            jax.ShapeDtypeStruct((8, block), F32),
+            jax.ShapeDtypeStruct((16, 8, 128), F32),
         ),
         in_specs=[pl.BlockSpec(memory_space=pltpu.VMEM)] * 11,
         out_specs=[pl.BlockSpec(memory_space=pltpu.VMEM)] * 6,
+        scratch_shapes=[pltpu.VMEM((8, 128), F32)],
         compiler_params=pltpu.CompilerParams(vmem_limit_bytes=32 * 1024 * 1024),
         cost_estimate=pl.CostEstimate(
             flops=master.size, bytes_accessed=master.size, transcendentals=0
         ),
     )(upper, far, lower, *others, master, mcode, mscale, scode, sscale)
+
+
+def finish_kernel(sums, master, update, new_master, new16, trust):
+    row = jnp.sum(sums[...], axis=0)
+    ratio = jnp.sqrt(row[0:1, :]) / (jnp.sqrt(row[1:2, :]) + 1e-06)
+    trust[...] = jnp.broadcast_to(ratio, trust.shape)
+    rate = 0.02 * ratio
+    rows, cols = master.shape
+    for at in range(0, cols, 128):
+        cut = slice(at, at + 128)
+        fresh = master[:, cut] - rate * update[:, cut]
+        new_master[:, cut] = fresh
+        new16[:, cut] = fresh.astype(BF16)
+
+
+def finish(sums, master, update):
+    whole = pl.BlockSpec(memory_space=pltpu.VMEM)
+    return pl.pallas_call(
+        finish_kernel,
+        out_shape=(
+            jax.ShapeDtypeStruct(master.shape, F32),
+            jax.ShapeDtypeStruct(master.shape, BF16),
+            jax.ShapeDtypeStruct((8, 128), F32),
+        ),
+        in_specs=[whole] * 3,
+        out_specs=[whole] * 3,
+        compiler_params=pltpu.CompilerParams(vmem_limit_bytes=32 * 1024 * 1024),
+        cost_estimate=pl.CostEstimate(
+            flops=master.size, bytes_accessed=master.size, transcendentals=0
+        ),
+    )(sums, master, update)
 
 
 def local(layer_input, out_grad, master, moment_code, moment_scale, second_code, second_scale):
@@ -140,20 +168,22 @@
     wings = [shift(weights, x=1), shift(weights, x=-1)]
     moved, wings = lax.optimization_barrier((moved, wings))
     across = [shift(moved[0][:4], high=1), shift(moved[1][4:], high=-1)]
-    moved = [moved[0], jnp.concatenate(across), moved[1]]
+    pieces = [(mine, 0, 0), (moved[0], 1, 0), (moved[1], 3, 0), (across[0], 2, 0), (across[1], 2, 4)]
     across = [shift(wings[0][:rows], x=1), shift(wings[1][rows:], x=-1)]
     near = jnp.concatenate(parts, axis=2).reshape(4 * few, 4 * cols)
     wide = lax.all_gather(near, "dp", axis=0, tiled=True, axis_index_groups=NEAR)
 
     groups = wide.reshape(8, 4, few, 4 * cols)
+    cuts = [
+        take(groups, (high + 4 - q) % 4, 1)[at : at + len(piece)].reshape(-1, 4 * cols)
+        for piece, q, at in pieces
+    ]
+    ready, cuts = lax.optimization_barrier(([piece for piece, _, _ in pieces], cuts))
     part = sum(
         jnp.einsum(
-            "tk,tn->kn",
-            piece.reshape(8 * few, 2 * rows),
-            take(groups, (high + 4 - q) % 4, 1).reshape(8 * few, 4 * cols),
-            preferred_element_type=F32,
+            "tk,tn->kn", piece.reshape(-1, 2 * rows), cut, preferred_element_type=F32
         )
-        for q, piece in enumerate([mine] + moved)
+        for piece, cut in zip(ready, cuts)
     )
     part = (part * inv_root).reshape(2, rows, 4 * cols)
     half = rows // 2
@@ -180,14 +210,11 @@
         take(upper, z, 0), far, block(lower, 0), others,
         master, moment_code, moment_scale, second_code, second_scale,
     )
-    sums = total_of(sums, "dp")
-    summed, sums = lax.optimization_barrier((summed, sums))
-    sums = total_of(sums, "tensor")
-    weight_sq, update_sq = sums[0, 0], sums[1, 0]
-    trust_ratio = jnp.sqrt(weight_sq) / (jnp.sqrt(update_sq) + 1e-06)
-    rate = 0.02 * trust_ratio
-    new_master = master - rate * update
-    new_weight = lax.all_gather(new_master.astype(BF16), "dp", axis=0, tiled=True)
+    spread = jnp.broadcast_to(jnp.sum(lax.all_to_all(sums, "dp", 0, 0, tiled=True), axis=0), sums.shape)
+    sums = lax.all_to_all(spread, "tensor", 0, 0, tiled=True)
+    new_master, new16, trust_ratio = finish(sums, master, update)
+    new_weight = lax.all_gather(after(new16, summed), "dp", axis=0, tiled=True)
+    trust_ratio = trust_ratio[0, 0]
 
     back = lax.all_to_all(
         after(summed, sums), "dp", 0, 0, tiled=True, axis_index_groups=NEAR

time: 208 us -> 193 us (0.928)
  waiting for transfers between devices: 80.9 us -> 66.2 us
  starting transfers between devices: 41.6 us -> 38.2 us
  between operations: 16.6 us -> 14 us
    reduce_scatter x1, waiting for transfers between devices: 8.22 us -> 0.01 us  [local(): lax.psum_scatter(outs.reshape(32 * few, 2 * rows), 'tensor', scatter_dime...]
    ppermute x20, waiting for transfers between devices: 40.4 us -> 35.7 us  [shift(): return lax.ppermute(array, BOTH, pairs)]
    all_gather x1, waiting for transfers between devices: 24.7 us -> 21.9 us  [local(): new_weight = lax.all_gather(after(new16, summed), 'dp', axis=0, tiled=True)]
    dot_general x4 -> x5, matrix products: 3.53 us -> 5.45 us  [local(): jnp.einsum('tk,tn->kn', piece.reshape(-1, 2 * rows), cut, preferred_eleme...]
    unnamed x31 -> x27, local copies, waits for them, and re-layouts: 11.2 us -> 11.7 us
  transfers between devices with their start and end apart: 25 -> 25, of which waited for: 13 -> 12; matrix products, arithmetic and copies ran while one was open for 9% -> 12% of each run, Pallas kernels for 1% -> 2%
where the time goes in v3:
time: 193 us
  waiting for transfers between devices  66.2 us (34%)
  starting transfers between devices  38.2 us (20%)
  blocking collectives  34.3 us (18%)
  local copies, waits for them, and re-layouts  21.8 us (11%)
  between operations  14 us (7%)
  matrix products  9.32 us (5%)
  other arithmetic  4.79 us (2%)
  Pallas kernels  3.84 us (2%)
    ppermute x20, waiting for transfers between devices, shift(): return lax.ppermute(array, BOTH, pairs)  35.7 us
    ppermute x20, starting transfers between devices, shift(): return lax.ppermute(array, BOTH, pairs)  26.7 us
    all_gather x1, waiting for transfers between devices, local(): new_weight = lax.all_gather(after(new16, summed), 'dp', axis=0, tiled=True)  21.9 us
    all_to_all x1, blocking collectives, local(): sums = lax.all_to_all(spread, 'tensor', 0, 0, tiled=True)  19.3 us
    all_to_all x1, blocking collectives, local(): lax.all_to_all(sums, 'dp', 0, 0, tiled=True)  15 us
    unnamed x27, local copies, waits for them, and re-layouts  11.7 us
    all_to_all x1, waiting for transfers between devices, local(): lax.all_to_all(after(summed, sums), 'dp', 0, 0, tiled=True, axis_index_gr...  8.65 us
    all_to_all x1, starting transfers between devices, local(): mine = lax.all_to_all(mine, 'dp', 0, 0, tiled=True, axis_index_groups=NEAR)  6.6 us
  transfers between devices with their start and end apart: 25, of which 12 were waited for; matrix products, arithmetic and copies ran while one was open for 12% of the time, Pallas kernels for 2%

profile of v3, /device:TPU:1, one launch (start us, length us, event | category | flops | bytes accessed | tf_op | source)
XLA Modules:
  0.0 192.6 jit_solution(86946221751663026)
XLA Ops:
  7.2 1.1 copy.32
  8.6 1.0 reshape.90
  9.6 6.6 %all-to-all-start = ((bf16[8,32,768]{2,1,0:T(8,128)(2,1)}), bf16[8,32,768]{2,1,0:T(8,128)(2,1)S(1)}, u32[]{:S(2)}, u32[]{:S(2)}) async-start(bf16[8,32,768]{2,1,0:T(8,128)(2,1)} %reshape.90), calls=%async_computation | async-start | bytes 786432 | tf_op jit(solution)/shard_map/all_to_all | solution.py:162
  16.2 1.1 convert_element_type.36
  17.3 1.1 collective-permute-start.3
  18.4 1.1 dynamic-slice_bitcast_fusion.1
  19.5 1.3 collective-permute-start
  20.8 2.5 %collective-permute-start.1 = (bf16[4,32,384]{2,1,0:T(8,128)(2,1)S(1)}, bf16[4,32,384]{2,1,0:T(8,128)(2,1)S(1)}, u32[]{:S(2)}, u32[]{:S(2)}) collective-permute-start(bf16[4,32,384]{2,1,0:T(8,128)(2,1)S(1)} %get-tuple-element.122), channel_id=1, source_target_pairs={{0,8},{1,9},{2,10},{3,11},{4,12},{5,13},{6,14},{7,15},{8,0},{9,1},... | collective-permute-start | bytes 294920 | tf_op jit(solution)/shard_map/ppermute | solution.py:30
  23.2 1.2 collective-permute-start.2
  24.8 3.1 %collective-permute-done.1 = bf16[4,32,384]{2,1,0:T(8,128)(2,1)S(1)} collective-permute-done((bf16[4,32,384]{2,1,0:T(8,128)(2,1)S(1)}, bf16[4,32,384]{2,1,0:T(8,128)(2,1)S(1)}, u32[]{:S(2)}, u32[]{:S(2)}) %collective-permute-start.1) | collective-permute-done | bytes 98336 | tf_op jit(solution)/shard_map/ppermute | solution.py:30
  29.6 2.1 %collective-permute-start.7 = (bf16[768,384]{1,0:T(8,128)(2,1)S(1)}, bf16[768,384]{1,0:T(8,128)(2,1)}, u32[]{:S(2)}, u32[]{:S(2)}) collective-permute-start(bf16[768,384]{1,0:T(8,128)(2,1)S(1)} %pad_maximum_fusion), channel_id=1, source_target_pairs={{0,12},{1,13},{2,14},{3,15},{4,0},{5,1},{6,2},{7,3},{8,4},{9,5},{1... | collective-permute-start | bytes 1769480 | tf_op jit(solution)/shard_map/ppermute | solution.py:30
  31.7 3.0 %collective-permute-start.4 = (bf16[8,32,768]{2,1,0:T(8,128)(2,1)S(1)}, bf16[8,32,768]{2,1,0:T(8,128)(2,1)S(1)}, u32[]{:S(2)}, u32[]{:S(2)}) collective-permute-start(bf16[8,32,768]{2,1,0:T(8,128)(2,1)S(1)} %all-to-all-done), channel_id=1, source_target_pairs={{0,1},{1,2},{2,3},{3,0},{4,5},{5,6},{6,7},{7,4},{8,9},{9,10},{10,1... | collective-permute-start | bytes 1179656 | tf_op jit(solution)/shard_map/ppermute | solution.py:30
  34.7 2.1 %collective-permute-start.5 = (bf16[8,32,768]{2,1,0:T(8,128)(2,1)S(1)}, bf16[8,32,768]{2,1,0:T(8,128)(2,1)S(1)}, u32[]{:S(2)}, u32[]{:S(2)}) collective-permute-start(bf16[8,32,768]{2,1,0:T(8,128)(2,1)S(1)} %all-to-all-done), channel_id=1, source_target_pairs={{0,3},{1,0},{2,1},{3,2},{4,7},{5,4},{6,5},{7,6},{8,11},{9,8},{10,9... | collective-permute-start | bytes 1179656 | tf_op jit(solution)/shard_map/ppermute | solution.py:30
  36.8 10.2 %collective-permute-done.4 = bf16[8,32,768]{2,1,0:T(8,128)(2,1)S(1)} collective-permute-done((bf16[8,32,768]{2,1,0:T(8,128)(2,1)S(1)}, bf16[8,32,768]{2,1,0:T(8,128)(2,1)S(1)}, u32[]{:S(2)}, u32[]{:S(2)}) %collective-permute-start.4) | collective-permute-done | bytes 393248 | tf_op jit(solution)/shard_map/ppermute | solution.py:30
  47.0 8.6 %collective-permute-done.5 = bf16[8,32,768]{2,1,0:T(8,128)(2,1)S(1)} collective-permute-done((bf16[8,32,768]{2,1,0:T(8,128)(2,1)S(1)}, bf16[8,32,768]{2,1,0:T(8,128)(2,1)S(1)}, u32[]{:S(2)}, u32[]{:S(2)}) %collective-permute-start.5) | collective-permute-done | bytes 393248 | tf_op jit(solution)/shard_map/ppermute | solution.py:30
  55.6 0.8 copy-done.6
  56.4 2.6 %collective-permute-start.10 = (bf16[4,32,768]{2,1,0:T(8,128)(2,1)S(1)}, bf16[4,32,768]{2,1,0:T(8,128)(2,1)}, u32[]{:S(2)}, u32[]{:S(2)}) collective-permute-start(bf16[4,32,768]{2,1,0:T(8,128)(2,1)S(1)} %slice.63), channel_id=1, source_target_pairs={{0,1},{1,2},{2,3},{3,0},{4,5},{5,6},{6,7},{7,4},{8,9},{9,10},{10,1... | collective-permute-start | bytes 589832 | tf_op jit(solution)/shard_map/ppermute | solution.py:30
  59.0 1.2 collective-permute-start.11
  60.2 1.0 slice.61
  61.3 1.0 slice.62
  62.3 2.9 %collective-permute-start.9 = (bf16[384,384]{1,0:T(8,128)(2,1)S(1)}, bf16[384,384]{1,0:T(8,128)(2,1)}, u32[]{:S(2)}, u32[]{:S(2)}) collective-permute-start(bf16[384,384]{1,0:T(8,128)(2,1)S(1)} %slice.62), channel_id=1, source_target_pairs={{0,12},{1,13},{2,14},{3,15},{4,0},{5,1},{6,2},{7,3},{8,4},{9,5},{1... | collective-permute-start | bytes 884744 | tf_op jit(solution)/shard_map/ppermute | solution.py:30
  65.2 2.0 %constant_dynamic-slice_fusion.2 = (bf16[8,1,32,1536]{3,2,1,0:T(8,128)(2,1)S(1)}, bf16[8,1,32,1536]{3,2,1,0:T(8,128)(2,1)S(1)}, bf16[8,1,32,1536]{3,2,1,0:T(8,128)(2,1)S(1)}) fusion(bf16[8,4,32,1536]{3,2,1,0:T(8,128)(2,1)} %bitcast.62, s32[]{:T(128)S(6)} %select_n.111, s32[]{:T(128)S(6)} %select_n.109, s32[]{:T(128)S(6)} %select_n.107), kind=kLoop, calls=%fused_computation.32 | loop fusion | bytes 4718604 | tf_op jit(solution)/shard_map/jit(dynamic_index_in_dim)/dynamic_slice | solution.py:34
  68.7 0.8 fusion.20
  69.5 0.8 fusion.22
  70.3 1.7 fusion.23
  72.0 1.3 add_multiply_fusion
  73.9 1.6 copy-done.3
  77.2 3.9 %multiply_convert_fusion = bf16[1024,768]{1,0:T(8,128)(2,1)S(1)} fusion(bf16[1024,1536]{1,0:T(8,128)(2,1)S(1)} %copy-done.4, bf16[768,384]{1,0:T(8,128)(2,1)} %collective-permute-done.7, bf16[384,384]{1,0:T(8,128)(2,1)} %collective-permute-done.9, bf16[384,384]{1,0:T(8,128)(2,1)} %collective-permute-done.8, bf16[768,384]{1,0:T(8,128)(2,1)S(1)} %copy-done.7, ...), kind=kOutput, calls=%fused_computation.1 | convolution fusion | flops 2431647744 | bytes 7077888 | tf_op jit(solution)/shard_map/tn,kn->tk/dot_general | solution.py:203
  81.6 1.6 collective-permute-done.13
  83.2 6.9 %collective-permute-done.14 = bf16[2,192,384]{2,1,0:T(8,128)(2,1)S(1)} collective-permute-done((bf16[2,192,384]{2,1,0:T(8,128)(2,1)S(1)}, bf16[2,192,384]{2,1,0:T(8,128)(2,1)S(1)}, u32[]{:S(2)}, u32[]{:S(2)}) %collective-permute-start.14) | collective-permute-done | bytes 294944 | tf_op jit(solution)/shard_map/ppermute | solution.py:30
  90.1 1.2 fusion.17
  91.3 1.3 copy.26
  92.7 1.3 slice_add_fusion
  94.0 3.0 %collective-permute-start.16 = (bf16[192,384]{1,0:T(8,128)(2,1)S(1)}, bf16[192,384]{1,0:T(8,128)(2,1)S(1)}, u32[]{:S(2)}, u32[]{:S(2)}) collective-permute-start(bf16[192,384]{1,0:T(8,128)(2,1)S(1)} %fusion.15), channel_id=1, source_target_pairs={{0,128},{1,129},{2,130},{3,131},{4,132},{5,133},{6,134},{7,135},{8... | collective-permute-start | bytes 442376 | tf_op jit(solution)/shard_map/ppermute | solution.py:30
  97.3 1.3 collective-permute-start.19
  98.9 1.0 slice.82.lower
  99.9 1.5 collective-permute-done.17.one
  101.4 1.4 collective-permute-done.18.two
  102.8 1.5 collective-permute-done.19.three
  104.3 2.8 %shard_map.134 = (f32[384,384]{1,0:T(8,128)S(1)}, bf16[384,384]{1,0:T(8,128)(2,1)}, f32[384,3]{1,0:T(8,128)S(1)}, bf16[384,384]{1,0:T(8,128)(2,1)}, f32[384,3]{1,0:T(8,128)S(1)}, /*index=5*/f32[16,8,128]{2,1,0:T(8,128)S(1)}) custom-call(f32[192,384]{1,0:T(8,128)S(1)} %dynamic-slice_bitcast_fusion.upper, bf16[192,384]{1,0:T(8,128)(2,1)S(1)} %collective-permute-done.16.far, ...), custom_call_target="tpu_custom_call" | custom-call | flops 147456 | bytes 147456 | tf_op jit(solution)/shard_map/pallas_call | solution.py:100
  107.1 15.0 %all_to_all.20 = f32[16,8,128]{2,1,0:T(8,128)S(1)} all-to-all(f32[16,8,128]{2,1,0:T(8,128)S(1)} %get-tuple-element.71), channel_id=1, replica_groups=mesh['dp'=16,'tensor'=16] {'dp'}, dimensions={0} | all-to-all | bytes 131072 | tf_op jit(solution)/shard_map/all_to_all | solution.py:213
  122.2 19.3 %all_to_all.21.sums = f32[16,8,128]{2,1,0:T(8,128)S(1)} all-to-all(f32[16,8,128]{2,1,0:T(8,128)S(1)} %broadcast_in_dim.3), channel_id=1, replica_groups=mesh['dp'=16,'tensor'=16] {'tensor'}, dimensions={0} | all-to-all | bytes 131072 | tf_op jit(solution)/shard_map/all_to_all | solution.py:214
  141.4 1.0 shard_map.135
  142.5 4.9 %all-to-all-start.3 = ((bf16[8,32,768]{2,1,0:T(8,128)(2,1)}), bf16[8,32,768]{2,1,0:T(8,128)(2,1)S(1)}, u32[]{:S(2)}, u32[]{:S(2)}) async-start(bf16[8,32,768]{2,1,0:T(8,128)(2,1)} %bitcast.80), calls=%async_computation.4 | async-start | bytes 786432 | tf_op jit(solution)/shard_map/all_to_all | solution.py:219
  149.2 8.7 %all-to-all-done.3 = bf16[8,32,768]{2,1,0:T(8,128)(2,1)S(1)} async-done(((bf16[8,32,768]{2,1,0:T(8,128)(2,1)}), bf16[8,32,768]{2,1,0:T(8,128)(2,1)S(1)}, u32[]{:S(2)}, u32[]{:S(2)}) %all-to-all-start.3) | async-done | bytes 393248 | tf_op jit(solution)/shard_map/all_to_all | solution.py:219
  158.4 0.8 copy.33
  159.2 21.9 %all-gather.5.cloned.1.call-done = bf16[6144,384]{1,0:T(8,128)(2,1)} async-done(((bf16[384,384]{1,0:T(8,128)(2,1)}), bf16[6144,384]{1,0:T(8,128)(2,1)}) %all-gather.5.cloned.1.call-update) | async-done | bytes 4718608 | tf_op jit(solution)/shard_map/all_gather | solution.py:216
  181.0 5.0 %copy.37 = bf16[6144,384]{1,0:T(8,128)(2,1)} copy(bf16[6144,384]{1,0:T(8,128)(2,1)} %all-gather.5.cloned.1.call-done) | data formatting | bytes 9437184
  (71 shorter events, 9.8 us)
Async XLA Ops:
  7.2 21.6 %copy-start = (f32[384,384]{1,0:T(8,128)S(1)}, f32[384,384]{1,0:T(8,128)}, u32[]{:S(2)}) copy-start(f32[384,384]{1,0:T(8,128)} %master.3) | copy-start | bytes 1769476
  9.6 18.3 %all-to-all-start = ((bf16[8,32,768]{2,1,0:T(8,128)(2,1)}), bf16[8,32,768]{2,1,0:T(8,128)(2,1)S(1)}, u32[]{:S(2)}, u32[]{:S(2)}) async-start(bf16[8,32,768]{2,1,0:T(8,128)(2,1)} %reshape.90), calls=%async_computation | async-start | bytes 786432 | tf_op jit(solution)/shard_map/all_to_all | solution.py:162
  16.2 49.0 %all-gather.3.cloned.1.call-start = ((), (), s32[]{:S(2)}) async-start(), calls=%async_computation.5 | async-start | bytes 3538944 | tf_op jit(solution)/shard_map/all_gather | solution.py:174
  17.3 10.6 %collective-permute-start.3 = (bf16[384,384]{1,0:T(8,128)(2,1)S(1)}, bf16[384,384]{1,0:T(8,128)(2,1)S(1)}, u32[]{:S(2)}, u32[]{:S(2)}) collective-permute-start(bf16[384,384]{1,0:T(8,128)(2,1)S(1)} %convert_element_type.36), channel_id=1, source_target_pairs={{0,128},{1,129},{2,130},{3,131},{4,132},{5,133},{6,134},{7,135},{8... | collective-permute-start | bytes 884744 | tf_op jit(solution)/shard_map/ppermute | solution.py:30
  19.5 5.3 %collective-permute-start = (bf16[4,32,384]{2,1,0:T(8,128)(2,1)S(1)}, bf16[4,32,384]{2,1,0:T(8,128)(2,1)S(1)}, u32[]{:S(2)}, u32[]{:S(2)}) collective-permute-start(bf16[4,32,384]{2,1,0:T(8,128)(2,1)S(1)} %get-tuple-element.123), channel_id=1, source_target_pairs={{0,4},{1,5},{2,6},{3,7},{4,8},{5,9},{6,10},{7,11},{8,12},{9,13},{1... | collective-permute-start | bytes 294920 | tf_op jit(solution)/shard_map/ppermute | solution.py:30
  20.8 7.1 %collective-permute-start.1 = (bf16[4,32,384]{2,1,0:T(8,128)(2,1)S(1)}, bf16[4,32,384]{2,1,0:T(8,128)(2,1)S(1)}, u32[]{:S(2)}, u32[]{:S(2)}) collective-permute-start(bf16[4,32,384]{2,1,0:T(8,128)(2,1)S(1)} %get-tuple-element.122), channel_id=1, source_target_pairs={{0,8},{1,9},{2,10},{3,11},{4,12},{5,13},{6,14},{7,15},{8,0},{9,1},... | collective-permute-start | bytes 294920 | tf_op jit(solution)/shard_map/ppermute | solution.py:30
  23.2 4.7 %collective-permute-start.2 = (bf16[4,32,384]{2,1,0:T(8,128)(2,1)S(1)}, bf16[4,32,384]{2,1,0:T(8,128)(2,1)S(1)}, u32[]{:S(2)}, u32[]{:S(2)}) collective-permute-start(bf16[4,32,384]{2,1,0:T(8,128)(2,1)S(1)} %get-tuple-element.121), channel_id=1, source_target_pairs={{0,12},{1,13},{2,14},{3,15},{4,0},{5,1},{6,2},{7,3},{8,4},{9,5},{1... | collective-permute-start | bytes 294920 | tf_op jit(solution)/shard_map/ppermute | solution.py:30
  28.7 113.7 %reduce-scatter.2.cloned.1.call-start = ((), (), s32[]{:S(2)}) async-start(), calls=%async_computation.6 | async-start | bytes 1966080 | tf_op jit(solution)/shard_map/reduce_scatter | solution.py:205
  29.0 26.6 %collective-permute-start.6 = (bf16[768,384]{1,0:T(8,128)(2,1)S(1)}, bf16[768,384]{1,0:T(8,128)(2,1)S(1)}, u32[]{:S(2)}, u32[]{:S(2)}) collective-permute-start(bf16[768,384]{1,0:T(8,128)(2,1)S(1)} %pad_maximum_fusion), channel_id=1, source_target_pairs={{0,4},{1,5},{2,6},{3,7},{4,8},{5,9},{6,10},{7,11},{8,12},{9,13},{1... | collective-permute-start | bytes 1769480 | tf_op jit(solution)/shard_map/ppermute | solution.py:30
  29.6 26.9 %collective-permute-start.7 = (bf16[768,384]{1,0:T(8,128)(2,1)S(1)}, bf16[768,384]{1,0:T(8,128)(2,1)}, u32[]{:S(2)}, u32[]{:S(2)}) collective-permute-start(bf16[768,384]{1,0:T(8,128)(2,1)S(1)} %pad_maximum_fusion), channel_id=1, source_target_pairs={{0,12},{1,13},{2,14},{3,15},{4,0},{5,1},{6,2},{7,3},{8,4},{9,5},{1... | collective-permute-start | bytes 1769480 | tf_op jit(solution)/shard_map/ppermute | solution.py:30
  31.7 15.3 %collective-permute-start.4 = (bf16[8,32,768]{2,1,0:T(8,128)(2,1)S(1)}, bf16[8,32,768]{2,1,0:T(8,128)(2,1)S(1)}, u32[]{:S(2)}, u32[]{:S(2)}) collective-permute-start(bf16[8,32,768]{2,1,0:T(8,128)(2,1)S(1)} %all-to-all-done), channel_id=1, source_target_pairs={{0,1},{1,2},{2,3},{3,0},{4,5},{5,6},{6,7},{7,4},{8,9},{9,10},{10,1... | collective-permute-start | bytes 1179656 | tf_op jit(solution)/shard_map/ppermute | solution.py:30
  34.7 20.9 %collective-permute-start.5 = (bf16[8,32,768]{2,1,0:T(8,128)(2,1)S(1)}, bf16[8,32,768]{2,1,0:T(8,128)(2,1)S(1)}, u32[]{:S(2)}, u32[]{:S(2)}) collective-permute-start(bf16[8,32,768]{2,1,0:T(8,128)(2,1)S(1)} %all-to-all-done), channel_id=1, source_target_pairs={{0,3},{1,0},{2,1},{3,2},{4,7},{5,4},{6,5},{7,6},{8,11},{9,8},{10,9... | collective-permute-start | bytes 1179656 | tf_op jit(solution)/shard_map/ppermute | solution.py:30
  55.6 0.8 copy-start.6
  56.4 11.4 %collective-permute-start.10 = (bf16[4,32,768]{2,1,0:T(8,128)(2,1)S(1)}, bf16[4,32,768]{2,1,0:T(8,128)(2,1)}, u32[]{:S(2)}, u32[]{:S(2)}) collective-permute-start(bf16[4,32,768]{2,1,0:T(8,128)(2,1)S(1)} %slice.63), channel_id=1, source_target_pairs={{0,1},{1,2},{2,3},{3,0},{4,5},{5,6},{6,7},{7,4},{8,9},{9,10},{10,1... | collective-permute-start | bytes 589832 | tf_op jit(solution)/shard_map/ppermute | solution.py:30
  59.0 8.9 %collective-permute-start.11 = (bf16[4,32,768]{2,1,0:T(8,128)(2,1)S(1)}, bf16[4,32,768]{2,1,0:T(8,128)(2,1)S(1)}, u32[]{:S(2)}, u32[]{:S(2)}) collective-permute-start(bf16[4,32,768]{2,1,0:T(8,128)(2,1)S(1)} %slice.64), channel_id=1, source_target_pairs={{0,3},{1,0},{2,1},{3,2},{4,7},{5,4},{6,5},{7,6},{8,11},{9,8},{10,9... | collective-permute-start | bytes 589832 | tf_op jit(solution)/shard_map/ppermute | solution.py:30
  61.2 15.3 %collective-permute-start.8 = (bf16[384,384]{1,0:T(8,128)(2,1)S(1)}, bf16[384,384]{1,0:T(8,128)(2,1)}, u32[]{:S(2)}, u32[]{:S(2)}) collective-permute-start(bf16[384,384]{1,0:T(8,128)(2,1)S(1)} %slice.61), channel_id=1, source_target_pairs={{0,4},{1,5},{2,6},{3,7},{4,8},{5,9},{6,10},{7,11},{8,12},{9,13},{1... | collective-permute-start | bytes 884744 | tf_op jit(solution)/shard_map/ppermute | solution.py:30
  62.3 14.9 %collective-permute-start.9 = (bf16[384,384]{1,0:T(8,128)(2,1)S(1)}, bf16[384,384]{1,0:T(8,128)(2,1)}, u32[]{:S(2)}, u32[]{:S(2)}) collective-permute-start(bf16[384,384]{1,0:T(8,128)(2,1)S(1)} %slice.62), channel_id=1, source_target_pairs={{0,12},{1,13},{2,14},{3,15},{4,0},{5,1},{6,2},{7,3},{8,4},{9,5},{1... | collective-permute-start | bytes 884744 | tf_op jit(solution)/shard_map/ppermute | solution.py:30
  65.2 2.6 %copy-start.4 = (bf16[1024,1536]{1,0:T(8,128)(2,1)S(1)}, bf16[1024,1536]{1,0:T(8,128)(2,1)}, u32[]{:S(2)}) copy-start(bf16[1024,1536]{1,0:T(8,128)(2,1)} %all-gather.3.cloned.1.call-done) | copy-start | bytes 9437188
  73.4 2.2 %copy-start.3 = (f32[768,1536]{1,0:T(8,128)}, f32[768,1536]{1,0:T(8,128)S(1)}, u32[]{:S(2)}) copy-start(f32[768,1536]{1,0:T(8,128)S(1)} %add_multiply_fusion) | copy-start | bytes 14155780
  73.6 3.6 %copy-start.7 = (bf16[768,384]{1,0:T(8,128)(2,1)S(1)}, bf16[768,384]{1,0:T(8,128)(2,1)}, u32[]{:S(2)}) copy-start(bf16[768,384]{1,0:T(8,128)(2,1)} %copy-done.6) | copy-start | bytes 1769476
  75.6 14.5 %collective-permute-start.15 = (bf16[192,1536]{1,0:T(8,128)(2,1)S(1)}, bf16[192,1536]{1,0:T(8,128)(2,1)S(1)}, u32[]{:S(2)}, u32[]{:S(2)}) collective-permute-start(bf16[192,1536]{1,0:T(8,128)(2,1)S(1)} %fusion.14), channel_id=1, source_target_pairs={{0,128},{1,129},{2,130},{3,131},{4,132},{5,133},{6,134},{7,135},{8... | collective-permute-start | bytes 1769480 | tf_op jit(solution)/shard_map/ppermute | solution.py:30
  75.7 5.9 %collective-permute-start.12 = (bf16[2,192,384]{2,1,0:T(8,128)(2,1)S(1)}, bf16[2,192,384]{2,1,0:T(8,128)(2,1)S(1)}, u32[]{:S(2)}, u32[]{:S(2)}) collective-permute-start(bf16[2,192,384]{2,1,0:T(8,128)(2,1)S(1)} %get-tuple-element.115), channel_id=1, source_target_pairs={{0,12},{1,13},{2,14},{3,15},{4,0},{5,1},{6,2},{7,3},{8,4},{9,5},{1... | collective-permute-start | bytes 884744 | tf_op jit(solution)/shard_map/ppermute | solution.py:30
  76.0 7.2 %collective-permute-start.13 = (bf16[2,192,384]{2,1,0:T(8,128)(2,1)S(1)}, bf16[2,192,384]{2,1,0:T(8,128)(2,1)S(1)}, u32[]{:S(2)}, u32[]{:S(2)}) collective-permute-start(bf16[2,192,384]{2,1,0:T(8,128)(2,1)S(1)} %get-tuple-element.114), channel_id=1, source_target_pairs={{0,8},{1,9},{2,10},{3,11},{4,12},{5,13},{6,14},{7,15},{8,0},{9,1},... | collective-permute-start | bytes 884744 | tf_op jit(solution)/shard_map/ppermute | solution.py:30
  76.6 13.5 %collective-permute-start.14 = (bf16[2,192,384]{2,1,0:T(8,128)(2,1)S(1)}, bf16[2,192,384]{2,1,0:T(8,128)(2,1)S(1)}, u32[]{:S(2)}, u32[]{:S(2)}) collective-permute-start(bf16[2,192,384]{2,1,0:T(8,128)(2,1)S(1)} %get-tuple-element.113), channel_id=1, source_target_pairs={{0,4},{1,5},{2,6},{3,7},{4,8},{5,9},{6,10},{7,11},{8,12},{9,13},{1... | collective-permute-start | bytes 884744 | tf_op jit(solution)/shard_map/ppermute | solution.py:30
  90.1 2.6 %copy-start.5 = (bf16[2,192,384]{2,1,0:T(8,128)(2,1)}, bf16[2,192,384]{2,1,0:T(8,128)(2,1)S(1)}, u32[]{:S(2)}) copy-start(bf16[2,192,384]{2,1,0:T(8,128)(2,1)S(1)} %collective-permute-done.14) | copy-start | bytes 884740
  91.3 7.3 %copy-start.8 = (f32[384,3]{0,1:T(4,128)S(1)}, f32[384,3]{0,1:T(4,128)}, u32[]{:S(2)}) copy-start(f32[384,3]{0,1:T(4,128)} %param.11) | copy-start | bytes 13828
  91.3 7.4 %copy-start.9 = (f32[384,3]{0,1:T(4,128)S(1)}, f32[384,3]{0,1:T(4,128)}, u32[]{:S(2)}) copy-start(f32[384,3]{0,1:T(4,128)} %param.13) | copy-start | bytes 13828
  91.3 13.0 %copy-start.1 = (bf16[384,384]{1,0:T(8,128)(2,1)S(1)}, bf16[384,384]{1,0:T(8,128)(2,1)}, u32[]{:S(2)}) copy-start(bf16[384,384]{1,0:T(8,128)(2,1)} %mcode.1) | copy-start | bytes 884740
  91.3 13.0 %copy-start.2 = (bf16[384,384]{1,0:T(8,128)(2,1)S(1)}, bf16[384,384]{1,0:T(8,128)(2,1)}, u32[]{:S(2)}) copy-start(bf16[384,384]{1,0:T(8,128)(2,1)} %scode.1) | copy-start | bytes 884740
  92.6 88.4 %all-gather.5.cloned.1.call-start = ((), (), s32[]{:S(2)}) async-start(), calls=%async_computation.7 | async-start | bytes 5013504 | tf_op jit(solution)/shard_map/all_gather | solution.py:216
  94.0 5.9 %collective-permute-start.16 = (bf16[192,384]{1,0:T(8,128)(2,1)S(1)}, bf16[192,384]{1,0:T(8,128)(2,1)S(1)}, u32[]{:S(2)}, u32[]{:S(2)}) collective-permute-start(bf16[192,384]{1,0:T(8,128)(2,1)S(1)} %fusion.15), channel_id=1, source_target_pairs={{0,128},{1,129},{2,130},{3,131},{4,132},{5,133},{6,134},{7,135},{8... | collective-permute-start | bytes 442376 | tf_op jit(solution)/shard_map/ppermute | solution.py:30
  97.0 4.4 %collective-permute-start.17 = (bf16[192,384]{1,0:T(8,128)(2,1)S(1)}, bf16[192,384]{1,0:T(8,128)(2,1)S(1)}, u32[]{:S(2)}, u32[]{:S(2)}) collective-permute-start(bf16[192,384]{1,0:T(8,128)(2,1)S(1)} %get-tuple-element.118), channel_id=1, source_target_pairs={{0,12},{1,13},{2,14},{3,15},{4,0},{5,1},{6,2},{7,3},{8,4},{9,5},{1... | collective-permute-start | bytes 442376 | tf_op jit(solution)/shard_map/ppermute | solution.py:30
  97.1 5.7 %collective-permute-start.18 = (bf16[192,384]{1,0:T(8,128)(2,1)S(1)}, bf16[192,384]{1,0:T(8,128)(2,1)S(1)}, u32[]{:S(2)}, u32[]{:S(2)}) collective-permute-start(bf16[192,384]{1,0:T(8,128)(2,1)S(1)} %get-tuple-element.117), channel_id=1, source_target_pairs={{0,8},{1,9},{2,10},{3,11},{4,12},{5,13},{6,14},{7,15},{8,0},{9,1},... | collective-permute-start | bytes 442376 | tf_op jit(solution)/shard_map/ppermute | solution.py:30
  97.3 7.0 %collective-permute-start.19 = (bf16[192,384]{1,0:T(8,128)(2,1)S(1)}, bf16[192,384]{1,0:T(8,128)(2,1)S(1)}, u32[]{:S(2)}, u32[]{:S(2)}) collective-permute-start(bf16[192,384]{1,0:T(8,128)(2,1)S(1)} %get-tuple-element.116), channel_id=1, source_target_pairs={{0,4},{1,5},{2,6},{3,7},{4,8},{5,9},{6,10},{7,11},{8,12},{9,13},{1... | collective-permute-start | bytes 442376 | tf_op jit(solution)/shard_map/ppermute | solution.py:30
  142.5 15.4 %all-to-all-start.3 = ((bf16[8,32,768]{2,1,0:T(8,128)(2,1)}), bf16[8,32,768]{2,1,0:T(8,128)(2,1)S(1)}, u32[]{:S(2)}, u32[]{:S(2)}) async-start(bf16[8,32,768]{2,1,0:T(8,128)(2,1)} %bitcast.80), calls=%async_computation.4 | async-start | bytes 786432 | tf_op jit(solution)/shard_map/all_to_all | solution.py:219
Sparse Core Ops, SparseCore 0:
  28.9 32.8 all-gather.2
  92.7 42.2 reduce-scatter.1
  142.6 38.4 all-gather.4

commit v4 on v3

--- a/solution.py
+++ b/solution.py
@@ -148,6 +148,24 @@
     )(sums, master, update)
 
 
+def copy_kernel(source, target):
+    target[...] = source[...]
+
+
+def copied(array):
+    rows, cols = array.shape
+    some = pl.BlockSpec((rows // 6, cols), lambda i: (i, 0))
+    return pl.pallas_call(
+        copy_kernel,
+        out_shape=jax.ShapeDtypeStruct(array.shape, array.dtype),
+        grid=(6,),
+        in_specs=[some],
+        out_specs=some,
+        compiler_params=pltpu.CompilerParams(vmem_limit_bytes=16 * 1024 * 1024),
+        cost_estimate=pl.CostEstimate(flops=0, bytes_accessed=4 * array.size, transcendentals=0),
+    )(array)
+
+
 def local(layer_input, out_grad, master, moment_code, moment_scale, second_code, second_scale):
     inv_root = 1.0 / math.sqrt(FEAT_IN)
     d, t = lax.axis_index("dp"), lax.axis_index("tensor")
@@ -201,9 +219,10 @@
     across = lax.optimization_barrier((across, sends))[0]
     weights = jnp.concatenate([weights, wings[0], jnp.concatenate(across), wings[1]], axis=1)
     outs = jnp.einsum("tn,kn->tk", wide, weights, preferred_element_type=F32) * inv_root
-    outs = after(outs.astype(BF16), lower).reshape(8, 4, few, 2 * rows).transpose(1, 0, 2, 3)
+    outs = outs.astype(BF16).reshape(8, 4, few, 2 * rows).transpose(1, 0, 2, 3)
+    outs = after(outs.reshape(32 * few, 2 * rows), lower)
     summed = lax.psum_scatter(
-        outs.reshape(32 * few, 2 * rows), "tensor", scatter_dimension=0, tiled=True, axis_index_groups=LINE
+        outs, "tensor", scatter_dimension=0, tiled=True, axis_index_groups=LINE
     ).reshape(8, few, 2 * rows)
 
     update, new_moment_code, new_moment_scale, new_second_code, new_second_scale, sums = moments(
@@ -214,6 +233,7 @@
     sums = lax.all_to_all(spread, "tensor", 0, 0, tiled=True)
     new_master, new16, trust_ratio = finish(sums, master, update)
     new_weight = lax.all_gather(after(new16, summed), "dp", axis=0, tiled=True)
+    new_weight = copied(new_weight)
     trust_ratio = trust_ratio[0, 0]
 
     back = lax.all_to_all(

time: 193 us -> 193 us (level)
  Pallas kernels: 3.84 us -> 6.93 us
    pallas_call x0 -> x1, Pallas kernels: none -> 3.1 us  [copied(): pl.pallas_call(copy_kernel, out_shape=jax.ShapeDtypeStruct(array.shape, a...]
    unnamed x27 -> x26, local copies, waits for them, and re-layouts: 11.7 us -> 9.02 us
    all_to_all x1, blocking collectives: 19.3 us -> 16.9 us  [local(): sums = lax.all_to_all(spread, 'tensor', 0, 0, tiled=True)]
  transfers between devices with their start and end apart: 25 -> 25, of which waited for: 12 -> 11; matrix products, arithmetic and copies ran while one was open for 12% -> 13% of each run, Pallas kernels for 2% -> 2%
where the time goes in v4:
time: 193 us; the launch traced here: 192 us
  waiting for transfers between devices  64.7 us (34%)
  starting transfers between devices  38.2 us (20%)
  blocking collectives  33.7 us (17%)
  local copies, waits for them, and re-layouts  20.5 us (11%)
  between operations  14 us (7%)
  matrix products  9.31 us (5%)
  Pallas kernels  6.93 us (4%)
  other arithmetic  4.71 us (2%)
    ppermute x20, waiting for transfers between devices, shift(): return lax.ppermute(array, BOTH, pairs)  34.5 us
    ppermute x20, starting transfers between devices, shift(): return lax.ppermute(array, BOTH, pairs)  26.5 us
    all_gather x1, waiting for transfers between devices, local(): new_weight = lax.all_gather(after(new16, summed), 'dp', axis=0, tiled=True)  21.3 us
    all_to_all x1, blocking collectives, local(): sums = lax.all_to_all(spread, 'tensor', 0, 0, tiled=True)  16.9 us
    all_to_all x1, blocking collectives, local(): lax.all_to_all(sums, 'dp', 0, 0, tiled=True)  16.8 us
    unnamed x26, local copies, waits for them, and re-layouts  9.02 us
    all_to_all x1, waiting for transfers between devices, local(): lax.all_to_all(after(summed, sums), 'dp', 0, 0, tiled=True, axis_index_gr...  8.85 us
    all_to_all x1, starting transfers between devices, local(): mine = lax.all_to_all(mine, 'dp', 0, 0, tiled=True, axis_index_groups=NEAR)  6.6 us
  transfers between devices with their start and end apart: 25, of which 11 were waited for; matrix products, arithmetic and copies ran while one was open for 13% of the time, Pallas kernels for 2%

profile of v4, /device:TPU:1, one launch (start us, length us, event | category | flops | bytes accessed | tf_op | source)
XLA Modules:
  0.0 192.1 jit_solution(16942952419158883770)
XLA Ops:
  7.2 1.1 copy.32
  8.6 1.0 reshape.90
  9.6 6.6 %all-to-all-start = ((bf16[8,32,768]{2,1,0:T(8,128)(2,1)}), bf16[8,32,768]{2,1,0:T(8,128)(2,1)S(1)}, u32[]{:S(2)}, u32[]{:S(2)}) async-start(bf16[8,32,768]{2,1,0:T(8,128)(2,1)} %reshape.90), calls=%async_computation | async-start | bytes 786432 | tf_op jit(solution)/shard_map/all_to_all | solution.py:180
  16.2 1.1 convert_element_type.36
  17.3 1.1 collective-permute-start.3
  18.4 1.1 dynamic-slice_bitcast_fusion.1
  19.5 1.3 collective-permute-start
  20.8 2.5 %collective-permute-start.1 = (bf16[4,32,384]{2,1,0:T(8,128)(2,1)S(1)}, bf16[4,32,384]{2,1,0:T(8,128)(2,1)S(1)}, u32[]{:S(2)}, u32[]{:S(2)}) collective-permute-start(bf16[4,32,384]{2,1,0:T(8,128)(2,1)S(1)} %get-tuple-element.122), channel_id=1, source_target_pairs={{0,8},{1,9},{2,10},{3,11},{4,12},{5,13},{6,14},{7,15},{8,0},{9,1},... | collective-permute-start | bytes 294920 | tf_op jit(solution)/shard_map/ppermute | solution.py:30
  23.2 1.2 collective-permute-start.2
  24.8 3.1 %collective-permute-done.1 = bf16[4,32,384]{2,1,0:T(8,128)(2,1)S(1)} collective-permute-done((bf16[4,32,384]{2,1,0:T(8,128)(2,1)S(1)}, bf16[4,32,384]{2,1,0:T(8,128)(2,1)S(1)}, u32[]{:S(2)}, u32[]{:S(2)}) %collective-permute-start.1) | collective-permute-done | bytes 98336 | tf_op jit(solution)/shard_map/ppermute | solution.py:30
  29.6 2.1 %collective-permute-start.7 = (bf16[768,384]{1,0:T(8,128)(2,1)S(1)}, bf16[768,384]{1,0:T(8,128)(2,1)}, u32[]{:S(2)}, u32[]{:S(2)}) collective-permute-start(bf16[768,384]{1,0:T(8,128)(2,1)S(1)} %pad_maximum_fusion), channel_id=1, source_target_pairs={{0,12},{1,13},{2,14},{3,15},{4,0},{5,1},{6,2},{7,3},{8,4},{9,5},{1... | collective-permute-start | bytes 1769480 | tf_op jit(solution)/shard_map/ppermute | solution.py:30
  31.7 3.0 %collective-permute-start.4 = (bf16[8,32,768]{2,1,0:T(8,128)(2,1)S(1)}, bf16[8,32,768]{2,1,0:T(8,128)(2,1)S(1)}, u32[]{:S(2)}, u32[]{:S(2)}) collective-permute-start(bf16[8,32,768]{2,1,0:T(8,128)(2,1)S(1)} %all-to-all-done), channel_id=1, source_target_pairs={{0,1},{1,2},{2,3},{3,0},{4,5},{5,6},{6,7},{7,4},{8,9},{9,10},{10,1... | collective-permute-start | bytes 1179656 | tf_op jit(solution)/shard_map/ppermute | solution.py:30
  34.7 2.1 %collective-permute-start.5 = (bf16[8,32,768]{2,1,0:T(8,128)(2,1)S(1)}, bf16[8,32,768]{2,1,0:T(8,128)(2,1)S(1)}, u32[]{:S(2)}, u32[]{:S(2)}) collective-permute-start(bf16[8,32,768]{2,1,0:T(8,128)(2,1)S(1)} %all-to-all-done), channel_id=1, source_target_pairs={{0,3},{1,0},{2,1},{3,2},{4,7},{5,4},{6,5},{7,6},{8,11},{9,8},{10,9... | collective-permute-start | bytes 1179656 | tf_op jit(solution)/shard_map/ppermute | solution.py:30
  36.8 10.2 %collective-permute-done.4 = bf16[8,32,768]{2,1,0:T(8,128)(2,1)S(1)} collective-permute-done((bf16[8,32,768]{2,1,0:T(8,128)(2,1)S(1)}, bf16[8,32,768]{2,1,0:T(8,128)(2,1)S(1)}, u32[]{:S(2)}, u32[]{:S(2)}) %collective-permute-start.4) | collective-permute-done | bytes 393248 | tf_op jit(solution)/shard_map/ppermute | solution.py:30
  47.0 8.6 %collective-permute-done.5 = bf16[8,32,768]{2,1,0:T(8,128)(2,1)S(1)} collective-permute-done((bf16[8,32,768]{2,1,0:T(8,128)(2,1)S(1)}, bf16[8,32,768]{2,1,0:T(8,128)(2,1)S(1)}, u32[]{:S(2)}, u32[]{:S(2)}) %collective-permute-start.5) | collective-permute-done | bytes 393248 | tf_op jit(solution)/shard_map/ppermute | solution.py:30
  55.6 0.8 copy-done.6
  56.4 2.6 %collective-permute-start.10 = (bf16[4,32,768]{2,1,0:T(8,128)(2,1)S(1)}, bf16[4,32,768]{2,1,0:T(8,128)(2,1)}, u32[]{:S(2)}, u32[]{:S(2)}) collective-permute-start(bf16[4,32,768]{2,1,0:T(8,128)(2,1)S(1)} %slice.63), channel_id=1, source_target_pairs={{0,1},{1,2},{2,3},{3,0},{4,5},{5,6},{6,7},{7,4},{8,9},{9,10},{10,1... | collective-permute-start | bytes 589832 | tf_op jit(solution)/shard_map/ppermute | solution.py:30
  59.0 1.2 collective-permute-start.11
  60.2 1.0 slice.61
  61.3 1.0 slice.62
  62.3 2.9 %collective-permute-start.9 = (bf16[384,384]{1,0:T(8,128)(2,1)S(1)}, bf16[384,384]{1,0:T(8,128)(2,1)}, u32[]{:S(2)}, u32[]{:S(2)}) collective-permute-start(bf16[384,384]{1,0:T(8,128)(2,1)S(1)} %slice.62), channel_id=1, source_target_pairs={{0,12},{1,13},{2,14},{3,15},{4,0},{5,1},{6,2},{7,3},{8,4},{9,5},{1... | collective-permute-start | bytes 884744 | tf_op jit(solution)/shard_map/ppermute | solution.py:30
  65.2 2.0 %constant_dynamic-slice_fusion.2 = (bf16[8,1,32,1536]{3,2,1,0:T(8,128)(2,1)S(1)}, bf16[8,1,32,1536]{3,2,1,0:T(8,128)(2,1)S(1)}, bf16[8,1,32,1536]{3,2,1,0:T(8,128)(2,1)S(1)}) fusion(bf16[8,4,32,1536]{3,2,1,0:T(8,128)(2,1)} %bitcast.62, s32[]{:T(128)S(6)} %select_n.111, s32[]{:T(128)S(6)} %select_n.109, s32[]{:T(128)S(6)} %select_n.107), kind=kLoop, calls=%fused_computation.32 | loop fusion | bytes 4718604 | tf_op jit(solution)/shard_map/jit(dynamic_index_in_dim)/dynamic_slice | solution.py:34
  68.7 0.8 fusion.20
  69.5 0.8 fusion.22
  70.3 1.7 fusion.23
  72.0 1.3 add_multiply_fusion
  73.9 1.6 copy-done.4
  77.2 3.9 %multiply_convert_fusion = bf16[1024,768]{1,0:T(8,128)(2,1)S(1)} fusion(bf16[1024,1536]{1,0:T(8,128)(2,1)S(1)} %copy-done.5, bf16[768,384]{1,0:T(8,128)(2,1)} %collective-permute-done.7, bf16[384,384]{1,0:T(8,128)(2,1)} %collective-permute-done.9, bf16[384,384]{1,0:T(8,128)(2,1)} %collective-permute-done.8, bf16[768,384]{1,0:T(8,128)(2,1)S(1)} %copy-done.7, ...), kind=kOutput, calls=%fused_computation.1 | convolution fusion | flops 2431647744 | bytes 7077888 | tf_op jit(solution)/shard_map/tn,kn->tk/dot_general | solution.py:221
  81.1 1.3 copy.26
  83.2 6.9 %collective-permute-done.14 = bf16[2,192,384]{2,1,0:T(8,128)(2,1)S(1)} collective-permute-done((bf16[2,192,384]{2,1,0:T(8,128)(2,1)S(1)}, bf16[2,192,384]{2,1,0:T(8,128)(2,1)S(1)}, u32[]{:S(2)}, u32[]{:S(2)}) %collective-permute-start.14) | collective-permute-done | bytes 294944 | tf_op jit(solution)/shard_map/ppermute | solution.py:30
  90.1 1.2 fusion.17
  91.3 1.2 slice_add_fusion
  93.2 2.9 %collective-permute-start.16 = (bf16[192,384]{1,0:T(8,128)(2,1)}, bf16[192,384]{1,0:T(8,128)(2,1)S(1)}, u32[]{:S(2)}, u32[]{:S(2)}) collective-permute-start(bf16[192,384]{1,0:T(8,128)(2,1)} %fusion.15), channel_id=1, source_target_pairs={{0,128},{1,129},{2,130},{3,131},{4,132},{5,133},{6,134},{7,135},{8... | collective-permute-start | bytes 442376 | tf_op jit(solution)/shard_map/ppermute | solution.py:30
  97.0 1.4 collective-permute-start.19
  98.7 1.0 slice.82.lower
  99.7 1.7 collective-permute-done.17.one
  101.4 1.3 collective-permute-done.18.two
  102.7 1.5 collective-permute-done.19.three
  104.2 2.8 %shard_map.134 = (f32[384,384]{1,0:T(8,128)S(1)}, bf16[384,384]{1,0:T(8,128)(2,1)}, f32[384,3]{1,0:T(8,128)S(1)}, bf16[384,384]{1,0:T(8,128)(2,1)}, f32[384,3]{1,0:T(8,128)S(1)}, /*index=5*/f32[16,8,128]{2,1,0:T(8,128)S(1)}) custom-call(f32[192,384]{1,0:T(8,128)S(1)} %dynamic-slice_bitcast_fusion.upper, bf16[192,384]{1,0:T(8,128)(2,1)S(1)} %collective-permute-done.16.far, ...), custom_call_target="tpu_custom_call" | custom-call | flops 147456 | bytes 147456 | tf_op jit(solution)/shard_map/pallas_call | solution.py:100
  107.0 16.8 %all_to_all.20 = f32[16,8,128]{2,1,0:T(8,128)S(1)} all-to-all(f32[16,8,128]{2,1,0:T(8,128)S(1)} %get-tuple-element.71), channel_id=1, replica_groups=mesh['dp'=16,'tensor'=16] {'dp'}, dimensions={0} | all-to-all | bytes 131072 | tf_op jit(solution)/shard_map/all_to_all | solution.py:232
  123.8 16.9 %all_to_all.21.sums = f32[16,8,128]{2,1,0:T(8,128)S(1)} all-to-all(f32[16,8,128]{2,1,0:T(8,128)S(1)} %broadcast_in_dim.3), channel_id=1, replica_groups=mesh['dp'=16,'tensor'=16] {'tensor'}, dimensions={0} | all-to-all | bytes 131072 | tf_op jit(solution)/shard_map/all_to_all | solution.py:233
  140.7 1.0 shard_map.135
  141.8 5.0 %all-to-all-start.3 = ((bf16[8,32,768]{2,1,0:T(8,128)(2,1)}), bf16[8,32,768]{2,1,0:T(8,128)(2,1)S(1)}, u32[]{:S(2)}, u32[]{:S(2)}) async-start(bf16[8,32,768]{2,1,0:T(8,128)(2,1)} %bitcast.80), calls=%async_computation.4 | async-start | bytes 786432 | tf_op jit(solution)/shard_map/all_to_all | solution.py:239
  148.7 8.8 %all-to-all-done.3 = bf16[8,32,768]{2,1,0:T(8,128)(2,1)S(1)} async-done(((bf16[8,32,768]{2,1,0:T(8,128)(2,1)}), bf16[8,32,768]{2,1,0:T(8,128)(2,1)S(1)}, u32[]{:S(2)}, u32[]{:S(2)}) %all-to-all-start.3) | async-done | bytes 393248 | tf_op jit(solution)/shard_map/all_to_all | solution.py:239
  158.0 0.8 copy.33
  158.8 21.3 %all-gather.5.cloned.1.call-done.source = bf16[6144,384]{1,0:T(8,128)(2,1)} async-done(((bf16[384,384]{1,0:T(8,128)(2,1)}), bf16[6144,384]{1,0:T(8,128)(2,1)}) %all-gather.5.cloned.1.call-update) | async-done | bytes 4718608 | tf_op jit(solution)/shard_map/all_gather | solution.py:235
  180.1 2.3 %copy-done.1 = bf16[6144,384]{1,0:T(8,128)(2,1)S(1)} copy-done((bf16[6144,384]{1,0:T(8,128)(2,1)S(1)}, bf16[6144,384]{1,0:T(8,128)(2,1)}, u32[]{:S(2)}) %copy-start.1) | copy-done | bytes 4718616
  182.5 3.1 %shard_map.136 = bf16[6144,384]{1,0:T(8,128)(2,1)} custom-call(bf16[6144,384]{1,0:T(8,128)(2,1)S(1)} %copy-done.1), custom_call_target="tpu_custom_call" | custom-call | bytes 9437184 | tf_op jit(solution)/shard_map/pallas_call | solution.py:158
  (71 shorter events, 11.2 us)
Async XLA Ops:
  7.2 21.6 %copy-start = (f32[384,384]{1,0:T(8,128)S(1)}, f32[384,384]{1,0:T(8,128)}, u32[]{:S(2)}) copy-start(f32[384,384]{1,0:T(8,128)} %master.3) | copy-start | bytes 1769476
  9.6 18.3 %all-to-all-start = ((bf16[8,32,768]{2,1,0:T(8,128)(2,1)}), bf16[8,32,768]{2,1,0:T(8,128)(2,1)S(1)}, u32[]{:S(2)}, u32[]{:S(2)}) async-start(bf16[8,32,768]{2,1,0:T(8,128)(2,1)} %reshape.90), calls=%async_computation | async-start | bytes 786432 | tf_op jit(solution)/shard_map/all_to_all | solution.py:180
  16.2 49.0 %all-gather.3.cloned.1.call-start = ((), (), s32[]{:S(2)}) async-start(), calls=%async_computation.5 | async-start | bytes 3538944 | tf_op jit(solution)/shard_map/all_gather | solution.py:192
  17.3 10.6 %collective-permute-start.3 = (bf16[384,384]{1,0:T(8,128)(2,1)S(1)}, bf16[384,384]{1,0:T(8,128)(2,1)S(1)}, u32[]{:S(2)}, u32[]{:S(2)}) collective-permute-start(bf16[384,384]{1,0:T(8,128)(2,1)S(1)} %convert_element_type.36), channel_id=1, source_target_pairs={{0,128},{1,129},{2,130},{3,131},{4,132},{5,133},{6,134},{7,135},{8... | collective-permute-start | bytes 884744 | tf_op jit(solution)/shard_map/ppermute | solution.py:30
  19.5 5.3 %collective-permute-start = (bf16[4,32,384]{2,1,0:T(8,128)(2,1)S(1)}, bf16[4,32,384]{2,1,0:T(8,128)(2,1)S(1)}, u32[]{:S(2)}, u32[]{:S(2)}) collective-permute-start(bf16[4,32,384]{2,1,0:T(8,128)(2,1)S(1)} %get-tuple-element.123), channel_id=1, source_target_pairs={{0,4},{1,5},{2,6},{3,7},{4,8},{5,9},{6,10},{7,11},{8,12},{9,13},{1... | collective-permute-start | bytes 294920 | tf_op jit(solution)/shard_map/ppermute | solution.py:30
  20.8 7.1 %collective-permute-start.1 = (bf16[4,32,384]{2,1,0:T(8,128)(2,1)S(1)}, bf16[4,32,384]{2,1,0:T(8,128)(2,1)S(1)}, u32[]{:S(2)}, u32[]{:S(2)}) collective-permute-start(bf16[4,32,384]{2,1,0:T(8,128)(2,1)S(1)} %get-tuple-element.122), channel_id=1, source_target_pairs={{0,8},{1,9},{2,10},{3,11},{4,12},{5,13},{6,14},{7,15},{8,0},{9,1},... | collective-permute-start | bytes 294920 | tf_op jit(solution)/shard_map/ppermute | solution.py:30
  23.2 4.7 %collective-permute-start.2 = (bf16[4,32,384]{2,1,0:T(8,128)(2,1)S(1)}, bf16[4,32,384]{2,1,0:T(8,128)(2,1)S(1)}, u32[]{:S(2)}, u32[]{:S(2)}) collective-permute-start(bf16[4,32,384]{2,1,0:T(8,128)(2,1)S(1)} %get-tuple-element.121), channel_id=1, source_target_pairs={{0,12},{1,13},{2,14},{3,15},{4,0},{5,1},{6,2},{7,3},{8,4},{9,5},{1... | collective-permute-start | bytes 294920 | tf_op jit(solution)/shard_map/ppermute | solution.py:30
  28.7 113.0 %reduce-scatter.2.cloned.1.call-start = ((), (), s32[]{:S(2)}) async-start(), calls=%async_computation.6 | async-start | bytes 1966080 | tf_op jit(solution)/shard_map/reduce_scatter | solution.py:224
  29.0 26.6 %collective-permute-start.6 = (bf16[768,384]{1,0:T(8,128)(2,1)S(1)}, bf16[768,384]{1,0:T(8,128)(2,1)S(1)}, u32[]{:S(2)}, u32[]{:S(2)}) collective-permute-start(bf16[768,384]{1,0:T(8,128)(2,1)S(1)} %pad_maximum_fusion), channel_id=1, source_target_pairs={{0,4},{1,5},{2,6},{3,7},{4,8},{5,9},{6,10},{7,11},{8,12},{9,13},{1... | collective-permute-start | bytes 1769480 | tf_op jit(solution)/shard_map/ppermute | solution.py:30
  29.6 26.9 %collective-permute-start.7 = (bf16[768,384]{1,0:T(8,128)(2,1)S(1)}, bf16[768,384]{1,0:T(8,128)(2,1)}, u32[]{:S(2)}, u32[]{:S(2)}) collective-permute-start(bf16[768,384]{1,0:T(8,128)(2,1)S(1)} %pad_maximum_fusion), channel_id=1, source_target_pairs={{0,12},{1,13},{2,14},{3,15},{4,0},{5,1},{6,2},{7,3},{8,4},{9,5},{1... | collective-permute-start | bytes 1769480 | tf_op jit(solution)/shard_map/ppermute | solution.py:30
  31.7 15.3 %collective-permute-start.4 = (bf16[8,32,768]{2,1,0:T(8,128)(2,1)S(1)}, bf16[8,32,768]{2,1,0:T(8,128)(2,1)S(1)}, u32[]{:S(2)}, u32[]{:S(2)}) collective-permute-start(bf16[8,32,768]{2,1,0:T(8,128)(2,1)S(1)} %all-to-all-done), channel_id=1, source_target_pairs={{0,1},{1,2},{2,3},{3,0},{4,5},{5,6},{6,7},{7,4},{8,9},{9,10},{10,1... | collective-permute-start | bytes 1179656 | tf_op jit(solution)/shard_map/ppermute | solution.py:30
  34.7 20.9 %collective-permute-start.5 = (bf16[8,32,768]{2,1,0:T(8,128)(2,1)S(1)}, bf16[8,32,768]{2,1,0:T(8,128)(2,1)S(1)}, u32[]{:S(2)}, u32[]{:S(2)}) collective-permute-start(bf16[8,32,768]{2,1,0:T(8,128)(2,1)S(1)} %all-to-all-done), channel_id=1, source_target_pairs={{0,3},{1,0},{2,1},{3,2},{4,7},{5,4},{6,5},{7,6},{8,11},{9,8},{10,9... | collective-permute-start | bytes 1179656 | tf_op jit(solution)/shard_map/ppermute | solution.py:30
  55.6 0.8 copy-start.6
  56.4 11.4 %collective-permute-start.10 = (bf16[4,32,768]{2,1,0:T(8,128)(2,1)S(1)}, bf16[4,32,768]{2,1,0:T(8,128)(2,1)}, u32[]{:S(2)}, u32[]{:S(2)}) collective-permute-start(bf16[4,32,768]{2,1,0:T(8,128)(2,1)S(1)} %slice.63), channel_id=1, source_target_pairs={{0,1},{1,2},{2,3},{3,0},{4,5},{5,6},{6,7},{7,4},{8,9},{9,10},{10,1... | collective-permute-start | bytes 589832 | tf_op jit(solution)/shard_map/ppermute | solution.py:30
  59.0 8.9 %collective-permute-start.11 = (bf16[4,32,768]{2,1,0:T(8,128)(2,1)S(1)}, bf16[4,32,768]{2,1,0:T(8,128)(2,1)S(1)}, u32[]{:S(2)}, u32[]{:S(2)}) collective-permute-start(bf16[4,32,768]{2,1,0:T(8,128)(2,1)S(1)} %slice.64), channel_id=1, source_target_pairs={{0,3},{1,0},{2,1},{3,2},{4,7},{5,4},{6,5},{7,6},{8,11},{9,8},{10,9... | collective-permute-start | bytes 589832 | tf_op jit(solution)/shard_map/ppermute | solution.py:30
  61.2 15.4 %collective-permute-start.8 = (bf16[384,384]{1,0:T(8,128)(2,1)S(1)}, bf16[384,384]{1,0:T(8,128)(2,1)}, u32[]{:S(2)}, u32[]{:S(2)}) collective-permute-start(bf16[384,384]{1,0:T(8,128)(2,1)S(1)} %slice.61), channel_id=1, source_target_pairs={{0,4},{1,5},{2,6},{3,7},{4,8},{5,9},{6,10},{7,11},{8,12},{9,13},{1... | collective-permute-start | bytes 884744 | tf_op jit(solution)/shard_map/ppermute | solution.py:30
  62.3 14.9 %collective-permute-start.9 = (bf16[384,384]{1,0:T(8,128)(2,1)S(1)}, bf16[384,384]{1,0:T(8,128)(2,1)}, u32[]{:S(2)}, u32[]{:S(2)}) collective-permute-start(bf16[384,384]{1,0:T(8,128)(2,1)S(1)} %slice.62), channel_id=1, source_target_pairs={{0,12},{1,13},{2,14},{3,15},{4,0},{5,1},{6,2},{7,3},{8,4},{9,5},{1... | collective-permute-start | bytes 884744 | tf_op jit(solution)/shard_map/ppermute | solution.py:30
  65.2 2.6 %copy-start.5 = (bf16[1024,1536]{1,0:T(8,128)(2,1)S(1)}, bf16[1024,1536]{1,0:T(8,128)(2,1)}, u32[]{:S(2)}) copy-start(bf16[1024,1536]{1,0:T(8,128)(2,1)} %all-gather.3.cloned.1.call-done) | copy-start | bytes 9437188
  73.4 2.2 %copy-start.4 = (f32[768,1536]{1,0:T(8,128)}, f32[768,1536]{1,0:T(8,128)S(1)}, u32[]{:S(2)}) copy-start(f32[768,1536]{1,0:T(8,128)S(1)} %add_multiply_fusion) | copy-start | bytes 14155780
  73.6 3.6 %copy-start.7 = (bf16[768,384]{1,0:T(8,128)(2,1)S(1)}, bf16[768,384]{1,0:T(8,128)(2,1)}, u32[]{:S(2)}) copy-start(bf16[768,384]{1,0:T(8,128)(2,1)} %copy-done.6) | copy-start | bytes 1769476
  75.6 14.5 %collective-permute-start.15 = (bf16[192,1536]{1,0:T(8,128)(2,1)S(1)}, bf16[192,1536]{1,0:T(8,128)(2,1)S(1)}, u32[]{:S(2)}, u32[]{:S(2)}) collective-permute-start(bf16[192,1536]{1,0:T(8,128)(2,1)S(1)} %fusion.14), channel_id=1, source_target_pairs={{0,128},{1,129},{2,130},{3,131},{4,132},{5,133},{6,134},{7,135},{8... | collective-permute-start | bytes 1769480 | tf_op jit(solution)/shard_map/ppermute | solution.py:30
  75.7 6.7 %collective-permute-start.12 = (bf16[2,192,384]{2,1,0:T(8,128)(2,1)S(1)}, bf16[2,192,384]{2,1,0:T(8,128)(2,1)S(1)}, u32[]{:S(2)}, u32[]{:S(2)}) collective-permute-start(bf16[2,192,384]{2,1,0:T(8,128)(2,1)S(1)} %get-tuple-element.115), channel_id=1, source_target_pairs={{0,12},{1,13},{2,14},{3,15},{4,0},{5,1},{6,2},{7,3},{8,4},{9,5},{1... | collective-permute-start | bytes 884744 | tf_op jit(solution)/shard_map/ppermute | solution.py:30
  76.0 7.2 %collective-permute-start.13 = (bf16[2,192,384]{2,1,0:T(8,128)(2,1)S(1)}, bf16[2,192,384]{2,1,0:T(8,128)(2,1)S(1)}, u32[]{:S(2)}, u32[]{:S(2)}) collective-permute-start(bf16[2,192,384]{2,1,0:T(8,128)(2,1)S(1)} %get-tuple-element.114), channel_id=1, source_target_pairs={{0,8},{1,9},{2,10},{3,11},{4,12},{5,13},{6,14},{7,15},{8,0},{9,1},... | collective-permute-start | bytes 884744 | tf_op jit(solution)/shard_map/ppermute | solution.py:30
  76.6 13.5 %collective-permute-start.14 = (bf16[2,192,384]{2,1,0:T(8,128)(2,1)S(1)}, bf16[2,192,384]{2,1,0:T(8,128)(2,1)S(1)}, u32[]{:S(2)}, u32[]{:S(2)}) collective-permute-start(bf16[2,192,384]{2,1,0:T(8,128)(2,1)S(1)} %get-tuple-element.113), channel_id=1, source_target_pairs={{0,4},{1,5},{2,6},{3,7},{4,8},{5,9},{6,10},{7,11},{8,12},{9,13},{1... | collective-permute-start | bytes 884744 | tf_op jit(solution)/shard_map/ppermute | solution.py:30
  82.4 16.0 %copy-start.8 = (f32[384,3]{0,1:T(4,128)S(1)}, f32[384,3]{0,1:T(4,128)}, u32[]{:S(2)}) copy-start(f32[384,3]{0,1:T(4,128)} %param.11) | copy-start | bytes 13828
  82.4 16.1 %copy-start.9 = (f32[384,3]{0,1:T(4,128)S(1)}, f32[384,3]{0,1:T(4,128)}, u32[]{:S(2)}) copy-start(f32[384,3]{0,1:T(4,128)} %param.13) | copy-start | bytes 13828
  82.4 21.8 %copy-start.2 = (bf16[384,384]{1,0:T(8,128)(2,1)S(1)}, bf16[384,384]{1,0:T(8,128)(2,1)}, u32[]{:S(2)}) copy-start(bf16[384,384]{1,0:T(8,128)(2,1)} %mcode.1) | copy-start | bytes 884740
  82.4 21.8 %copy-start.3 = (bf16[384,384]{1,0:T(8,128)(2,1)S(1)}, bf16[384,384]{1,0:T(8,128)(2,1)}, u32[]{:S(2)}) copy-start(bf16[384,384]{1,0:T(8,128)(2,1)} %scode.1) | copy-start | bytes 884740
  91.3 88.8 %all-gather.5.cloned.1.call-start = ((), (), s32[]{:S(2)}) async-start(), calls=%async_computation.7 | async-start | bytes 5013504 | tf_op jit(solution)/shard_map/all_gather | solution.py:235
  93.2 6.5 %collective-permute-start.16 = (bf16[192,384]{1,0:T(8,128)(2,1)}, bf16[192,384]{1,0:T(8,128)(2,1)S(1)}, u32[]{:S(2)}, u32[]{:S(2)}) collective-permute-start(bf16[192,384]{1,0:T(8,128)(2,1)} %fusion.15), channel_id=1, source_target_pairs={{0,128},{1,129},{2,130},{3,131},{4,132},{5,133},{6,134},{7,135},{8... | collective-permute-start | bytes 442376 | tf_op jit(solution)/shard_map/ppermute | solution.py:30
  96.9 4.5 %collective-permute-start.17 = (bf16[192,384]{1,0:T(8,128)(2,1)}, bf16[192,384]{1,0:T(8,128)(2,1)S(1)}, u32[]{:S(2)}, u32[]{:S(2)}) collective-permute-start(bf16[192,384]{1,0:T(8,128)(2,1)} %get-tuple-element.118), channel_id=1, source_target_pairs={{0,12},{1,13},{2,14},{3,15},{4,0},{5,1},{6,2},{7,3},{8,4},{9,5},{1... | collective-permute-start | bytes 442376 | tf_op jit(solution)/shard_map/ppermute | solution.py:30
  96.9 5.8 %collective-permute-start.18 = (bf16[192,384]{1,0:T(8,128)(2,1)}, bf16[192,384]{1,0:T(8,128)(2,1)S(1)}, u32[]{:S(2)}, u32[]{:S(2)}) collective-permute-start(bf16[192,384]{1,0:T(8,128)(2,1)} %get-tuple-element.117), channel_id=1, source_target_pairs={{0,8},{1,9},{2,10},{3,11},{4,12},{5,13},{6,14},{7,15},{8,0},{9,1},... | collective-permute-start | bytes 442376 | tf_op jit(solution)/shard_map/ppermute | solution.py:30
  97.0 7.2 %collective-permute-start.19 = (bf16[192,384]{1,0:T(8,128)(2,1)S(1)}, bf16[192,384]{1,0:T(8,128)(2,1)S(1)}, u32[]{:S(2)}, u32[]{:S(2)}) collective-permute-start(bf16[192,384]{1,0:T(8,128)(2,1)S(1)} %get-tuple-element.116), channel_id=1, source_target_pairs={{0,4},{1,5},{2,6},{3,7},{4,8},{5,9},{6,10},{7,11},{8,12},{9,13},{1... | collective-permute-start | bytes 442376 | tf_op jit(solution)/shard_map/ppermute | solution.py:30
  141.8 15.7 %all-to-all-start.3 = ((bf16[8,32,768]{2,1,0:T(8,128)(2,1)}), bf16[8,32,768]{2,1,0:T(8,128)(2,1)S(1)}, u32[]{:S(2)}, u32[]{:S(2)}) async-start(bf16[8,32,768]{2,1,0:T(8,128)(2,1)} %bitcast.80), calls=%async_computation.4 | async-start | bytes 786432 | tf_op jit(solution)/shard_map/all_to_all | solution.py:239
  180.1 2.3 %copy-start.1 = (bf16[6144,384]{1,0:T(8,128)(2,1)S(1)}, bf16[6144,384]{1,0:T(8,128)(2,1)}, u32[]{:S(2)}) copy-start(bf16[6144,384]{1,0:T(8,128)(2,1)} %all-gather.5.cloned.1.call-done.source) | copy-start | bytes 14155780
Sparse Core Ops, SparseCore 0:
  28.9 32.8 all-gather.2
  91.4 42.5 reduce-scatter.1
  141.9 38.1 all-gather.4

commit v5 on v4

--- a/solution.py
+++ b/solution.py
@@ -161,7 +161,7 @@
         grid=(6,),
         in_specs=[some],
         out_specs=some,
-        compiler_params=pltpu.CompilerParams(vmem_limit_bytes=16 * 1024 * 1024),
+        compiler_params=pltpu.CompilerParams(vmem_limit_bytes=60 * 1024 * 1024),
         cost_estimate=pl.CostEstimate(flops=0, bytes_accessed=4 * array.size, transcendentals=0),
     )(array)
 

time: 193 us -> 193 us (level)
  Pallas kernels: 6.93 us -> 9.87 us
  local copies, waits for them, and re-layouts: 20.5 us -> 18.2 us
    pallas_call x1, Pallas kernels: 3.1 us -> 6.03 us  [copied(): pl.pallas_call(copy_kernel, out_shape=jax.ShapeDtypeStruct(array.shape, a...]
    unnamed x26 -> x24, local copies, waits for them, and re-layouts: 9.02 us -> 6.68 us
where the time goes in v5:
time: 193 us
  waiting for transfers between devices  64.7 us (34%)
  starting transfers between devices  38.2 us (20%)
  blocking collectives  33.7 us (17%)
  local copies, waits for them, and re-layouts  18.2 us (9%)
  between operations  14 us (7%)
  Pallas kernels  9.87 us (5%)
  matrix products  9.31 us (5%)
  other arithmetic  4.71 us (2%)
    ppermute x20, waiting for transfers between devices, shift(): return lax.ppermute(array, BOTH, pairs)  34.5 us
    ppermute x20, starting transfers between devices, shift(): return lax.ppermute(array, BOTH, pairs)  26.5 us
    all_gather x1, waiting for transfers between devices, local(): new_weight = lax.all_gather(after(new16, summed), 'dp', axis=0, tiled=True)  21.3 us
    all_to_all x1, blocking collectives, local(): sums = lax.all_to_all(spread, 'tensor', 0, 0, tiled=True)  16.9 us
    all_to_all x1, blocking collectives, local(): lax.all_to_all(sums, 'dp', 0, 0, tiled=True)  16.8 us
    all_to_all x1, waiting for transfers between devices, local(): lax.all_to_all(after(summed, sums), 'dp', 0, 0, tiled=True, axis_index_gr...  8.85 us
    unnamed x24, local copies, waits for them, and re-layouts  6.68 us
    all_to_all x1, starting transfers between devices, local(): mine = lax.all_to_all(mine, 'dp', 0, 0, tiled=True, axis_index_groups=NEAR)  6.6 us
  transfers between devices with their start and end apart: 25, of which 11 were waited for; matrix products, arithmetic and copies ran while one was open for 13% of the time, Pallas kernels for 2%

profile of v5, /device:TPU:1, one launch (start us, length us, event | category | flops | bytes accessed | tf_op | source)
XLA Modules:
  0.0 192.7 jit_solution(4272299617934751384)
XLA Ops:
  7.2 1.1 copy.32
  8.6 1.0 reshape.90
  9.6 6.6 %all-to-all-start = ((bf16[8,32,768]{2,1,0:T(8,128)(2,1)}), bf16[8,32,768]{2,1,0:T(8,128)(2,1)S(1)}, u32[]{:S(2)}, u32[]{:S(2)}) async-start(bf16[8,32,768]{2,1,0:T(8,128)(2,1)} %reshape.90), calls=%async_computation | async-start | bytes 786432 | tf_op jit(solution)/shard_map/all_to_all | solution.py:180
  16.2 1.1 convert_element_type.36
  17.3 1.1 collective-permute-start.3
  18.4 1.1 dynamic-slice_bitcast_fusion.1
  19.5 1.3 collective-permute-start
  20.8 2.5 %collective-permute-start.1 = (bf16[4,32,384]{2,1,0:T(8,128)(2,1)S(1)}, bf16[4,32,384]{2,1,0:T(8,128)(2,1)S(1)}, u32[]{:S(2)}, u32[]{:S(2)}) collective-permute-start(bf16[4,32,384]{2,1,0:T(8,128)(2,1)S(1)} %get-tuple-element.122), channel_id=1, source_target_pairs={{0,8},{1,9},{2,10},{3,11},{4,12},{5,13},{6,14},{7,15},{8,0},{9,1},... | collective-permute-start | bytes 294920 | tf_op jit(solution)/shard_map/ppermute | solution.py:30
  23.2 1.2 collective-permute-start.2
  24.8 3.1 %collective-permute-done.1 = bf16[4,32,384]{2,1,0:T(8,128)(2,1)S(1)} collective-permute-done((bf16[4,32,384]{2,1,0:T(8,128)(2,1)S(1)}, bf16[4,32,384]{2,1,0:T(8,128)(2,1)S(1)}, u32[]{:S(2)}, u32[]{:S(2)}) %collective-permute-start.1) | collective-permute-done | bytes 98336 | tf_op jit(solution)/shard_map/ppermute | solution.py:30
  29.6 2.1 %collective-permute-start.7 = (bf16[768,384]{1,0:T(8,128)(2,1)S(1)}, bf16[768,384]{1,0:T(8,128)(2,1)}, u32[]{:S(2)}, u32[]{:S(2)}) collective-permute-start(bf16[768,384]{1,0:T(8,128)(2,1)S(1)} %pad_maximum_fusion), channel_id=1, source_target_pairs={{0,12},{1,13},{2,14},{3,15},{4,0},{5,1},{6,2},{7,3},{8,4},{9,5},{1... | collective-permute-start | bytes 1769480 | tf_op jit(solution)/shard_map/ppermute | solution.py:30
  31.7 3.0 %collective-permute-start.4 = (bf16[8,32,768]{2,1,0:T(8,128)(2,1)S(1)}, bf16[8,32,768]{2,1,0:T(8,128)(2,1)S(1)}, u32[]{:S(2)}, u32[]{:S(2)}) collective-permute-start(bf16[8,32,768]{2,1,0:T(8,128)(2,1)S(1)} %all-to-all-done), channel_id=1, source_target_pairs={{0,1},{1,2},{2,3},{3,0},{4,5},{5,6},{6,7},{7,4},{8,9},{9,10},{10,1... | collective-permute-start | bytes 1179656 | tf_op jit(solution)/shard_map/ppermute | solution.py:30
  34.7 2.1 %collective-permute-start.5 = (bf16[8,32,768]{2,1,0:T(8,128)(2,1)S(1)}, bf16[8,32,768]{2,1,0:T(8,128)(2,1)S(1)}, u32[]{:S(2)}, u32[]{:S(2)}) collective-permute-start(bf16[8,32,768]{2,1,0:T(8,128)(2,1)S(1)} %all-to-all-done), channel_id=1, source_target_pairs={{0,3},{1,0},{2,1},{3,2},{4,7},{5,4},{6,5},{7,6},{8,11},{9,8},{10,9... | collective-permute-start | bytes 1179656 | tf_op jit(solution)/shard_map/ppermute | solution.py:30
  36.8 10.2 %collective-permute-done.4 = bf16[8,32,768]{2,1,0:T(8,128)(2,1)S(1)} collective-permute-done((bf16[8,32,768]{2,1,0:T(8,128)(2,1)S(1)}, bf16[8,32,768]{2,1,0:T(8,128)(2,1)S(1)}, u32[]{:S(2)}, u32[]{:S(2)}) %collective-permute-start.4) | collective-permute-done | bytes 393248 | tf_op jit(solution)/shard_map/ppermute | solution.py:30
  47.0 8.6 %collective-permute-done.5 = bf16[8,32,768]{2,1,0:T(8,128)(2,1)S(1)} collective-permute-done((bf16[8,32,768]{2,1,0:T(8,128)(2,1)S(1)}, bf16[8,32,768]{2,1,0:T(8,128)(2,1)S(1)}, u32[]{:S(2)}, u32[]{:S(2)}) %collective-permute-start.5) | collective-permute-done | bytes 393248 | tf_op jit(solution)/shard_map/ppermute | solution.py:30
  55.6 0.8 copy-done.5
  56.4 2.6 %collective-permute-start.10 = (bf16[4,32,768]{2,1,0:T(8,128)(2,1)S(1)}, bf16[4,32,768]{2,1,0:T(8,128)(2,1)}, u32[]{:S(2)}, u32[]{:S(2)}) collective-permute-start(bf16[4,32,768]{2,1,0:T(8,128)(2,1)S(1)} %slice.63), channel_id=1, source_target_pairs={{0,1},{1,2},{2,3},{3,0},{4,5},{5,6},{6,7},{7,4},{8,9},{9,10},{10,1... | collective-permute-start | bytes 589832 | tf_op jit(solution)/shard_map/ppermute | solution.py:30
  59.0 1.2 collective-permute-start.11
  60.2 1.0 slice.61
  61.3 1.0 slice.62
  62.3 2.9 %collective-permute-start.9 = (bf16[384,384]{1,0:T(8,128)(2,1)S(1)}, bf16[384,384]{1,0:T(8,128)(2,1)}, u32[]{:S(2)}, u32[]{:S(2)}) collective-permute-start(bf16[384,384]{1,0:T(8,128)(2,1)S(1)} %slice.62), channel_id=1, source_target_pairs={{0,12},{1,13},{2,14},{3,15},{4,0},{5,1},{6,2},{7,3},{8,4},{9,5},{1... | collective-permute-start | bytes 884744 | tf_op jit(solution)/shard_map/ppermute | solution.py:30
  65.2 2.0 %constant_dynamic-slice_fusion.2 = (bf16[8,1,32,1536]{3,2,1,0:T(8,128)(2,1)S(1)}, bf16[8,1,32,1536]{3,2,1,0:T(8,128)(2,1)S(1)}, bf16[8,1,32,1536]{3,2,1,0:T(8,128)(2,1)S(1)}) fusion(bf16[8,4,32,1536]{3,2,1,0:T(8,128)(2,1)} %bitcast.62, s32[]{:T(128)S(6)} %select_n.111, s32[]{:T(128)S(6)} %select_n.109, s32[]{:T(128)S(6)} %select_n.107), kind=kLoop, calls=%fused_computation.32 | loop fusion | bytes 4718604 | tf_op jit(solution)/shard_map/jit(dynamic_index_in_dim)/dynamic_slice | solution.py:34
  67.9 0.8 fusion.21
  68.7 0.8 fusion.20
  69.5 0.8 fusion.22
  70.3 1.7 fusion.23
  72.0 1.3 add_multiply_fusion
  73.9 1.6 copy-done.3
  77.2 3.9 %multiply_convert_fusion = bf16[1024,768]{1,0:T(8,128)(2,1)S(1)} fusion(bf16[1024,1536]{1,0:T(8,128)(2,1)S(1)} %copy-done.4, bf16[768,384]{1,0:T(8,128)(2,1)} %collective-permute-done.7, bf16[384,384]{1,0:T(8,128)(2,1)} %collective-permute-done.9, bf16[384,384]{1,0:T(8,128)(2,1)} %collective-permute-done.8, bf16[768,384]{1,0:T(8,128)(2,1)S(1)} %copy-done.6, ...), kind=kOutput, calls=%fused_computation.1 | convolution fusion | flops 2431647744 | bytes 7077888 | tf_op jit(solution)/shard_map/tn,kn->tk/dot_general | solution.py:221
  81.1 1.3 copy.26
  83.2 6.9 %collective-permute-done.14 = bf16[2,192,384]{2,1,0:T(8,128)(2,1)S(1)} collective-permute-done((bf16[2,192,384]{2,1,0:T(8,128)(2,1)S(1)}, bf16[2,192,384]{2,1,0:T(8,128)(2,1)S(1)}, u32[]{:S(2)}, u32[]{:S(2)}) %collective-permute-start.14) | collective-permute-done | bytes 294944 | tf_op jit(solution)/shard_map/ppermute | solution.py:30
  90.1 1.2 fusion.17
  91.3 1.2 slice_add_fusion
  93.2 2.9 %collective-permute-start.16 = (bf16[192,384]{1,0:T(8,128)(2,1)}, bf16[192,384]{1,0:T(8,128)(2,1)S(1)}, u32[]{:S(2)}, u32[]{:S(2)}) collective-permute-start(bf16[192,384]{1,0:T(8,128)(2,1)} %fusion.15), channel_id=1, source_target_pairs={{0,128},{1,129},{2,130},{3,131},{4,132},{5,133},{6,134},{7,135},{8... | collective-permute-start | bytes 442376 | tf_op jit(solution)/shard_map/ppermute | solution.py:30
  97.0 1.4 collective-permute-start.19
  98.6 1.0 slice.82.lower
  99.7 1.7 collective-permute-done.17.one
  101.4 1.3 collective-permute-done.18.two
  102.7 1.5 collective-permute-done.19.three
  104.2 2.8 %shard_map.134 = (f32[384,384]{1,0:T(8,128)S(1)}, bf16[384,384]{1,0:T(8,128)(2,1)}, f32[384,3]{1,0:T(8,128)S(1)}, bf16[384,384]{1,0:T(8,128)(2,1)}, f32[384,3]{1,0:T(8,128)S(1)}, /*index=5*/f32[16,8,128]{2,1,0:T(8,128)S(1)}) custom-call(f32[192,384]{1,0:T(8,128)S(1)} %dynamic-slice_bitcast_fusion.upper, bf16[192,384]{1,0:T(8,128)(2,1)S(1)} %collective-permute-done.16.far, ...), custom_call_target="tpu_custom_call" | custom-call | flops 147456 | bytes 147456 | tf_op jit(solution)/shard_map/pallas_call | solution.py:100
  107.0 16.8 %all_to_all.20 = f32[16,8,128]{2,1,0:T(8,128)S(1)} all-to-all(f32[16,8,128]{2,1,0:T(8,128)S(1)} %get-tuple-element.71), channel_id=1, replica_groups=mesh['dp'=16,'tensor'=16] {'dp'}, dimensions={0} | all-to-all | bytes 131072 | tf_op jit(solution)/shard_map/all_to_all | solution.py:232
  123.8 16.9 %all_to_all.21.sums = f32[16,8,128]{2,1,0:T(8,128)S(1)} all-to-all(f32[16,8,128]{2,1,0:T(8,128)S(1)} %broadcast_in_dim.3), channel_id=1, replica_groups=mesh['dp'=16,'tensor'=16] {'tensor'}, dimensions={0} | all-to-all | bytes 131072 | tf_op jit(solution)/shard_map/all_to_all | solution.py:233
  140.7 1.0 shard_map.135
  141.8 5.0 %all-to-all-start.3 = ((bf16[8,32,768]{2,1,0:T(8,128)(2,1)}), bf16[8,32,768]{2,1,0:T(8,128)(2,1)S(1)}, u32[]{:S(2)}, u32[]{:S(2)}) async-start(bf16[8,32,768]{2,1,0:T(8,128)(2,1)} %bitcast.80), calls=%async_computation.4 | async-start | bytes 786432 | tf_op jit(solution)/shard_map/all_to_all | solution.py:239
  148.6 8.8 %all-to-all-done.3 = bf16[8,32,768]{2,1,0:T(8,128)(2,1)S(1)} async-done(((bf16[8,32,768]{2,1,0:T(8,128)(2,1)}), bf16[8,32,768]{2,1,0:T(8,128)(2,1)S(1)}, u32[]{:S(2)}, u32[]{:S(2)}) %all-to-all-start.3) | async-done | bytes 393248 | tf_op jit(solution)/shard_map/all_to_all | solution.py:239
  158.0 0.8 copy.33
  158.8 21.3 %all-gather.5.cloned.1.call-done.source = bf16[6144,384]{1,0:T(8,128)(2,1)} async-done(((bf16[384,384]{1,0:T(8,128)(2,1)}), bf16[6144,384]{1,0:T(8,128)(2,1)}) %all-gather.5.cloned.1.call-update) | async-done | bytes 4718608 | tf_op jit(solution)/shard_map/all_gather | solution.py:235
  180.1 6.0 %shard_map.136 = bf16[6144,384]{1,0:T(8,128)(2,1)} custom-call(bf16[6144,384]{1,0:T(8,128)(2,1)} %all-gather.5.cloned.1.call-done.source), custom_call_target="tpu_custom_call" | custom-call | bytes 9437184 | tf_op jit(solution)/shard_map/pallas_call | solution.py:158
  (69 shorter events, 10.5 us)
Async XLA Ops:
  7.2 21.6 %copy-start = (f32[384,384]{1,0:T(8,128)S(1)}, f32[384,384]{1,0:T(8,128)}, u32[]{:S(2)}) copy-start(f32[384,384]{1,0:T(8,128)} %master.3) | copy-start | bytes 1769476
  9.6 18.3 %all-to-all-start = ((bf16[8,32,768]{2,1,0:T(8,128)(2,1)}), bf16[8,32,768]{2,1,0:T(8,128)(2,1)S(1)}, u32[]{:S(2)}, u32[]{:S(2)}) async-start(bf16[8,32,768]{2,1,0:T(8,128)(2,1)} %reshape.90), calls=%async_computation | async-start | bytes 786432 | tf_op jit(solution)/shard_map/all_to_all | solution.py:180
  16.2 49.0 %all-gather.3.cloned.1.call-start = ((), (), s32[]{:S(2)}) async-start(), calls=%async_computation.5 | async-start | bytes 3538944 | tf_op jit(solution)/shard_map/all_gather | solution.py:192
  17.3 10.6 %collective-permute-start.3 = (bf16[384,384]{1,0:T(8,128)(2,1)S(1)}, bf16[384,384]{1,0:T(8,128)(2,1)S(1)}, u32[]{:S(2)}, u32[]{:S(2)}) collective-permute-start(bf16[384,384]{1,0:T(8,128)(2,1)S(1)} %convert_element_type.36), channel_id=1, source_target_pairs={{0,128},{1,129},{2,130},{3,131},{4,132},{5,133},{6,134},{7,135},{8... | collective-permute-start | bytes 884744 | tf_op jit(solution)/shard_map/ppermute | solution.py:30
  19.5 5.3 %collective-permute-start = (bf16[4,32,384]{2,1,0:T(8,128)(2,1)S(1)}, bf16[4,32,384]{2,1,0:T(8,128)(2,1)S(1)}, u32[]{:S(2)}, u32[]{:S(2)}) collective-permute-start(bf16[4,32,384]{2,1,0:T(8,128)(2,1)S(1)} %get-tuple-element.123), channel_id=1, source_target_pairs={{0,4},{1,5},{2,6},{3,7},{4,8},{5,9},{6,10},{7,11},{8,12},{9,13},{1... | collective-permute-start | bytes 294920 | tf_op jit(solution)/shard_map/ppermute | solution.py:30
  20.8 7.1 %collective-permute-start.1 = (bf16[4,32,384]{2,1,0:T(8,128)(2,1)S(1)}, bf16[4,32,384]{2,1,0:T(8,128)(2,1)S(1)}, u32[]{:S(2)}, u32[]{:S(2)}) collective-permute-start(bf16[4,32,384]{2,1,0:T(8,128)(2,1)S(1)} %get-tuple-element.122), channel_id=1, source_target_pairs={{0,8},{1,9},{2,10},{3,11},{4,12},{5,13},{6,14},{7,15},{8,0},{9,1},... | collective-permute-start | bytes 294920 | tf_op jit(solution)/shard_map/ppermute | solution.py:30
  23.2 4.7 %collective-permute-start.2 = (bf16[4,32,384]{2,1,0:T(8,128)(2,1)S(1)}, bf16[4,32,384]{2,1,0:T(8,128)(2,1)S(1)}, u32[]{:S(2)}, u32[]{:S(2)}) collective-permute-start(bf16[4,32,384]{2,1,0:T(8,128)(2,1)S(1)} %get-tuple-element.121), channel_id=1, source_target_pairs={{0,12},{1,13},{2,14},{3,15},{4,0},{5,1},{6,2},{7,3},{8,4},{9,5},{1... | collective-permute-start | bytes 294920 | tf_op jit(solution)/shard_map/ppermute | solution.py:30
  28.7 113.0 %reduce-scatter.2.cloned.1.call-start = ((), (), s32[]{:S(2)}) async-start(), calls=%async_computation.6 | async-start | bytes 1966080 | tf_op jit(solution)/shard_map/reduce_scatter | solution.py:224
  29.0 26.6 %collective-permute-start.6 = (bf16[768,384]{1,0:T(8,128)(2,1)S(1)}, bf16[768,384]{1,0:T(8,128)(2,1)S(1)}, u32[]{:S(2)}, u32[]{:S(2)}) collective-permute-start(bf16[768,384]{1,0:T(8,128)(2,1)S(1)} %pad_maximum_fusion), channel_id=1, source_target_pairs={{0,4},{1,5},{2,6},{3,7},{4,8},{5,9},{6,10},{7,11},{8,12},{9,13},{1... | collective-permute-start | bytes 1769480 | tf_op jit(solution)/shard_map/ppermute | solution.py:30
  29.6 26.9 %collective-permute-start.7 = (bf16[768,384]{1,0:T(8,128)(2,1)S(1)}, bf16[768,384]{1,0:T(8,128)(2,1)}, u32[]{:S(2)}, u32[]{:S(2)}) collective-permute-start(bf16[768,384]{1,0:T(8,128)(2,1)S(1)} %pad_maximum_fusion), channel_id=1, source_target_pairs={{0,12},{1,13},{2,14},{3,15},{4,0},{5,1},{6,2},{7,3},{8,4},{9,5},{1... | collective-permute-start | bytes 1769480 | tf_op jit(solution)/shard_map/ppermute | solution.py:30
  31.7 15.3 %collective-permute-start.4 = (bf16[8,32,768]{2,1,0:T(8,128)(2,1)S(1)}, bf16[8,32,768]{2,1,0:T(8,128)(2,1)S(1)}, u32[]{:S(2)}, u32[]{:S(2)}) collective-permute-start(bf16[8,32,768]{2,1,0:T(8,128)(2,1)S(1)} %all-to-all-done), channel_id=1, source_target_pairs={{0,1},{1,2},{2,3},{3,0},{4,5},{5,6},{6,7},{7,4},{8,9},{9,10},{10,1... | collective-permute-start | bytes 1179656 | tf_op jit(solution)/shard_map/ppermute | solution.py:30
  34.7 20.9 %collective-permute-start.5 = (bf16[8,32,768]{2,1,0:T(8,128)(2,1)S(1)}, bf16[8,32,768]{2,1,0:T(8,128)(2,1)S(1)}, u32[]{:S(2)}, u32[]{:S(2)}) collective-permute-start(bf16[8,32,768]{2,1,0:T(8,128)(2,1)S(1)} %all-to-all-done), channel_id=1, source_target_pairs={{0,3},{1,0},{2,1},{3,2},{4,7},{5,4},{6,5},{7,6},{8,11},{9,8},{10,9... | collective-permute-start | bytes 1179656 | tf_op jit(solution)/shard_map/ppermute | solution.py:30
  55.6 0.8 copy-start.5
  56.4 11.4 %collective-permute-start.10 = (bf16[4,32,768]{2,1,0:T(8,128)(2,1)S(1)}, bf16[4,32,768]{2,1,0:T(8,128)(2,1)}, u32[]{:S(2)}, u32[]{:S(2)}) collective-permute-start(bf16[4,32,768]{2,1,0:T(8,128)(2,1)S(1)} %slice.63), channel_id=1, source_target_pairs={{0,1},{1,2},{2,3},{3,0},{4,5},{5,6},{6,7},{7,4},{8,9},{9,10},{10,1... | collective-permute-start | bytes 589832 | tf_op jit(solution)/shard_map/ppermute | solution.py:30
  59.0 8.9 %collective-permute-start.11 = (bf16[4,32,768]{2,1,0:T(8,128)(2,1)S(1)}, bf16[4,32,768]{2,1,0:T(8,128)(2,1)S(1)}, u32[]{:S(2)}, u32[]{:S(2)}) collective-permute-start(bf16[4,32,768]{2,1,0:T(8,128)(2,1)S(1)} %slice.64), channel_id=1, source_target_pairs={{0,3},{1,0},{2,1},{3,2},{4,7},{5,4},{6,5},{7,6},{8,11},{9,8},{10,9... | collective-permute-start | bytes 589832 | tf_op jit(solution)/shard_map/ppermute | solution.py:30
  61.2 15.4 %collective-permute-start.8 = (bf16[384,384]{1,0:T(8,128)(2,1)S(1)}, bf16[384,384]{1,0:T(8,128)(2,1)}, u32[]{:S(2)}, u32[]{:S(2)}) collective-permute-start(bf16[384,384]{1,0:T(8,128)(2,1)S(1)} %slice.61), channel_id=1, source_target_pairs={{0,4},{1,5},{2,6},{3,7},{4,8},{5,9},{6,10},{7,11},{8,12},{9,13},{1... | collective-permute-start | bytes 884744 | tf_op jit(solution)/shard_map/ppermute | solution.py:30
  62.3 14.9 %collective-permute-start.9 = (bf16[384,384]{1,0:T(8,128)(2,1)S(1)}, bf16[384,384]{1,0:T(8,128)(2,1)}, u32[]{:S(2)}, u32[]{:S(2)}) collective-permute-start(bf16[384,384]{1,0:T(8,128)(2,1)S(1)} %slice.62), channel_id=1, source_target_pairs={{0,12},{1,13},{2,14},{3,15},{4,0},{5,1},{6,2},{7,3},{8,4},{9,5},{1... | collective-permute-start | bytes 884744 | tf_op jit(solution)/shard_map/ppermute | solution.py:30
  65.2 2.6 %copy-start.4 = (bf16[1024,1536]{1,0:T(8,128)(2,1)S(1)}, bf16[1024,1536]{1,0:T(8,128)(2,1)}, u32[]{:S(2)}) copy-start(bf16[1024,1536]{1,0:T(8,128)(2,1)} %all-gather.3.cloned.1.call-done) | copy-start | bytes 9437188
  73.4 2.2 %copy-start.3 = (f32[768,1536]{1,0:T(8,128)}, f32[768,1536]{1,0:T(8,128)S(1)}, u32[]{:S(2)}) copy-start(f32[768,1536]{1,0:T(8,128)S(1)} %add_multiply_fusion) | copy-start | bytes 14155780
  73.6 3.6 %copy-start.6 = (bf16[768,384]{1,0:T(8,128)(2,1)S(1)}, bf16[768,384]{1,0:T(8,128)(2,1)}, u32[]{:S(2)}) copy-start(bf16[768,384]{1,0:T(8,128)(2,1)} %copy-done.5) | copy-start | bytes 1769476
  75.6 14.5 %collective-permute-start.15 = (bf16[192,1536]{1,0:T(8,128)(2,1)S(1)}, bf16[192,1536]{1,0:T(8,128)(2,1)S(1)}, u32[]{:S(2)}, u32[]{:S(2)}) collective-permute-start(bf16[192,1536]{1,0:T(8,128)(2,1)S(1)} %fusion.14), channel_id=1, source_target_pairs={{0,128},{1,129},{2,130},{3,131},{4,132},{5,133},{6,134},{7,135},{8... | collective-permute-start | bytes 1769480 | tf_op jit(solution)/shard_map/ppermute | solution.py:30
  75.7 6.7 %collective-permute-start.12 = (bf16[2,192,384]{2,1,0:T(8,128)(2,1)S(1)}, bf16[2,192,384]{2,1,0:T(8,128)(2,1)S(1)}, u32[]{:S(2)}, u32[]{:S(2)}) collective-permute-start(bf16[2,192,384]{2,1,0:T(8,128)(2,1)S(1)} %get-tuple-element.115), channel_id=1, source_target_pairs={{0,12},{1,13},{2,14},{3,15},{4,0},{5,1},{6,2},{7,3},{8,4},{9,5},{1... | collective-permute-start | bytes 884744 | tf_op jit(solution)/shard_map/ppermute | solution.py:30
  76.0 7.2 %collective-permute-start.13 = (bf16[2,192,384]{2,1,0:T(8,128)(2,1)S(1)}, bf16[2,192,384]{2,1,0:T(8,128)(2,1)S(1)}, u32[]{:S(2)}, u32[]{:S(2)}) collective-permute-start(bf16[2,192,384]{2,1,0:T(8,128)(2,1)S(1)} %get-tuple-element.114), channel_id=1, source_target_pairs={{0,8},{1,9},{2,10},{3,11},{4,12},{5,13},{6,14},{7,15},{8,0},{9,1},... | collective-permute-start | bytes 884744 | tf_op jit(solution)/shard_map/ppermute | solution.py:30
  76.6 13.5 %collective-permute-start.14 = (bf16[2,192,384]{2,1,0:T(8,128)(2,1)S(1)}, bf16[2,192,384]{2,1,0:T(8,128)(2,1)S(1)}, u32[]{:S(2)}, u32[]{:S(2)}) collective-permute-start(bf16[2,192,384]{2,1,0:T(8,128)(2,1)S(1)} %get-tuple-element.113), channel_id=1, source_target_pairs={{0,4},{1,5},{2,6},{3,7},{4,8},{5,9},{6,10},{7,11},{8,12},{9,13},{1... | collective-permute-start | bytes 884744 | tf_op jit(solution)/shard_map/ppermute | solution.py:30
  82.4 16.0 %copy-start.7 = (f32[384,3]{0,1:T(4,128)S(1)}, f32[384,3]{0,1:T(4,128)}, u32[]{:S(2)}) copy-start(f32[384,3]{0,1:T(4,128)} %param.11) | copy-start | bytes 13828
  82.4 16.1 %copy-start.8 = (f32[384,3]{0,1:T(4,128)S(1)}, f32[384,3]{0,1:T(4,128)}, u32[]{:S(2)}) copy-start(f32[384,3]{0,1:T(4,128)} %param.13) | copy-start | bytes 13828
  82.4 21.8 %copy-start.1 = (bf16[384,384]{1,0:T(8,128)(2,1)S(1)}, bf16[384,384]{1,0:T(8,128)(2,1)}, u32[]{:S(2)}) copy-start(bf16[384,384]{1,0:T(8,128)(2,1)} %mcode.1) | copy-start | bytes 884740
  82.4 21.8 %copy-start.2 = (bf16[384,384]{1,0:T(8,128)(2,1)S(1)}, bf16[384,384]{1,0:T(8,128)(2,1)}, u32[]{:S(2)}) copy-start(bf16[384,384]{1,0:T(8,128)(2,1)} %scode.1) | copy-start | bytes 884740
  91.3 88.8 %all-gather.5.cloned.1.call-start = ((), (), s32[]{:S(2)}) async-start(), calls=%async_computation.7 | async-start | bytes 5013504 | tf_op jit(solution)/shard_map/all_gather | solution.py:235
  93.2 6.5 %collective-permute-start.16 = (bf16[192,384]{1,0:T(8,128)(2,1)}, bf16[192,384]{1,0:T(8,128)(2,1)S(1)}, u32[]{:S(2)}, u32[]{:S(2)}) collective-permute-start(bf16[192,384]{1,0:T(8,128)(2,1)} %fusion.15), channel_id=1, source_target_pairs={{0,128},{1,129},{2,130},{3,131},{4,132},{5,133},{6,134},{7,135},{8... | collective-permute-start | bytes 442376 | tf_op jit(solution)/shard_map/ppermute | solution.py:30
  96.9 4.5 %collective-permute-start.17 = (bf16[192,384]{1,0:T(8,128)(2,1)}, bf16[192,384]{1,0:T(8,128)(2,1)S(1)}, u32[]{:S(2)}, u32[]{:S(2)}) collective-permute-start(bf16[192,384]{1,0:T(8,128)(2,1)} %get-tuple-element.118), channel_id=1, source_target_pairs={{0,12},{1,13},{2,14},{3,15},{4,0},{5,1},{6,2},{7,3},{8,4},{9,5},{1... | collective-permute-start | bytes 442376 | tf_op jit(solution)/shard_map/ppermute | solution.py:30
  96.9 5.8 %collective-permute-start.18 = (bf16[192,384]{1,0:T(8,128)(2,1)}, bf16[192,384]{1,0:T(8,128)(2,1)S(1)}, u32[]{:S(2)}, u32[]{:S(2)}) collective-permute-start(bf16[192,384]{1,0:T(8,128)(2,1)} %get-tuple-element.117), channel_id=1, source_target_pairs={{0,8},{1,9},{2,10},{3,11},{4,12},{5,13},{6,14},{7,15},{8,0},{9,1},... | collective-permute-start | bytes 442376 | tf_op jit(solution)/shard_map/ppermute | solution.py:30
  97.0 7.2 %collective-permute-start.19 = (bf16[192,384]{1,0:T(8,128)(2,1)S(1)}, bf16[192,384]{1,0:T(8,128)(2,1)S(1)}, u32[]{:S(2)}, u32[]{:S(2)}) collective-permute-start(bf16[192,384]{1,0:T(8,128)(2,1)S(1)} %get-tuple-element.116), channel_id=1, source_target_pairs={{0,4},{1,5},{2,6},{3,7},{4,8},{5,9},{6,10},{7,11},{8,12},{9,13},{1... | collective-permute-start | bytes 442376 | tf_op jit(solution)/shard_map/ppermute | solution.py:30
  141.8 15.7 %all-to-all-start.3 = ((bf16[8,32,768]{2,1,0:T(8,128)(2,1)}), bf16[8,32,768]{2,1,0:T(8,128)(2,1)S(1)}, u32[]{:S(2)}, u32[]{:S(2)}) async-start(bf16[8,32,768]{2,1,0:T(8,128)(2,1)} %bitcast.80), calls=%async_computation.4 | async-start | bytes 786432 | tf_op jit(solution)/shard_map/all_to_all | solution.py:239
Sparse Core Ops, SparseCore 0:
  28.9 32.8 all-gather.2
  91.4 42.5 reduce-scatter.1
  141.9 38.1 all-gather.4
